TPU v7x, 32 devices: a whole 2x2x4 slice. The times are simulated.
32 devices in a mesh: rep: 8 (over y, x, core), grp: 4 (over z).
Axes of the slice: x: 2, y: 2, z: 4, core: 2. Of those that a mesh axis runs over, the one named last changes fastest.
Arguments:
- tokens: bfloat16 [4096, 1536], P(('rep', 'grp')), may hold values from -6 to 6
- attn_gain: bfloat16 [1536], P('grp'), may hold values from 0.5 to 1.5
- query_key_value_weight: bfloat16 [1536, 2560], P('grp'), may hold values from -0.15625 to 0.15625
- attn_proj: bfloat16 [1536, 1536], P('grp'), may hold values from -1.25 to 1.25
- mlp_gain: bfloat16 [1536], P('grp'), may hold values from 0.5 to 1.5
- w_router: bfloat16 [1536, 16], P('grp'), may hold values from -0.078125 to 0.078125
- w_gate_up: bfloat16 [1536, 16, 1024], P('grp'), may hold values from -0.15625 to 0.15625
- w_down: bfloat16 [1536, 16, 512], P('grp'), may hold values from -1 to 1
- prefix_len: int32 [32], P(('rep', 'grp')), may hold values from 0 to 128
- expert_ids: int32 [4096, 8], P(('rep', 'grp')), may hold values from 0 to 15, all different within a row
- priority: int32 [32, 1024], P(('rep', 'grp')), may hold values from 0 to 1023, each once within a row
- cotangent: bfloat16 [4096, 1536], P(('rep', 'grp')), may hold values from -6 to 6
Outputs:
- output: bfloat16 [4096, 1536], P(('rep', 'grp'))
- grad_tokens: float32 [4096, 1536], P(('rep', 'grp'))
- grad_attn_gain: float32 [1536], P('grp')
- grad_w_qkv: float32 [1536, 2560], P('grp')
- grad_attn_proj: float32 [1536, 1536], P('grp')
- grad_mlp_gain: float32 [1536], P('grp')
- grad_w_router: float32 [1536, 16], P('grp')
- grad_w_gate_up: float32 [1536, 16, 1024], P('grp')
- grad_w_down: float32 [1536, 16, 512], P('grp')
Inputs may be any that keep to these rules, and one draw needn't show every extreme that they name: `prefix_len`: positions below a sequence's prefix length attend to one another in both directions. `expert_ids`: the 8 experts of a token are different. `priority`: each row holds every number of 0 to 1023 once.
All inputs are finite; a program needn't handle non-finite values.
Results may differ from a plain program's by a relative error of at most 0.015.
Values may be sent and summed in bfloat16 or wider, within the bound.
A program may use at most 576 MiB of HBM per device.

v0:
```python
import jax
import jax.numpy as jnp
from jax import lax
from jax.sharding import PartitionSpec as P

QUERY_HEADS = 24
KEY_VALUE_HEADS = 8
HEAD_WIDTH = 64
HID = 512
TOPK = 8
EXPERTS = 16
CAP = 72


EPS = 1e-05


def rope_tables(sequence_length, head_size):
    half_width = head_size // 2
    position = jnp.arange(sequence_length, dtype=jnp.float32)[:, None]
    inverse_freq = 10000.0 ** (-jnp.arange(half_width, dtype=jnp.float32) * 2.0 / head_size)
    angles = position * inverse_freq[None, :]
    return (jnp.cos(angles), jnp.sin(angles))


def apply_rotary(values_in, cosine_table, sine_table):
    half_width = values_in.shape[-1] // 2
    front_half = values_in[..., :half_width]
    back_half = values_in[..., half_width:]
    cos_rows = cosine_table[:, None, :]
    sin_rows = sine_table[:, None, :]
    return jnp.concatenate(
        [
            front_half * cos_rows - back_half * sin_rows,
            back_half * cos_rows + front_half * sin_rows,
        ],
        axis=-1,
    )


def slot_plan(expert_ids, priority, experts, capacity):
    sequence_length, top_count = expert_ids.shape
    pair_count = sequence_length * top_count
    flat_ids = expert_ids.reshape(pair_count)
    numbers = jnp.arange(pair_count, dtype=jnp.int32)
    ordering = jnp.zeros((pair_count,), jnp.int32).at[priority.reshape(pair_count)].set(numbers)
    sorted_ids = flat_ids[ordering]
    one_hot = (sorted_ids[:, None] == jnp.arange(experts, dtype=jnp.int32)[None, :]).astype(
        jnp.int32
    )
    rank_rows = jnp.sum((jnp.cumsum(one_hot, axis=0) - 1) * one_hot, axis=1)
    slot_index = jnp.zeros((pair_count,), jnp.int32).at[ordering].set(rank_rows)
    target = jnp.where(slot_index < capacity, flat_ids * capacity + slot_index, experts * capacity)
    source_row = (
        jnp.full((experts * capacity + 1,), sequence_length, jnp.int32)
        .at[target]
        .set(numbers // top_count)
    )
    return (target, source_row[: experts * capacity])


def shards(
    tokens,
    attn_gain,
    query_key_value_weight,
    attn_proj,
    mlp_gain,
    w_router,
    w_gate_up,
    w_down,
    prefix_len,
    expert_ids,
    priority,
    cotangent,
):
    sequence_length = tokens.shape[0]
    width = tokens.shape[1]
    gain_one, qkv_full, proj_full, gain_two, router_full = (
        lax.all_gather(attn_gain, "grp", axis=0, tiled=True),
        lax.all_gather(query_key_value_weight, "grp", axis=0, tiled=True),
        lax.all_gather(attn_proj, "grp", axis=0, tiled=True),
        lax.all_gather(mlp_gain, "grp", axis=0, tiled=True),
        lax.all_gather(w_router, "grp", axis=0, tiled=True),
    )
    tokens_f = tokens.astype(jnp.float32)
    inverse_one = lax.rsqrt(jnp.mean(tokens_f * tokens_f, axis=1, keepdims=True) + EPS)
    normed_one = tokens_f * inverse_one
    gain_one_f = gain_one.astype(jnp.float32)
    act_one = (normed_one * gain_one_f).astype(jnp.bfloat16)
    projected_rows = jnp.dot(act_one, qkv_full, preferred_element_type=jnp.float32)
    query_feature_width = QUERY_HEADS * HEAD_WIDTH
    key_feature_width = KEY_VALUE_HEADS * HEAD_WIDTH
    heads_per_group = QUERY_HEADS // KEY_VALUE_HEADS
    cosine_table, sine_table = rope_tables(sequence_length, HEAD_WIDTH)
    query_rows = (
        apply_rotary(
            projected_rows[:, :query_feature_width].reshape(
                sequence_length, QUERY_HEADS, HEAD_WIDTH
            ),
            cosine_table,
            sine_table,
        )
        .astype(jnp.bfloat16)
        .reshape(sequence_length, KEY_VALUE_HEADS, heads_per_group, HEAD_WIDTH)
    )
    key_matrix = apply_rotary(
        projected_rows[:, query_feature_width : query_feature_width + key_feature_width].reshape(
            sequence_length, KEY_VALUE_HEADS, HEAD_WIDTH
        ),
        cosine_table,
        sine_table,
    ).astype(jnp.bfloat16)
    value_matrix = (
        projected_rows[:, query_feature_width + key_feature_width :]
        .reshape(sequence_length, KEY_VALUE_HEADS, HEAD_WIDTH)
        .astype(jnp.bfloat16)
    )
    score_scale = HEAD_WIDTH ** (-0.5)
    row_pos = jnp.arange(sequence_length)[:, None]
    col_pos = jnp.arange(sequence_length)[None, :]
    allowed = (col_pos <= row_pos) | (col_pos < prefix_len[0])
    scores = (
        jnp.einsum("shgd,thd->hgst", query_rows, key_matrix, preferred_element_type=jnp.float32)
        * score_scale
    )
    scores = jnp.where(allowed, scores, -1e30)
    exps_row = jnp.exp(scores - jnp.max(scores, axis=-1, keepdims=True))
    attn_probs = exps_row / jnp.sum(exps_row, axis=-1, keepdims=True)
    probs_low = attn_probs.astype(jnp.bfloat16)
    attended = (
        jnp.einsum("hgst,thd->shgd", probs_low, value_matrix, preferred_element_type=jnp.float32)
        .reshape(sequence_length, query_feature_width)
        .astype(jnp.bfloat16)
    )
    residual = tokens_f + jnp.dot(attended, proj_full, preferred_element_type=jnp.float32)
    inverse_two = lax.rsqrt(jnp.mean(residual * residual, axis=1, keepdims=True) + EPS)
    normed_two = residual * inverse_two
    gain_two_f = gain_two.astype(jnp.float32)
    act_two = (normed_two * gain_two_f).astype(jnp.bfloat16)
    logits = jnp.dot(act_two, router_full, preferred_element_type=jnp.float32)
    choose = (expert_ids[:, :, None] == jnp.arange(EXPERTS, dtype=jnp.int32)[None, None, :]).astype(
        jnp.float32
    )
    chosen = jnp.sum(choose * logits[:, None, :], axis=2)
    gate_exp = jnp.exp(chosen - jnp.max(chosen, axis=1, keepdims=True))
    gates = gate_exp / jnp.sum(gate_exp, axis=1, keepdims=True)
    target, source_row = slot_plan(expert_ids, priority, EXPERTS, CAP)
    padded = jnp.concatenate([act_two, jnp.zeros((1, width), jnp.bfloat16)], axis=0)
    slots_in = padded[source_row].reshape(EXPERTS, CAP, width)
    inputs_part = slots_in
    gate_up = jnp.einsum(
        "ecd,deh->ech",
        inputs_part,
        lax.all_gather(w_gate_up, "grp", axis=0, tiled=True),
        preferred_element_type=jnp.float32,
    )
    gate_part = gate_up[..., :HID]
    up_part = gate_up[..., HID:]
    sigmoid_g = jax.nn.sigmoid(gate_part)
    silu_g = gate_part * sigmoid_g
    hidden_low = (silu_g * up_part).astype(jnp.bfloat16)
    expert_out = jnp.einsum(
        "ech,deh->ecd",
        hidden_low,
        lax.all_gather(w_down, "grp", axis=0, tiled=True),
        preferred_element_type=jnp.float32,
    )
    out_pad = jnp.concatenate(
        [expert_out.reshape(EXPERTS * CAP, width), jnp.zeros((1, width), jnp.float32)], axis=0
    )
    picked = out_pad[target].reshape(sequence_length, TOPK, width)
    output = residual + jnp.sum(gates[:, :, None] * picked, axis=1)
    grad_out_f = cotangent.astype(jnp.float32)
    grad_gates = jnp.sum(grad_out_f[:, None, :] * picked, axis=2)
    spread = (gates[:, :, None] * grad_out_f[:, None, :]).reshape(sequence_length * TOPK, width)
    grad_slots = (
        jnp.zeros((EXPERTS * CAP + 1, width), jnp.float32).at[target].add(spread)[: EXPERTS * CAP]
    )
    grad_slots = grad_slots.reshape(EXPERTS, CAP, width).astype(jnp.bfloat16)
    grads_part = grad_slots
    grad_hidden = jnp.einsum(
        "ecd,deh->ech",
        grads_part,
        lax.all_gather(w_down, "grp", axis=0, tiled=True),
        preferred_element_type=jnp.float32,
    )
    grad_gate_part = grad_hidden * up_part * sigmoid_g * (1.0 + gate_part * (1.0 - sigmoid_g))
    grad_up_part = grad_hidden * silu_g
    grad_gate_up = jnp.concatenate([grad_gate_part, grad_up_part], axis=2).astype(jnp.bfloat16)
    grad_slot_inputs = jnp.einsum(
        "ech,deh->ecd",
        grad_gate_up,
        lax.all_gather(w_gate_up, "grp", axis=0, tiled=True),
        preferred_element_type=jnp.float32,
    )
    grad_act_two = (
        jnp.zeros((sequence_length + 1, width), jnp.float32)
        .at[source_row]
        .add(grad_slot_inputs.reshape(EXPERTS * CAP, width))[:sequence_length]
    )
    gate_mean = jnp.sum(gates * grad_gates, axis=1, keepdims=True)
    grad_chosen = gates * (grad_gates - gate_mean)
    grad_logits = jnp.sum(choose * grad_chosen[:, :, None], axis=1).astype(jnp.bfloat16)
    grad_act_two = grad_act_two + jnp.dot(
        grad_logits, router_full.T, preferred_element_type=jnp.float32
    )
    router_term = jnp.dot(act_two.T, grad_logits, preferred_element_type=jnp.float32)
    gain_two_term = jnp.sum(grad_act_two * normed_two, axis=0)
    scaled_two = grad_act_two * gain_two_f
    grad_residual = grad_out_f + inverse_two * (
        scaled_two - normed_two * jnp.mean(scaled_two * normed_two, axis=1, keepdims=True)
    )
    grad_res_low = grad_residual.astype(jnp.bfloat16)
    proj_term = jnp.dot(attended.T, grad_res_low, preferred_element_type=jnp.float32)
    grad_att = (
        jnp.dot(grad_res_low, proj_full.T, preferred_element_type=jnp.float32)
        .astype(jnp.bfloat16)
        .reshape(sequence_length, KEY_VALUE_HEADS, heads_per_group, HEAD_WIDTH)
    )
    grad_values = jnp.einsum(
        "hgst,shgd->thd", probs_low, grad_att, preferred_element_type=jnp.float32
    )
    grad_probs = jnp.einsum(
        "shgd,thd->hgst", grad_att, value_matrix, preferred_element_type=jnp.float32
    )
    grad_scores = (
        attn_probs * (grad_probs - jnp.sum(attn_probs * grad_probs, axis=-1, keepdims=True))
    ).astype(jnp.bfloat16)
    grad_queries = (
        jnp.einsum("hgst,thd->shgd", grad_scores, key_matrix, preferred_element_type=jnp.float32)
        * score_scale
    )
    grad_keys = (
        jnp.einsum("hgst,shgd->thd", grad_scores, query_rows, preferred_element_type=jnp.float32)
        * score_scale
    )
    grad_queries = apply_rotary(
        grad_queries.reshape(sequence_length, QUERY_HEADS, HEAD_WIDTH), cosine_table, -sine_table
    ).reshape(sequence_length, query_feature_width)
    grad_keys = apply_rotary(grad_keys, cosine_table, -sine_table).reshape(
        sequence_length, key_feature_width
    )
    grad_projected = jnp.concatenate(
        [grad_queries, grad_keys, grad_values.reshape(sequence_length, key_feature_width)], axis=1
    ).astype(jnp.bfloat16)
    qkv_term = jnp.dot(act_one.T, grad_projected, preferred_element_type=jnp.float32)
    grad_act_one = jnp.dot(grad_projected, qkv_full.T, preferred_element_type=jnp.float32)
    gain_one_term = jnp.sum(grad_act_one * normed_one, axis=0)
    scaled_one = grad_act_one * gain_one_f
    grad_tokens = grad_residual + inverse_one * (
        scaled_one - normed_one * jnp.mean(scaled_one * normed_one, axis=1, keepdims=True)
    )
    owned_gain_one, owned_qkv, owned_proj, owned_gain_two, owned_router = (
        lax.psum_scatter(gain_one_term, "grp", scatter_dimension=0, tiled=True),
        lax.psum_scatter(qkv_term, "grp", scatter_dimension=0, tiled=True),
        lax.psum_scatter(proj_term, "grp", scatter_dimension=0, tiled=True),
        lax.psum_scatter(gain_two_term, "grp", scatter_dimension=0, tiled=True),
        lax.psum_scatter(router_term, "grp", scatter_dimension=0, tiled=True),
    )
    inputs_part = slots_in
    grads_part = grad_slots
    gate_up_term = jnp.einsum(
        "ecd,ech->deh", inputs_part, grad_gate_up, preferred_element_type=jnp.float32
    )
    down_term = jnp.einsum(
        "ecd,ech->deh", grads_part, hidden_low, preferred_element_type=jnp.float32
    )
    owned_experts = lax.psum_scatter(
        jnp.concatenate([gate_up_term, down_term], axis=2), "grp", scatter_dimension=0, tiled=True
    )
    summed = lax.psum(
        (owned_gain_one, owned_qkv, owned_proj, owned_gain_two, owned_router, owned_experts), "rep"
    )
    expert_total = summed[5]
    return (
        output.astype(jnp.bfloat16),
        grad_tokens,
        summed[0],
        summed[1],
        summed[2],
        summed[3],
        summed[4],
        expert_total[:, :, : 2 * HID],
        expert_total[:, :, 2 * HID :],
    )


def solution(mesh):
    in_specs = (
        P(("rep", "grp"), None),
        P("grp"),
        P("grp", None),
        P("grp", None),
        P("grp"),
        P("grp", None),
        P("grp", None, None),
        P("grp", None, None),
        P(("rep", "grp")),
        P(("rep", "grp"), None),
        P(("rep", "grp"), None),
        P(("rep", "grp"), None),
    )
    out_specs = (
        P(("rep", "grp"), None),
        P(("rep", "grp"), None),
        P("grp"),
        P("grp", None),
        P("grp", None),
        P("grp"),
        P("grp", None),
        P("grp", None, None),
        P("grp", None, None),
    )
    return jax.shard_map(shards, mesh=mesh, in_specs=in_specs, out_specs=out_specs, check_vma=False)
```

profile of v0, /device:TPU:0, one launch (start us, length us, event | category | flops | bytes accessed | tf_op | source)
XLA Modules:
  0.0 5103.2 jit_solution(7775412672875975308)
XLA Ops:
  8.7 14.8 copy.107
  23.5 9.5 copy.108
  33.9 13.6 all-gather.1
  47.5 14.3 all-gather
  85.4 18.0 all_gather.27
  104.5 49.8 all-gather.7.cloned.1.call-done
  164.7 78.8 %all-gather.9.cloned.1.call-done = bf16[1536,1536]{1,0:T(8,128)(2,1)} async-done(((bf16[384,1536]{1,0:T(8,128)(2,1)}), bf16[1536,1536]{1,0:T(8,128)(2,1)}) %all-gather.9.cloned.1.call-update) | async-done | bytes 4718608 | tf_op jit(solution)/shard_map/all_gather | solution.py:81
  249.5 16.0 scatter_custom_fusion.3
  276.8 804.7 %all-gather.11.cloned.1.call-done = bf16[1536,16,1024]{2,0,1:T(8,128)(2,1)} async-done(((bf16[384,16,1024]{2,0,1:T(8,128)(2,1)}), bf16[1536,16,1024]{2,0,1:T(8,128)(2,1)}) %all-gather.11.cloned.1.call-update) | async-done | bytes 50331664 | tf_op jit(solution)/shard_map/all_gather | solution.py:154
  1081.5 27.5 fusion.75
  1109.0 397.5 %all-gather.13.cloned.1.call-done = bf16[1536,16,512]{2,0,1:T(8,128)(2,1)} async-done(((bf16[384,16,512]{2,0,1:T(8,128)(2,1)}), bf16[1536,16,512]{2,0,1:T(8,128)(2,1)}) %all-gather.13.cloned.1.call-update) | async-done | bytes 25165840 | tf_op jit(solution)/shard_map/all_gather | solution.py:165
  1506.5 16.0 multiply_convert_fusion.1
  1522.5 24.3 fusion.12
  1546.8 17.0 scatter_custom_fusion.4
  1563.9 15.8 fusion.76
  1579.7 6.5 concatenate.43
  1586.3 10.8 gather_fusion.2
  1604.6 6.4 fusion.34
  1619.4 8.2 fusion.32
  1627.9 21.9 convolution_bitcast_fusion.1
  1649.8 37.2 convolution_bitcast_fusion
  1687.0 99.1 %pad_maximum_fusion = f32[1536,16,1536]{0,2,1:T(8,128)} fusion(f32[1536,16,512]{0,2,1:T(8,128)} %convolution_bitcast_fusion.1, f32[1536,16,1024]{0,2,1:T(8,128)} %convolution_bitcast_fusion), kind=kLoop, calls=%fused_computation.9 | loop fusion | flops 37748736 | bytes 301989888 | tf_op jit(solution)/shard_map/concatenate | solution.py:269
  1788.0 248.9 %reduce-scatter.5.cloned.1.call-done = f32[384,2560]{1,0:T(8,128)} async-done(((f32[1536,2560]{1,0:T(8,128)}), f32[384,2560]{1,0:T(8,128)}) %reduce-scatter.5.cloned.1.call-update) | async-done | bytes 3932176 | tf_op jit(solution)/shard_map/reduce_scatter | solution.py:255
  2036.9 2449.7 %reduce-scatter.11.cloned.1.call-done = f32[384,16,1536]{0,2,1:T(8,128)} async-done(((f32[1536,16,1536]{0,2,1:T(8,128)}), f32[384,16,1536]{0,2,1:T(8,128)}) %reduce-scatter.11.cloned.1.call-update) | async-done | bytes 37748752 | tf_op jit(solution)/shard_map/reduce_scatter | solution.py:268
  4488.7 6.1 fusion.26
  4494.8 19.6 all-reduce.6
  4515.8 25.1 all-reduce.4
  4540.9 484.3 %all-reduce.9.cloned.1.call-done = (f32[384,2560]{1,0:T(8,128)}, f32[384,1536]{1,0:T(8,128)}, f32[384,16,1536]{0,2,1:T(8,128)}) async-done(((f32[384,2560]{1,0:T(8,128)}, f32[384,1536]{1,0:T(8,128)}, f32[384,16,1536]{0,2,1:T(8,128)}), (f32[384,2560]{1,0:T(8,128)}, f32[384,1536]{1,0:T(8,128)}, f32[384,16,1536]{0,2,1:T(8,128)})) %all-reduce.9.cloned.1.call-update) | async-done | bytes 44040208 | tf_op jit(solution)/shard_map/psum | solution.py:271
  5025.2 10.6 slice.107
  5035.8 17.3 slice.106
  5053.1 24.8 copy.116
  5077.9 12.6 copy.117
  (240 shorter events, 79.6 us)
Async XLA Ops:
  7.2 147.1 %all-gather.7.cloned.1.call-start = ((), (), s32[]{:S(2)}) async-start(), calls=%async_computation.4 | async-start | bytes 9830400 | tf_op jit(solution)/shard_map/all_gather | solution.py:80
  7.9 235.6 %all-gather.9.cloned.1.call-start = ((), (), s32[]{:S(2)}) async-start(), calls=%async_computation.5 | async-start | bytes 5898240 | tf_op jit(solution)/shard_map/all_gather | solution.py:81
  8.7 1072.8 %all-gather.11.cloned.1.call-start = ((), (), s32[]{:S(2)}) async-start(), calls=%async_computation.6 | async-start | bytes 62914560 | tf_op jit(solution)/shard_map/all_gather | solution.py:154
  23.5 1483.0 %all-gather.13.cloned.1.call-start = ((), (), s32[]{:S(2)}) async-start(), calls=%async_computation.7 | async-start | bytes 31457280 | tf_op jit(solution)/shard_map/all_gather | solution.py:165
  33.0 28.9 copy-start.46
  33.0 29.1 copy-start.63
  33.1 42.8 copy-start.16
  33.1 52.3 %copy-start.58 = (bf16[384,16]{0,1:T(8,128)(2,1)S(1)}, bf16[384,16]{0,1:T(8,128)(2,1)}, u32[]{:S(2)}) copy-start(bf16[384,16]{0,1:T(8,128)(2,1)} %param.17) | copy-start | bytes 36868
  33.1 70.4 %copy-start.2 = (bf16[128,1536]{1,0:T(8,128)(2,1)S(1)}, bf16[128,1536]{1,0:T(8,128)(2,1)}, u32[]{:S(2)}) copy-start(bf16[128,1536]{1,0:T(8,128)(2,1)} %param.12) | copy-start | bytes 1179652
  33.1 1754.9 %reduce-scatter.7.cloned.1.call-start = ((), (), s32[]{:S(2)}) async-start(), calls=%async_computation.9 | async-start | bytes 11796480 | tf_op jit(solution)/shard_map/reduce_scatter | solution.py:256
  47.5 199.3 %copy-start.41 = (f32[1536]{0:T(1024)}, f32[1536]{0:T(1024)S(1)}, u32[]{:S(2)}) copy-start(f32[1536]{0:T(1024)S(1)} %reshape.406) | copy-start | bytes 18436
  61.9 96.9 %copy-start.30 = (f32[1536]{0:T(1024)}, f32[1536]{0:T(1024)S(1)}, u32[]{:S(2)}) copy-start(f32[1536]{0:T(1024)S(1)} %reshape.405) | copy-start | bytes 18436
  76.0 173.5 %copy-start.10 = (f32[128,1536]{1,0:T(8,128)}, f32[128,1536]{1,0:T(8,128)S(1)}, u32[]{:S(2)}) copy-start(f32[128,1536]{1,0:T(8,128)S(1)} %convert_element_type.80) | copy-start | bytes 2359300
  103.4 144.4 %copy-start.28 = (bf16[1536,16]{0,1:T(8,128)(2,1)}, bf16[1536,16]{0,1:T(8,128)(2,1)S(1)}, u32[]{:S(2)}) copy-start(bf16[1536,16]{0,1:T(8,128)(2,1)S(1)} %all_gather.27) | copy-start | bytes 147460
  103.4 55.4 %copy-start.49 = (s32[1152]{0:T(1024)}, s32[1152]{0:T(1024)S(1)}, u32[]{:S(2)}) copy-start(s32[1152]{0:T(1024)S(1)} %compare_select_fusion.1) | copy-start | bytes 13828
  103.6 55.2 %copy-start.53 = (f32[128]{0:T(128)}, f32[128]{0:T(128)S(1)}, u32[]{:S(2)}) copy-start(f32[128]{0:T(128)S(1)} %add_rsqrt_fusion.1) | copy-start | bytes 1540
  163.3 83.4 %copy-start.17 = (f32[8,3,128,128]{2,3,1,0:T(8,128)}, f32[8,3,128,128]{2,3,1,0:T(8,128)S(1)}, u32[]{:S(2)}) copy-start(f32[8,3,128,128]{2,3,1,0:T(8,128)S(1)} %get-tuple-element.89) | copy-start | bytes 4718596
  163.3 83.4 %copy-start.50 = (f32[8,3,128]{2,1,0:T(4,128)}, f32[8,3,128]{2,1,0:T(4,128)S(1)}, u32[]{:S(2)}) copy-start(f32[8,3,128]{2,1,0:T(4,128)S(1)} %get-tuple-element.88) | copy-start | bytes 36868
  164.7 82.0 %copy-start.15 = (bf16[8,64,3,128]{3,1,2,0:T(8,128)(2,1)}, bf16[8,64,3,128]{3,1,2,0:T(8,128)(2,1)S(1)}, u32[]{:S(2)}) copy-start(bf16[8,64,3,128]{3,1,2,0:T(8,128)(2,1)S(1)} %convolution_convert_fusion.1) | copy-start | bytes 1179652
  247.8 17.8 copy-start.12
  248.1 17.5 copy-start.56
  248.6 16.9 copy-start.59
  1081.5 425.0 %copy-start.1 = (bf16[1152,1536]{1,0:T(8,128)(2,1)S(1)}, bf16[1152,1536]{1,0:T(8,128)(2,1)}, u32[]{:S(2)}) copy-start(bf16[1152,1536]{1,0:T(8,128)(2,1)} %slice.136) | copy-start | bytes 10616836
  1522.5 41.3 copy-start.9
  1586.2 10.8 copy-start.11
  1586.3 10.8 copy-start.25
  1611.1 425.9 %reduce-scatter.5.cloned.1.call-start = ((), (), s32[]{:S(2)}) async-start(), calls=%async_computation.8 | async-start | bytes 19660800 | tf_op jit(solution)/shard_map/reduce_scatter | solution.py:255
  1627.6 22.2 copy-start
  1627.6 2859.1 %reduce-scatter.11.cloned.1.call-start = ((), (), s32[]{:S(2)}) async-start(), calls=%async_computation.11 | async-start | bytes 188743680 | tf_op jit(solution)/shard_map/reduce_scatter | solution.py:268
  1786.2 2729.6 %reduce-scatter.9.cloned.1.call-start = ((), (), s32[]{:S(2)}) async-start(), calls=%async_computation.10 | async-start | bytes 122880 | tf_op jit(solution)/shard_map/reduce_scatter | solution.py:258
  1788.0 3237.2 %all-reduce.9.cloned.1.call-start = ((), (), s32[]{:S(2)}) async-start(), calls=%async_computation.12 | async-start | bytes 88080384 | tf_op jit(solution)/shard_map/psum | solution.py:271
  4488.6 25.9 copy-start.8
  (44 other events, 121.3 us)
Sparse Core Ops, SparseCore 0:
  9.6 144.6 all-gather.6
  155.9 87.5 all-gather.8
  245.7 835.7 all-gather.10
  1082.9 423.5 all-gather.12
  1611.2 159.4 reduce-scatter.6
  1773.4 263.4 reduce-scatter.4
  2039.3 2447.3 reduce-scatter.10
  4489.6 20.9 reduce-scatter.8
  4514.7 510.4 all-reduce.8
where the time goes:
time: 5110 us; the launch traced here: 5100 us
  waiting for transfers between devices  4520 us (88%)
  matrix products  182 us (4%)
  local copies, waits for them, and re-layouts  149 us (3%)
  other arithmetic  148 us (3%)
  blocking collectives  90.7 us (2%)
    reduce_scatter x1, waiting for transfers between devices, shards(): lax.psum_scatter(jnp.concatenate([gate_up_term, down_term], axis=2), 'grp...  2450 us
    all_gather x1, waiting for transfers between devices, shards(): lax.all_gather(w_gate_up, 'grp', axis=0, tiled=True)  805 us
    psum x1, waiting for transfers between devices, shards(): lax.psum((owned_gain_one, owned_qkv, owned_proj, owned_gain_two, owned_ro...  484 us
    all_gather x1, waiting for transfers between devices, shards(): lax.all_gather(w_down, 'grp', axis=0, tiled=True)  398 us
    reduce_scatter x1, waiting for transfers between devices, shards(): lax.psum_scatter(qkv_term, 'grp', scatter_dimension=0, tiled=True)  249 us
  transfers between devices with their start and end apart: 9, of which 7 were waited for; matrix products, arithmetic and copies ran while one was open for 6% of the time, Pallas kernels for 0%

commit v1 on v0

v1 whole, which is shorter than its diff:
```python
import jax
import jax.numpy as jnp
from jax import lax
from jax.sharding import PartitionSpec as P

QUERY_HEADS = 24
KEY_VALUE_HEADS = 8
HEAD_WIDTH = 64
HID = 512
EXPERTS = 16
CAP = 72
EPS = 1e-05
BF = jnp.bfloat16
F32 = jnp.float32
QPK = QUERY_HEADS // KEY_VALUE_HEADS
BIG = 1 << 20


def dot(a, b):
    return jnp.dot(a, b, preferred_element_type=F32)


def rope_tables(length):
    half = HEAD_WIDTH // 2
    position = jnp.arange(length, dtype=F32)[:, None]
    inverse_freq = 10000.0 ** (-jnp.arange(half, dtype=F32) * 2.0 / HEAD_WIDTH)
    angles = position * inverse_freq[None, :]
    return jnp.cos(angles), jnp.sin(angles)


def rotate(v, cos, sin):
    half = HEAD_WIDTH // 2
    a, b = v[..., :half], v[..., half:]
    return jnp.concatenate([a * cos - b * sin, b * cos + a * sin], axis=-1)


def routing(expert_ids, priority, logits):
    seq, top = expert_ids.shape
    choose = expert_ids[:, :, None] == jnp.arange(EXPERTS, dtype=jnp.int32)[None, None, :]
    chosen = jnp.any(choose, axis=1)
    rank_of = jnp.sum(jnp.where(choose, priority.reshape(seq, top)[:, :, None], 0), axis=1)
    rank_of = jnp.where(chosen, rank_of, BIG)
    slot = jnp.sum((rank_of[None, :, :] < rank_of[:, None, :]).astype(jnp.int32), axis=1)
    kept = chosen & (slot < CAP)
    top_logit = jnp.max(jnp.where(chosen, logits, -jnp.inf), axis=1, keepdims=True)
    gate_exp = jnp.where(chosen, jnp.exp(jnp.where(chosen, logits - top_logit, 0.0)), 0.0)
    gates = gate_exp / jnp.sum(gate_exp, axis=1, keepdims=True)
    return gates, kept


def shards(
    reps,
    grps,
    tokens,
    attn_gain,
    query_key_value_weight,
    attn_proj,
    mlp_gain,
    w_router,
    w_gate_up,
    w_down,
    prefix_len,
    expert_ids,
    priority,
    cotangent,
):
    seq, width = tokens.shape
    own = width // grps
    local_experts = EXPERTS // grps
    heads = KEY_VALUE_HEADS
    groups = None if reps == heads else [list(range(i, i + heads)) for i in range(0, reps, heads)]
    rep, grp = lax.axis_index("rep"), lax.axis_index("grp")
    head = lax.rem(rep, heads)
    qw, hw = QPK * HEAD_WIDTH, HEAD_WIDTH
    q_all = QUERY_HEADS * HEAD_WIDTH

    small = jnp.concatenate([attn_gain[:, None], mlp_gain[:, None], w_router], axis=1)
    small = lax.all_gather(small, "grp", axis=0, tiled=True)
    gain_one, gain_two = small[:, 0].astype(F32)[None, :], small[:, 1].astype(F32)[None, :]
    router = small[:, 2:]
    qkv_cols = jnp.concatenate(
        [
            lax.dynamic_slice_in_dim(query_key_value_weight, head * qw, qw, 1),
            lax.dynamic_slice_in_dim(query_key_value_weight, q_all + head * hw, hw, 1),
            lax.dynamic_slice_in_dim(query_key_value_weight, q_all + heads * hw + head * hw, hw, 1),
        ],
        axis=1,
    )
    qkv_head = lax.all_gather(qkv_cols, "grp", axis=0, tiled=True)
    row = head * qw + jnp.arange(qw)
    mine = (row // own) == grp
    proj_rows = jnp.where(mine[:, None], jnp.take(attn_proj, jnp.where(mine, row - grp * own, 0), axis=0), 0)
    proj_head = lax.psum(proj_rows, "grp")

    piece = own // reps
    gu_piece = lax.dynamic_slice_in_dim(w_gate_up, rep * piece, piece, 0)
    dn_piece = lax.dynamic_slice_in_dim(w_down, rep * piece, piece, 0)
    both = jnp.concatenate([gu_piece, dn_piece], axis=2)
    both = both.reshape(piece, grps, local_experts, 3 * HID).transpose(1, 2, 0, 3)
    both = lax.all_to_all(both, "grp", 0, 0, tiled=True)
    both = lax.all_gather(both, "rep", axis=0, tiled=False)
    both = both.transpose(2, 1, 0, 3, 4).reshape(local_experts, width, 3 * HID)
    wgu, wdn = both[:, :, : 2 * HID], both[:, :, 2 * HID :]

    tokens_f = tokens.astype(F32)
    inverse_one = lax.rsqrt(jnp.mean(tokens_f * tokens_f, axis=1, keepdims=True) + EPS)
    normed_one = tokens_f * inverse_one
    act_one = (normed_one * gain_one).astype(BF)
    act_plane = lax.all_gather(act_one, "rep", axis=0, tiled=True, axis_index_groups=groups)
    prefix_plane = lax.all_gather(prefix_len, "rep", axis=0, tiled=True, axis_index_groups=groups)
    cos, sin = rope_tables(seq)
    projected = dot(act_plane, qkv_head).reshape(heads, seq, QPK + 2, HEAD_WIDTH)
    cos_b, sin_b = cos[None, :, None, :], sin[None, :, None, :]
    turned = rotate(projected[:, :, : QPK + 1], cos_b, sin_b).astype(BF)
    query = turned[:, :, :QPK]
    key = turned[:, :, QPK]
    value = projected[:, :, QPK + 1].astype(BF)
    scale = HEAD_WIDTH ** (-0.5)
    row_pos, col_pos = jnp.arange(seq)[:, None], jnp.arange(seq)[None, :]
    allowed = (col_pos <= row_pos)[None] | (col_pos[None] < prefix_plane[:, None, None])
    scores = jnp.einsum("bsgd,btd->bgst", query, key, preferred_element_type=F32) * scale
    scores = jnp.where(allowed[:, None], scores, -1e30)
    exps = jnp.exp(scores - jnp.max(scores, axis=-1, keepdims=True))
    probs = exps / jnp.sum(exps, axis=-1, keepdims=True)
    probs_low = probs.astype(BF)
    attended = jnp.einsum("bgst,btd->bsgd", probs_low, value, preferred_element_type=F32)
    attended = attended.astype(BF).reshape(heads * seq, qw)
    part = dot(attended, proj_head).astype(BF)
    part = lax.psum_scatter(part, "rep", scatter_dimension=0, tiled=True, axis_index_groups=groups)
    residual = tokens_f + part.astype(F32)
    inverse_two = lax.rsqrt(jnp.mean(residual * residual, axis=1, keepdims=True) + EPS)
    normed_two = residual * inverse_two
    act_two = (normed_two * gain_two).astype(BF)
    gates, kept = routing(expert_ids, priority, dot(act_two, router))

    dy_all = lax.all_gather(cotangent, "grp", axis=0, tiled=True)
    x_all = lax.all_gather(act_two, "grp", axis=0, tiled=True)
    weight = lax.all_gather(jnp.where(kept, gates, 0.0), "grp", axis=0, tiled=True)
    weight = lax.dynamic_slice_in_dim(weight, grp * local_experts, local_experts, 1).T[:, :, None]
    gate_up = jnp.einsum("td,edh->eth", x_all, wgu, preferred_element_type=F32)
    g, u = gate_up[..., :HID], gate_up[..., HID:]
    sig = jax.nn.sigmoid(g)
    silu = g * sig
    hidden = silu * u
    hidden_w = (hidden * weight).astype(BF)
    back = jnp.einsum("td,edh->eth", dy_all, wdn, preferred_element_type=F32)
    grad_gate_part = jnp.sum(back * hidden, axis=2)
    grad_hidden = back * weight
    ggu = jnp.concatenate(
        [grad_hidden * u * sig * (1.0 + g * (1.0 - sig)), grad_hidden * silu], axis=2
    ).astype(BF)
    out_part = jnp.einsum("eth,edh->td", hidden_w, wdn, preferred_element_type=F32).astype(BF)
    gact_part = jnp.einsum("eth,edh->td", ggu, wgu, preferred_element_type=F32).astype(BF)
    gact = lax.psum_scatter(gact_part, "grp", scatter_dimension=0, tiled=True).astype(F32)
    grad_gates = lax.all_to_all(grad_gate_part.T, "grp", 0, 1, tiled=True)
    grad_gates = jnp.where(kept, grad_gates, 0.0)
    gw_gu = jnp.einsum("td,eth->edh", x_all, ggu, preferred_element_type=F32).astype(BF)
    gw_dn = jnp.einsum("td,eth->edh", dy_all, hidden_w, preferred_element_type=F32).astype(BF)
    gw = jnp.concatenate([gw_gu, gw_dn], axis=2)
    gw = gw.reshape(local_experts, grps, reps, piece, 3 * HID).transpose(2, 1, 3, 0, 4)
    gw = gw.reshape(reps * grps * piece, EXPERTS // grps * 3 * HID)
    gw = lax.psum_scatter(gw, "rep", scatter_dimension=0, tiled=True)
    gw = gw.reshape(grps, piece, local_experts, 3 * HID)
    gw = lax.all_to_all(gw, "grp", 0, 0, tiled=True)
    gw = gw.transpose(1, 0, 2, 3).reshape(piece, EXPERTS, 3 * HID)
    gw = lax.all_gather(gw, "rep", axis=0, tiled=True)
    grad_gu = gw[:, :, : 2 * HID].astype(F32)
    grad_dn = gw[:, :, 2 * HID :].astype(F32)
    out = lax.psum_scatter(out_part, "grp", scatter_dimension=0, tiled=True).astype(F32)
    output = (residual + out).astype(BF)

    grad_logits = (gates * (grad_gates - jnp.sum(gates * grad_gates, axis=1, keepdims=True))).astype(BF)
    gact = gact + dot(grad_logits, router.T)
    router_term = dot(act_two.T, grad_logits)
    gain_two_term = jnp.sum(gact * normed_two, axis=0)
    scaled = gact * gain_two
    dy = cotangent.astype(F32)
    grad_residual = dy + inverse_two * (
        scaled - normed_two * jnp.mean(scaled * normed_two, axis=1, keepdims=True)
    )
    gres_low = grad_residual.astype(BF)

    gres_plane = lax.all_gather(gres_low, "rep", axis=0, tiled=True, axis_index_groups=groups)
    proj_term = dot(attended.T, gres_plane)
    grad_att = dot(gres_plane, proj_head.T).astype(BF).reshape(heads, seq, QPK, HEAD_WIDTH)
    grad_value = jnp.einsum("bgst,bsgd->btd", probs_low, grad_att, preferred_element_type=F32)
    grad_probs = jnp.einsum("bsgd,btd->bgst", grad_att, value, preferred_element_type=F32)
    grad_scores = (
        probs * (grad_probs - jnp.sum(probs * grad_probs, axis=-1, keepdims=True))
    ).astype(BF)
    grad_query = jnp.einsum("bgst,btd->bsgd", grad_scores, key, preferred_element_type=F32) * scale
    grad_key = jnp.einsum("bgst,bsgd->btd", grad_scores, query, preferred_element_type=F32) * scale
    turned_back = rotate(
        jnp.concatenate([grad_query, grad_key[:, :, None]], axis=2), cos_b, -sin_b
    )
    gproj = jnp.concatenate([turned_back, grad_value[:, :, None]], axis=2).astype(BF)
    gproj = gproj.reshape(heads * seq, qw + 2 * hw)
    qkv_term = dot(act_plane.T, gproj)
    gact_one = dot(gproj, qkv_head.T).astype(BF)
    gact_one = lax.psum_scatter(
        gact_one, "rep", scatter_dimension=0, tiled=True, axis_index_groups=groups
    ).astype(F32)
    gain_one_term = jnp.sum(gact_one * normed_one, axis=0)
    scaled_one = gact_one * gain_one
    grad_tokens = grad_residual + inverse_one * (
        scaled_one - normed_one * jnp.mean(scaled_one * normed_one, axis=1, keepdims=True)
    )

    qkv_own = lax.psum_scatter(qkv_term.astype(BF), "grp", scatter_dimension=0, tiled=True)
    proj_sum = lax.psum(proj_term.astype(BF), "grp")
    if groups is not None:
        across = [[i + heads * j for j in range(reps // heads)] for i in range(heads)]
        qkv_own = lax.psum(qkv_own, "rep", axis_index_groups=across)
        proj_sum = lax.psum(proj_sum, "rep", axis_index_groups=across)
    qkv_own = lax.all_gather(qkv_own, "rep", axis=0, tiled=False, axis_index_groups=groups)
    qkv_own = qkv_own.astype(F32)
    grad_qkv = jnp.concatenate(
        [
            qkv_own[:, :, lo:hi].transpose(1, 0, 2).reshape(own, -1)
            for lo, hi in ((0, qw), (qw, qw + hw), (qw + hw, qw + 2 * hw))
        ],
        axis=1,
    )
    proj_all = lax.all_gather(proj_sum, "rep", axis=0, tiled=True, axis_index_groups=groups)
    grad_proj = lax.dynamic_slice_in_dim(proj_all, grp * own, own, 0).astype(F32)
    terms = jnp.concatenate([gain_one_term[:, None], gain_two_term[:, None], router_term], axis=1)
    terms = lax.psum(lax.psum_scatter(terms, "grp", scatter_dimension=0, tiled=True), "rep")
    return (
        output,
        grad_tokens,
        terms[:, 0],
        grad_qkv,
        grad_proj,
        terms[:, 1],
        terms[:, 2:],
        grad_gu,
        grad_dn,
    )


def solution(mesh):
    tok, par = ("rep", "grp"), "grp"
    in_specs = (
        P(tok, None),
        P(par),
        P(par, None),
        P(par, None),
        P(par),
        P(par, None),
        P(par, None, None),
        P(par, None, None),
        P(tok),
        P(tok, None),
        P(tok, None),
        P(tok, None),
    )
    out_specs = (
        P(tok, None),
        P(tok, None),
        P(par),
        P(par, None),
        P(par, None),
        P(par),
        P(par, None),
        P(par, None, None),
        P(par, None, None),
    )
    reps, grps = mesh.shape["rep"], mesh.shape["grp"]

    def body(*args):
        return shards(reps, grps, *args)

    return jax.shard_map(body, mesh=mesh, in_specs=in_specs, out_specs=out_specs, check_vma=False)
```

time: 5110 us -> 1030 us (0.20)
  waiting for transfers between devices: 4520 us -> 454 us
  blocking collectives: 90.7 us -> 230 us
  matrix products: 182 us -> 89.6 us
  other arithmetic: 148 us -> 70.9 us
    reduce_scatter x4 -> x6, waiting for transfers between devices: 2700 us -> 148 us  [the longest x1 111 us: shards(): gw = lax.psum_scatter(gw, 'rep', scatter_dimension=0, tiled=True)]
    all_gather x4 -> x8, waiting for transfers between devices: 1330 us -> 299 us  [the longest x1 98.3 us: shards(): gw = lax.all_gather(gw, 'rep', axis=0, tiled=True)]
    psum x1 -> x2, waiting for transfers between devices: 484 us -> 0.05 us  [the longest x1 0.03 us: shards(): proj_head = lax.psum(proj_rows, 'grp')]
    all_to_all x0 -> x2, blocking collectives: none -> 140 us  [the longest x1 84.3 us: shards(): gw = lax.all_to_all(gw, 'grp', 0, 0, tiled=True)]
    dot_general x20, matrix products: 180 us -> 87.8 us  [the longest x9 22.2 us: dot(): return jnp.dot(a, b, preferred_element_type=F32)]
    concatenate x3 -> x7, other arithmetic: 99.2 us -> 24.9 us  [the longest x1 20.9 us: shards(): gw = jnp.concatenate([gw_gu, gw_dn], axis=2)]
  transfers between devices with their start and end apart: 9 -> 18, of which waited for: 7 -> 11; matrix products, arithmetic and copies ran while one was open for 6% -> 19% of each run, Pallas kernels for 0% -> 0%
where the time goes in v1:
time: 1030 us; the launch traced here: 1020 us
  waiting for transfers between devices  454 us (44%)
  blocking collectives  230 us (22%)
  local copies, waits for them, and re-layouts  154 us (15%)
  matrix products  89.6 us (9%)
  other arithmetic  70.9 us (7%)
  between operations  17.6 us (2%)
    reduce_scatter x1, waiting for transfers between devices, shards(): gw = lax.psum_scatter(gw, 'rep', scatter_dimension=0, tiled=True)  111 us
    all_gather x1, waiting for transfers between devices, shards(): gw = lax.all_gather(gw, 'rep', axis=0, tiled=True)  98.3 us
    all_gather x1, waiting for transfers between devices, shards(): both = lax.all_gather(both, 'rep', axis=0, tiled=False)  88.9 us
    all_to_all x1, blocking collectives, shards(): gw = lax.all_to_all(gw, 'grp', 0, 0, tiled=True)  84.3 us
    unnamed x85, local copies, waits for them, and re-layouts  72.8 us
    all_to_all x1, blocking collectives, shards(): both = lax.all_to_all(both, 'grp', 0, 0, tiled=True)  56 us
    reduce_scatter x1, waiting for transfers between devices, shards(): lax.psum_scatter(gact_part, 'grp', scatter_dimension=0, tiled=True)  33.6 us
    all_gather x1, waiting for transfers between devices, shards(): lax.all_gather(gres_low, 'rep', axis=0, tiled=True, axis_index_groups=gro...  31.3 us
  transfers between devices with their start and end apart: 18, of which 11 were waited for; matrix products, arithmetic and copies ran while one was open for 19% of the time, Pallas kernels for 0%

profile of v1, /device:TPU:0, one launch (start us, length us, event | category | flops | bytes accessed | tf_op | source)
XLA Modules:
  0.0 1020.9 jit_solution(18360861975439800956)
XLA Ops:
  11.4 14.9 %all_gather.42 = bf16[1536,18]{0,1:T(8,128)(2,1)S(1)} all-gather(bf16[384,18]{0,1:T(8,128)(2,1)S(1)} %pad_maximum_fusion.17), channel_id=1, replica_groups=mesh['rep'=8,'grp'=4] {'grp'}, dimensions={0}, use_global_device_ids=true | all-gather | bytes 69120 | tf_op jit(solution)/shard_map/all_gather | solution.py:78
  32.6 8.0 all-reduce
  43.2 30.3 %all_gather.44 = bf16[1536,320]{1,0:T(8,128)(2,1)S(1)} all-gather(bf16[384,320]{1,0:T(8,128)(2,1)S(1)} %pad_maximum_fusion.9), channel_id=1, replica_groups=mesh['rep'=8,'grp'=4] {'grp'}, dimensions={0}, use_global_device_ids=true | all-gather | bytes 1228800 | tf_op jit(solution)/shard_map/all_gather | solution.py:89
  89.5 56.0 %all_to_all.29 = bf16[4,4,48,1536]{3,2,1,0:T(8,128)(2,1)} all-to-all(bf16[4,4,48,1536]{3,2,1,0:T(8,128)(2,1)S(1)} %bitcast.193), channel_id=1, replica_groups=mesh['rep'=8,'grp'=4] {'grp'}, dimensions={0} | all-to-all | bytes 4718592 | tf_op jit(solution)/shard_map/all_to_all | solution.py:100
  154.7 88.9 %all-gather.23.cloned.1.call-done = bf16[32,4,48,1536]{3,2,1,0:T(8,128)(2,1)} async-done(((bf16[4,4,48,1536]{3,2,1,0:T(8,128)(2,1)}), bf16[32,4,48,1536]{3,2,1,0:T(8,128)(2,1)}) %all-gather.23.cloned.1.call-update) | async-done | bytes 18874384 | tf_op jit(solution)/shard_map/all_gather | solution.py:101
  243.6 17.1 %copy.160 = bf16[4,4,8,48,1536]{4,3,2,1,0:T(8,128)(2,1)} copy(bf16[4,4,8,48,1536]{4,3,0,1,2:T(8,128)(2,1)} %bitcast.188) | data formatting | bytes 37748736 | tf_op jit(solution)/shard_map/transpose | solution.py:102
  260.8 22.1 %all-gather.13.cloned.1.call-done = bf16[512,1536]{1,0:T(8,128)(2,1)} async-done(((bf16[128,1536]{1,0:T(8,128)(2,1)}), bf16[512,1536]{1,0:T(8,128)(2,1)}) %all-gather.13.cloned.1.call-update) | async-done | bytes 1572880 | tf_op jit(solution)/shard_map/all_gather | solution.py:137
  282.8 12.3 %fusion.18 = f32[4,512,1024]{1,2,0:T(8,128)} fusion(bf16[4,1536,1536]{2,1,0:T(8,128)(2,1)} %bitcast.184, bf16[512,1536]{1,0:T(8,128)(2,1)} %all-gather.13.cloned.1.call-done), kind=kOutput, calls=%fused_computation.31 | convolution fusion | flops 6442450944 | bytes 22544384 | tf_op jit(solution)/shard_map/td,edh->eth/dot_general | solution.py:140
  295.2 25.2 %all-gather.15.cloned.1.call-done = bf16[512,1536]{1,0:T(8,128)(2,1)} async-done(((bf16[128,1536]{1,0:T(8,128)(2,1)}), bf16[512,1536]{1,0:T(8,128)(2,1)}) %all-gather.15.cloned.1.call-update) | async-done | bytes 1572880 | tf_op jit(solution)/shard_map/all_gather | solution.py:136
  320.3 12.6 %fusion.10 = (f32[4,512]{1,0:T(4,128)}, f32[4,512,512]{2,1,0:T(8,128)}) fusion(f32[4,512,1024]{1,2,0:T(8,128)} %fusion.18, bf16[512,1536]{1,0:T(8,128)(2,1)} %all-gather.15.cloned.1.call-done, bf16[4,1536,1536]{2,1,0:T(8,128)(2,1)} %bitcast.185), kind=kOutput, calls=%fused_computation.19 | convolution fusion | flops 3228563456 | bytes 20455424 | tf_op jit(solution)/shard_map/td,edh->eth/dot_general | solution.py:146
  341.8 13.5 %all_gather.49 = f32[512,16]{0,1:T(8,128)S(1)} all-gather(f32[128,16]{0,1:T(8,128)S(1)} %get-tuple-element.80), channel_id=1, replica_groups=mesh['rep'=8,'grp'=4] {'grp'}, dimensions={0}, use_global_device_ids=true | all-gather | bytes 40960 | tf_op jit(solution)/shard_map/all_gather | solution.py:138
  355.3 6.9 multiply_convert_fusion.1
  364.2 10.8 %fusion.24 = bf16[512,1536]{1,0:T(8,128)(2,1)} fusion(bf16[4,1536,1536]{2,1,0:T(8,128)(2,1)} %bitcast.186, bf16[4,512,512]{1,2,0:T(8,128)(2,1)S(1)} %get-tuple-element.65, bf16[4,512,512]{1,2,0:T(8,128)(2,1)S(1)} %get-tuple-element.64), kind=kOutput, calls=%fused_computation.33 | convolution fusion | flops 6451625984 | bytes 18350080 | tf_op jit(solution)/shard_map/eth,edh->td/dot_general | solution.py:153
  375.1 33.6 %reduce-scatter.14.cloned.1.call-done = bf16[128,1536]{1,0:T(8,128)(2,1)} async-done(((bf16[512,1536]{1,0:T(8,128)(2,1)}), bf16[128,1536]{1,0:T(8,128)(2,1)}) %reduce-scatter.14.cloned.1.call-update) | async-done | bytes 393232 | tf_op jit(solution)/shard_map/reduce_scatter | solution.py:154
  412.3 31.3 %all-gather.17.cloned.1.call-done = bf16[1024,1536]{1,0:T(8,128)(2,1)} async-done(((bf16[128,1536]{1,0:T(8,128)(2,1)}), bf16[1024,1536]{1,0:T(8,128)(2,1)}) %all-gather.17.cloned.1.call-update) | async-done | bytes 3145744 | tf_op jit(solution)/shard_map/all_gather | solution.py:183
  461.6 7.0 convert_bitcast_fusion
  468.6 10.6 %fusion.5 = bf16[4,1536,1024]{1,2,0:T(8,128)(2,1)} fusion(bf16[4,512,512]{1,2,0:T(8,128)(2,1)S(1)} %copy-done.15, bf16[4,512,512]{1,2,0:T(8,128)(2,1)S(1)} %copy-done.13, bf16[512,1536]{1,0:T(8,128)(2,1)S(1)} %copy-done.34), kind=kOutput, calls=%fused_computation.9 | convolution fusion | flops 6457131008 | bytes 18350080 | tf_op jit(solution)/shard_map/td,eth->edh/dot_general | solution.py:157
  480.9 20.9 %pad_maximum_fusion = bf16[4,1536,1536]{1,2,0:T(8,128)(2,1)} fusion(bf16[4,1536,512]{1,2,0:T(8,128)(2,1)} %convert_bitcast_fusion, bf16[4,1536,1024]{1,2,0:T(8,128)(2,1)} %fusion.5), kind=kLoop, calls=%fused_computation.2 | loop fusion | flops 37748736 | bytes 37748736 | tf_op jit(solution)/shard_map/concatenate | solution.py:159
  501.8 24.7 %copy.178 = bf16[4,1536,1536]{2,1,0:T(8,128)(2,1)} copy(bf16[4,1536,1536]{1,2,0:T(8,128)(2,1)} %pad_maximum_fusion) | data formatting | bytes 37748736 | tf_op jit(solution)/shard_map/concatenate | solution.py:159
  526.5 21.6 %copy.179 = bf16[8,4,48,4,1536]{4,3,2,1,0:T(4,128)(2,1)S(1)} copy(bf16[8,4,48,4,1536]{4,2,0,1,3:T(8,128)(2,1)} %bitcast.182) | data formatting | bytes 37748736 | tf_op jit(solution)/shard_map/transpose | solution.py:160
  548.1 9.7 copy.207
  559.4 7.4 fusion.21
  572.7 111.4 %reduce-scatter.20.cloned.1.call-done = bf16[192,6144]{1,0:T(8,128)(2,1)} async-done(((bf16[1536,6144]{1,0:T(8,128)(2,1)}), bf16[192,6144]{1,0:T(8,128)(2,1)}) %reduce-scatter.20.cloned.1.call-update) | async-done | bytes 2359312 | tf_op jit(solution)/shard_map/reduce_scatter | solution.py:162
  687.7 84.3 %all_to_all.30 = bf16[4,48,4,1536]{3,2,1,0:T(4,128)(2,1)S(1)} all-to-all(bf16[4,48,4,1536]{3,2,1,0:T(4,128)(2,1)S(1)} %reshape.284), channel_id=1, replica_groups=mesh['rep'=8,'grp'=4] {'grp'}, dimensions={0} | all-to-all | bytes 4718592 | tf_op jit(solution)/shard_map/all_to_all | solution.py:164
  780.0 23.5 %psum.22 = f32[384,18]{0,1:T(8,128)S(1)} all-reduce(f32[384,18]{0,1:T(8,128)} %reduce-scatter.18.cloned.1.call-done), channel_id=1, replica_groups=mesh['rep'=8,'grp'=4] {'rep'}, use_global_device_ids=true, to_apply=%region_22.23 | all-reduce | flops 6912 | bytes 55296 | tf_op jit(solution)/shard_map/psum | solution.py:227
  814.5 5.5 copy.181
  820.0 29.4 %all-gather.19.cloned.1.call-done = bf16[1536,1536]{1,0:T(8,128)(2,1)} async-done(((bf16[192,1536]{1,0:T(8,128)(2,1)}), bf16[1536,1536]{1,0:T(8,128)(2,1)}) %all-gather.19.cloned.1.call-update) | async-done | bytes 4718608 | tf_op jit(solution)/shard_map/all_gather | solution.py:224
  852.4 98.3 %all-gather.21.cloned.1.call-done = bf16[384,16,1536]{2,0,1:T(8,128)(2,1)} async-done(((bf16[48,16,1536]{2,0,1:T(8,128)(2,1)}), bf16[384,16,1536]{2,0,1:T(8,128)(2,1)}) %all-gather.21.cloned.1.call-update) | async-done | bytes 18874384 | tf_op jit(solution)/shard_map/all_gather | solution.py:166
  950.7 9.3 slice_convert_fusion.1
  960.0 16.6 %copy.183 = f32[384,16,512]{2,1,0:T(8,128)} copy(f32[384,16,512]{2,0,1:T(8,128)} %slice_convert_fusion.1) | data formatting | bytes 25165824
  976.6 7.4 slice_convert_fusion
  984.0 29.1 %copy.182 = f32[384,16,1024]{2,1,0:T(8,128)} copy(f32[384,16,1024]{2,0,1:T(8,128)S(1)} %slice_convert_fusion) | data formatting | bytes 50331648
  (209 shorter events, 103.1 us)
Async XLA Ops:
  8.0 20.4 %copy-start = (bf16[384,1536]{1,0:T(8,128)(2,1)S(1)}, bf16[384,1536]{1,0:T(8,128)(2,1)}, u32[]{:S(2)}) copy-start(bf16[384,1536]{1,0:T(8,128)(2,1)} %param.15) | copy-start | bytes 3538948
  8.0 65.7 %all-gather.11.cloned.1.call-start = ((), (), s32[]{:S(2)}) async-start(), calls=%async_computation.10 | async-start | bytes 3538944 | tf_op jit(solution)/shard_map/all_gather | solution.py:109
  9.3 19.0 %copy-start.27 = (f32[128]{0:T(128)}, f32[128]{0:T(128)S(1)}, u32[]{:S(2)}) copy-start(f32[128]{0:T(128)S(1)} %add_rsqrt_fusion.1) | copy-start | bytes 1540
  28.3 53.1 %all-reduce.4.cloned.1.call-start = ((), (), s32[]{:S(2)}) async-start(), calls=%async_computation.11 | async-start | bytes 1179648 | tf_op jit(solution)/shard_map/psum | solution.py:93
  30.5 115.1 %reduce-scatter.10.cloned.1.call-start = ((), (), s32[]{:S(2)}) async-start(), calls=%async_computation.12 | async-start | bytes 3538944 | tf_op jit(solution)/shard_map/reduce_scatter | solution.py:129
  85.2 158.5 %all-gather.23.cloned.1.call-start = ((), (), s32[]{:S(2)}) async-start(), calls=%async_computation.24 | async-start | bytes 21233664 | tf_op jit(solution)/shard_map/all_gather | solution.py:101
  89.5 56.1 %copy-start.2 = (bf16[128,1536]{1,0:T(8,128)(2,1)S(1)}, bf16[128,1536]{1,0:T(8,128)(2,1)}, u32[]{:S(2)}) copy-start(bf16[128,1536]{1,0:T(8,128)(2,1)} %param.12) | copy-start | bytes 1179652
  145.5 137.3 %all-gather.13.cloned.1.call-start = ((), (), s32[]{:S(2)}) async-start(), calls=%async_computation.13 | async-start | bytes 1966080 | tf_op jit(solution)/shard_map/all_gather | solution.py:137
  146.8 263.4 %copy-start.25 = (f32[128]{0:T(128)}, f32[128]{0:T(128)S(1)}, u32[]{:S(2)}) copy-start(f32[128]{0:T(128)S(1)} %add_rsqrt_fusion) | copy-start | bytes 1540
  148.8 171.5 %all-gather.15.cloned.1.call-start = ((), (), s32[]{:S(2)}) async-start(), calls=%async_computation.15 | async-start | bytes 1966080 | tf_op jit(solution)/shard_map/all_gather | solution.py:136
  332.9 8.8 all-to-all-start.1
  336.1 72.6 %reduce-scatter.14.cloned.1.call-start = ((), (), s32[]{:S(2)}) async-start(), calls=%async_computation.16 | async-start | bytes 1966080 | tf_op jit(solution)/shard_map/reduce_scatter | solution.py:154
  364.2 44.5 %copy-start.3 = (bf16[128,1536]{1,0:T(8,128)(2,1)S(1)}, bf16[128,1536]{1,0:T(8,128)(2,1)}, u32[]{:S(2)}) copy-start(bf16[128,1536]{1,0:T(8,128)(2,1)} %reduce-scatter.10.cloned.1.call-done) | copy-start | bytes 1179652
  375.1 36.0 %copy-start.7 = (bf16[128,1536]{1,0:T(8,128)(2,1)S(1)}, bf16[128,1536]{1,0:T(8,128)(2,1)}, u32[]{:S(2)}) copy-start(bf16[128,1536]{1,0:T(8,128)(2,1)} %param.23) | copy-start | bytes 1179652
  375.1 68.5 %all-gather.17.cloned.1.call-start = ((), (), s32[]{:S(2)}) async-start(), calls=%async_computation.17 | async-start | bytes 3538944 | tf_op jit(solution)/shard_map/all_gather | solution.py:183
  410.2 36.5 %copy-start.31 = (f32[128]{0:T(128)}, f32[128]{0:T(128)S(1)}, u32[]{:S(2)}) copy-start(f32[128]{0:T(128)S(1)} %broadcast_multiply_fusion.1) | copy-start | bytes 1540
  412.2 34.6 %copy-start.23 = (f32[8,3,128]{2,1,0:T(4,128)S(1)}, f32[8,3,128]{2,1,0:T(4,128)}, u32[]{:S(2)}) copy-start(f32[8,3,128]{2,1,0:T(4,128)} %copy-done.22) | copy-start | bytes 36868
  412.2 154.8 %reduce-scatter.16.cloned.1.call-start = ((), (), s32[]{:S(2)}) async-start(), calls=%async_computation.18 | async-start | bytes 3538944 | tf_op jit(solution)/shard_map/reduce_scatter | solution.py:200
  454.7 115.1 %reduce-scatter.22.cloned.1.call-start = ((), (), s32[]{:S(2)}) async-start(), calls=%async_computation.26 | async-start | bytes 1474560
  461.4 110.4 %all-reduce.6.cloned.1.call-start = ((), (), s32[]{:S(2)}) async-start(), calls=%async_computation.20 | async-start | bytes 1179648 | tf_op jit(solution)/shard_map/psum | solution.py:210
  461.6 7.0 copy-start.13
  468.6 10.6 %copy-start.9 = (bf16[1024,1536]{1,0:T(8,128)(2,1)S(1)}, bf16[1024,1536]{1,0:T(8,128)(2,1)}, u32[]{:S(2)}) copy-start(bf16[1024,1536]{1,0:T(8,128)(2,1)} %all-gather.17.cloned.1.call-done) | copy-start | bytes 9437188
  480.9 203.3 %reduce-scatter.20.cloned.1.call-start = ((), (), s32[]{:S(2)}) async-start(), calls=%async_computation.22 | async-start | bytes 21233664 | tf_op jit(solution)/shard_map/reduce_scatter | solution.py:162
  557.8 9.0 copy-start.6
  557.8 9.2 copy-start.19
  557.9 9.2 copy-start.28
  557.9 216.0 %reduce-scatter.12.cloned.1.call-start = ((), (), s32[]{:S(2)}) async-start(), calls=%async_computation.14 | async-start | bytes 1966080 | tf_op jit(solution)/shard_map/reduce_scatter | solution.py:169
  566.8 213.1 %reduce-scatter.18.cloned.1.call-start = ((), (), s32[]{:S(2)}) async-start(), calls=%async_computation.19 | async-start | bytes 184320 | tf_op jit(solution)/shard_map/reduce_scatter | solution.py:227
  569.7 238.7 %all-gather.25.cloned.1.call-start = ((), (), s32[]{:S(2)}) async-start(), calls=%async_computation.25 | async-start | bytes 2211840 | tf_op jit(solution)/shard_map/all_gather | solution.py:215
  571.7 277.7 %all-gather.19.cloned.1.call-start = ((), (), s32[]{:S(2)}) async-start(), calls=%async_computation.21 | async-start | bytes 5308416 | tf_op jit(solution)/shard_map/all_gather | solution.py:224
  572.4 378.2 %all-gather.21.cloned.1.call-start = ((), (), s32[]{:S(2)}) async-start(), calls=%async_computation.23 | async-start | bytes 21233664 | tf_op jit(solution)/shard_map/all_gather | solution.py:166
  984.0 29.1 %copy-start.1 = (bf16[384,1536]{1,0:T(8,128)(2,1)S(1)}, bf16[384,1536]{1,0:T(8,128)(2,1)}, u32[]{:S(2)}) copy-start(bf16[384,1536]{1,0:T(8,128)(2,1)} %param.15) | copy-start | bytes 3538948
  (22 other events, 60.6 us)
Sparse Core Ops, SparseCore 0:
  28.4 33.5 all-gather.10
  85.3 46.5 reduce-scatter.9
  145.7 97.9 all-gather.22
  245.7 37.0 all-gather.12
  284.3 35.9 all-gather.14
  412.3 31.1 all-gather.16
  454.8 46.2 reduce-scatter.15
  503.4 35.9 reduce-scatter.21
  558.0 126.1 reduce-scatter.19
  686.9 60.2 reduce-scatter.11
  750.0 29.9 reduce-scatter.17
  782.4 26.0 all-gather.24
  810.5 38.8 all-gather.18
  851.9 98.7 all-gather.20
Sparse Core Ops, SparseCore 1:
  31.7 48.7 all-reduce.3
  375.2 33.5 reduce-scatter.13
  480.9 51.6 all-reduce.5

commit v2 on v1

--- a/solution.py
+++ b/solution.py
@@ -1,6 +1,8 @@
 import jax
 import jax.numpy as jnp
 from jax import lax
+from jax.experimental import pallas as pl
+from jax.experimental.pallas import tpu as pltpu
 from jax.sharding import PartitionSpec as P
 
 QUERY_HEADS = 24
@@ -14,6 +16,7 @@
 F32 = jnp.float32
 QPK = QUERY_HEADS // KEY_VALUE_HEADS
 BIG = 1 << 20
+MESH = pl.DeviceIdType.MESH
 
 
 def dot(a, b):
@@ -46,6 +49,237 @@
     gate_exp = jnp.where(chosen, jnp.exp(jnp.where(chosen, logits - top_logit, 0.0)), 0.0)
     gates = gate_exp / jnp.sum(gate_exp, axis=1, keepdims=True)
     return gates, kept
+
+
+def place():
+    r, z = lax.axis_index("rep"), lax.axis_index("grp")
+    return r // 4, (r // 2) % 2, r % 2, z
+
+
+def flip(bit, by):
+    return bit + by * (1 - 2 * bit)
+
+
+def grads_kernel(nq, x_ref, dy_ref, ggu_ref, hw_ref, gu_out, dn_out,
+                 gw, recv1, send2, recv2, zs, zr, ag, sb, ib, st,
+                 s1, r1, s2, r2, sz, rz, sa, ra, ss, rs, so):
+    y, x, c, z = place()
+    half = HID // 2
+    wide = 3 * half
+
+    def slot(a, b):
+        return flip(y, a * c + b * (1 - c)) * 2 + flip(x, a * (1 - c) + b * c)
+
+    def dev(p, core, zz):
+        return (p * 2 + core, zz)
+
+    p0 = slot(0, 0)
+    d1, d2, dsib = dev(slot(1, 0), c, z), dev(slot(0, 1), c, z), dev(p0, 1 - c, z)
+    zk = [lax.rem(z + k, 4) for k in range(4)]
+    barrier = pltpu.get_barrier_semaphore()
+    for to in (d1, d2, dsib, dev(p0, c, zk[1]), dev(p0, c, zk[2]), dev(p0, c, zk[3])):
+        pl.semaphore_signal(barrier, 1, device_id=to, device_id_type=MESH)
+    pl.semaphore_wait(barrier, 6)
+
+    def copy1(q, b):
+        return pltpu.make_async_remote_copy(
+            gw.at[q // 2, slot(1, b), q % 2], recv1.at[q, b], s1.at[q, b], r1.at[q, b],
+            device_id=d1, device_id_type=MESH)
+
+    def copy2(q):
+        return pltpu.make_async_remote_copy(
+            send2.at[q % 2], recv2.at[q], s2.at[q], r2.at[q], device_id=d2, device_id_type=MESH)
+
+    def copyz(q, k):
+        return pltpu.make_async_remote_copy(
+            zs.at[q % 2, zk[k]], zr.at[q, z], sz.at[q, k - 1], rz.at[q, k - 1],
+            device_id=dev(p0, c, zk[k]), device_id_type=MESH)
+
+    def copya(q, i):
+        src, dst = ((0, 1), (0, 2), (1, 3))[i]
+        return pltpu.make_async_remote_copy(
+            ag.at[q, src], ag.at[q, dst], sa.at[q, i], ra.at[q, i],
+            device_id=d1 if i == 0 else d2, device_id_type=MESH)
+
+    def copys(q, i):
+        return pltpu.make_async_remote_copy(
+            ag.at[q, i], sb.at[q, i], ss.at[q, i], rs.at[q, i], device_id=dsib, device_id_type=MESH)
+
+    def out_copies(q, k, p, core):
+        rows = 256
+        at = pl.multiple_of(((q // 2) * 128 + p * 32 + (q % 2) * 16) * EXPERTS, rows)
+        lo = pl.multiple_of(core * half, half)
+        hi = pl.multiple_of(HID + core * half, half)
+        pairs = ((gu_out.at[pl.ds(at, rows), pl.ds(lo, half)], 0),
+                 (gu_out.at[pl.ds(at, rows), pl.ds(hi, half)], half),
+                 (dn_out.at[pl.ds(at, rows), pl.ds(lo, half)], 2 * half))
+        return [pltpu.make_async_copy(st.at[k, :, pl.ds(off, half)], ref, so.at[k, i])
+                for i, (ref, off) in enumerate(pairs)]
+
+    def emit(q, k, first, p, core, ref):
+        @pl.when(jnp.logical_not(first))
+        def _():
+            for one in out_copies(q, k, p, core):
+                one.wait()
+        st[k] = ref[...].astype(F32)
+        for one in out_copies(q, k, p, core):
+            one.start()
+
+    def stage1(q):
+        @pl.when(q % 2 == 0)
+        def _():
+            q3 = q // 2
+            xs = jnp.concatenate(
+                [x_ref[:, pl.ds(pl.multiple_of(zz * 384 + q3 * 128, 128), 128)] for zz in range(4)], axis=1)
+            ds_ = jnp.concatenate(
+                [dy_ref[:, pl.ds(pl.multiple_of(zz * 384 + q3 * 128, 128), 128)] for zz in range(4)], axis=1)
+
+            def one(j, _):
+                up = lax.dot_general(xs, ggu_ref[j], (((0,), (0,)), ((), ())),
+                                     preferred_element_type=F32).astype(BF)
+                dn = lax.dot_general(ds_, hw_ref[j], (((0,), (0,)), ((), ())),
+                                     preferred_element_type=F32).astype(BF)
+                for zz in range(4):
+                    for p in range(4):
+                        for h in range(2):
+                            at = zz * 128 + p * 32 + h * 16
+                            gw[q3, p, h, zz, j, :, : 2 * half] = up[at : at + 16]
+                            gw[q3, p, h, zz, j, :, 2 * half :] = dn[at : at + 16]
+                return 0
+            lax.fori_loop(0, 4, one, 0)
+        for b in range(2):
+            copy1(q, b).start()
+
+    def stage2(q):
+        for b in range(2):
+            copy1(q, b).wait_recv()
+
+        def one(zz, _):
+            send2[q % 2, zz] = (gw[q // 2, slot(0, 1), q % 2, zz].astype(F32)
+                                + recv1[q, 1, zz].astype(F32)).astype(BF)
+            return 0
+        lax.fori_loop(0, 4, one, 0)
+        copy2(q).start()
+
+    def stage3(q):
+        copy2(q).wait()
+
+        def one(zz, _):
+            zs[q % 2, zz] = (gw[q // 2, p0, q % 2, zz].astype(F32) + recv1[q, 0, zz].astype(F32)
+                             + recv2[q, zz].astype(F32)).astype(BF)
+            return 0
+        lax.fori_loop(0, 4, one, 0)
+        for k in range(1, 4):
+            copyz(q, k).start()
+        zr[q, z] = zs[q % 2, z]
+
+    def stage4(q):
+        for k in range(1, 4):
+            copyz(q, k).wait()
+        for zz in range(4):
+            for j in range(4):
+                for l in range(wide // 128):
+                    ib[l, pl.ds(zz * 4 + j, 16, stride=EXPERTS), :] = (
+                        zr[q, zz, j, :, l * 128 : (l + 1) * 128].astype(F32))
+        for l in range(wide // 128):
+            ag[q, 0, :, l * 128 : (l + 1) * 128] = ib[l].astype(BF)
+        copya(q, 0).start()
+        copys(q, 0).start()
+
+    def stage5(q):
+        copya(q, 0).wait_recv()
+        copya(q, 1).start()
+        copya(q, 2).start()
+        copys(q, 1).start()
+        emit(q, 0, q == 0, p0, c, ag.at[q, 0])
+        emit(q, 1, q == 0, slot(1, 0), c, ag.at[q, 1])
+
+    def stage6(q):
+        copya(q, 1).wait_recv()
+        copya(q, 2).wait_recv()
+        copys(q, 2).start()
+        copys(q, 3).start()
+        emit(q, 2, q == 0, slot(0, 1), c, ag.at[q, 2])
+        emit(q, 3, q == 0, slot(1, 1), c, ag.at[q, 3])
+
+    def stage7(q):
+        for i in range(4):
+            copys(q, i).wait_recv()
+        for i, p in enumerate((p0, slot(0, 1), slot(1, 0), slot(1, 1))):
+            emit(q, i, False, p, 1 - c, sb.at[q, i])
+        for i in range(4):
+            copys(q, i).wait_send()
+        for i in range(3):
+            copya(q, i).wait_send()
+        for b in range(2):
+            copy1(q, b).wait_send()
+
+    stages = (stage1, stage2, stage3, stage4, stage5, stage6, stage7)
+
+    def step(t, _):
+        for i, stage in enumerate(stages):
+            q = t - i
+
+            @pl.when((q >= 0) & (q < nq))
+            def _(stage=stage, q=q):
+                stage(q)
+        return 0
+
+    lax.fori_loop(0, nq + len(stages) - 1, step, 0)
+    for k in range(4):
+        for one in out_copies(0, k, p0, c):
+            one.wait()
+
+
+def expert_grads(xs, dys, ggu, hw):
+    nq, half, wide = 6, HID // 2, 3 * HID // 2
+    piece = (4, 4, 16, wide)
+    sem = pltpu.SemaphoreType.DMA
+    return pl.pallas_call(
+        lambda *a: grads_kernel(nq, *a),
+        out_shape=(jax.ShapeDtypeStruct((384 * 16, 2 * HID), F32), jax.ShapeDtypeStruct((384 * 16, HID), F32)),
+        in_specs=[pl.BlockSpec(memory_space=pltpu.VMEM)] * 4,
+        out_specs=[pl.BlockSpec(memory_space=pl.ANY)] * 2,
+        scratch_shapes=[
+            pltpu.VMEM((3, 4, 2) + piece, BF),
+            pltpu.VMEM((nq, 2) + piece, BF),
+            pltpu.VMEM((2,) + piece, BF),
+            pltpu.VMEM((nq,) + piece, BF),
+            pltpu.VMEM((2,) + piece, BF),
+            pltpu.VMEM((nq,) + piece, BF),
+            pltpu.VMEM((nq, 4, 256, wide), BF),
+            pltpu.VMEM((nq, 4, 256, wide), BF),
+            pltpu.VMEM((wide // 128, 256, 128), F32),
+            pltpu.VMEM((4, 256, wide), F32),
+            sem((nq, 2)), sem((nq, 2)), sem((nq,)), sem((nq,)), sem((nq, 3)), sem((nq, 3)),
+            sem((nq, 3)), sem((nq, 3)), sem((nq, 4)), sem((nq, 4)), sem((4, 3)),
+        ],
+        compiler_params=pltpu.CompilerParams(
+            collective_id=3, has_side_effects=True, vmem_limit_bytes=62 * 1024 * 1024),
+        name="expert_grads",
+    )(xs, dys, ggu, hw)
+
+
+def expert_grads_general(reps, grps, xs, dys, ggu, hw):
+    local, half, width = ggu.shape[0], HID // 2, xs.shape[1]
+    own = width // grps
+    chips = reps // 2
+    piece = own // chips
+    same_core = [[2 * i + c for i in range(chips)] for c in range(2)]
+    pairs = [[2 * i, 2 * i + 1] for i in range(chips)]
+    up = jnp.einsum("td,eth->edh", xs, ggu, preferred_element_type=F32).astype(BF)
+    down = jnp.einsum("td,eth->edh", dys, hw, preferred_element_type=F32).astype(BF)
+    gw = jnp.concatenate([up, down], axis=2)
+    gw = gw.reshape(local, grps, chips, piece, 3 * half).transpose(2, 1, 3, 0, 4)
+    gw = gw.reshape(chips * grps * piece, local * 3 * half)
+    gw = lax.psum_scatter(gw, "rep", scatter_dimension=0, tiled=True, axis_index_groups=same_core)
+    gw = lax.all_to_all(gw.reshape(grps, piece, local, 3 * half), "grp", 0, 0, tiled=True)
+    gw = gw.transpose(1, 0, 2, 3).reshape(piece, EXPERTS, 3 * half)
+    gw = lax.all_gather(gw, "rep", axis=0, tiled=True, axis_index_groups=same_core)
+    gw = lax.all_gather(gw, "rep", axis=0, tiled=False, axis_index_groups=pairs).astype(F32)
+    gw = gw.reshape(2, own * EXPERTS, 3, half)
+    gw = jnp.moveaxis(gw, 0, 2).reshape(own * EXPERTS, 3 * HID)
+    return gw[:, : 2 * HID], gw[:, 2 * HID :]
 
 
 def shards(
@@ -92,15 +326,25 @@
     proj_rows = jnp.where(mine[:, None], jnp.take(attn_proj, jnp.where(mine, row - grp * own, 0), axis=0), 0)
     proj_head = lax.psum(proj_rows, "grp")
 
-    piece = own // reps
-    gu_piece = lax.dynamic_slice_in_dim(w_gate_up, rep * piece, piece, 0)
-    dn_piece = lax.dynamic_slice_in_dim(w_down, rep * piece, piece, 0)
-    both = jnp.concatenate([gu_piece, dn_piece], axis=2)
-    both = both.reshape(piece, grps, local_experts, 3 * HID).transpose(1, 2, 0, 3)
+    core, chip, chips, half = lax.rem(rep, 2), rep // 2, reps // 2, HID // 2
+    pairs = [[2 * i, 2 * i + 1] for i in range(chips)]
+    same_core = [[2 * i + c for i in range(chips)] for c in range(2)]
+    piece = own // chips
+    gu_piece = lax.dynamic_slice_in_dim(w_gate_up, chip * piece, piece, 0)
+    dn_piece = lax.dynamic_slice_in_dim(w_down, chip * piece, piece, 0)
+    both = jnp.concatenate(
+        [
+            lax.dynamic_slice_in_dim(gu_piece, core * half, half, 2),
+            lax.dynamic_slice_in_dim(gu_piece, HID + core * half, half, 2),
+            lax.dynamic_slice_in_dim(dn_piece, core * half, half, 2),
+        ],
+        axis=2,
+    )
+    both = both.reshape(piece, grps, local_experts, 3 * half).transpose(1, 2, 0, 3)
     both = lax.all_to_all(both, "grp", 0, 0, tiled=True)
-    both = lax.all_gather(both, "rep", axis=0, tiled=False)
-    both = both.transpose(2, 1, 0, 3, 4).reshape(local_experts, width, 3 * HID)
-    wgu, wdn = both[:, :, : 2 * HID], both[:, :, 2 * HID :]
+    both = lax.all_gather(both, "rep", axis=0, tiled=False, axis_index_groups=same_core)
+    both = both.transpose(2, 1, 0, 3, 4).reshape(local_experts, width, 3 * half)
+    wgu, wdn = both[:, :, : 2 * half], both[:, :, 2 * half :]
 
     tokens_f = tokens.astype(F32)
     inverse_one = lax.rsqrt(jnp.mean(tokens_f * tokens_f, axis=1, keepdims=True) + EPS)
@@ -133,12 +377,20 @@
     act_two = (normed_two * gain_two).astype(BF)
     gates, kept = routing(expert_ids, priority, dot(act_two, router))
 
-    dy_all = lax.all_gather(cotangent, "grp", axis=0, tiled=True)
-    x_all = lax.all_gather(act_two, "grp", axis=0, tiled=True)
-    weight = lax.all_gather(jnp.where(kept, gates, 0.0), "grp", axis=0, tiled=True)
+    def column(v):
+        v = lax.all_gather(v, "grp", axis=0, tiled=True)
+        return lax.all_gather(v, "rep", axis=0, tiled=True, axis_index_groups=pairs)
+
+    def to_owners(v):
+        v = lax.psum_scatter(v, "rep", scatter_dimension=0, tiled=True, axis_index_groups=pairs)
+        return lax.psum_scatter(v, "grp", scatter_dimension=0, tiled=True).astype(F32)
+
+    dy_all = column(cotangent)
+    x_all = column(act_two)
+    weight = column(jnp.where(kept, gates, 0.0))
     weight = lax.dynamic_slice_in_dim(weight, grp * local_experts, local_experts, 1).T[:, :, None]
     gate_up = jnp.einsum("td,edh->eth", x_all, wgu, preferred_element_type=F32)
-    g, u = gate_up[..., :HID], gate_up[..., HID:]
+    g, u = gate_up[..., :half], gate_up[..., half:]
     sig = jax.nn.sigmoid(g)
     silu = g * sig
     hidden = silu * u
@@ -151,23 +403,20 @@
     ).astype(BF)
     out_part = jnp.einsum("eth,edh->td", hidden_w, wdn, preferred_element_type=F32).astype(BF)
     gact_part = jnp.einsum("eth,edh->td", ggu, wgu, preferred_element_type=F32).astype(BF)
-    gact = lax.psum_scatter(gact_part, "grp", scatter_dimension=0, tiled=True).astype(F32)
-    grad_gates = lax.all_to_all(grad_gate_part.T, "grp", 0, 1, tiled=True)
+    gact = to_owners(gact_part)
+    grad_gates = lax.psum_scatter(
+        grad_gate_part.T, "rep", scatter_dimension=0, tiled=True, axis_index_groups=pairs
+    )
+    grad_gates = lax.all_to_all(grad_gates, "grp", 0, 1, tiled=True)
     grad_gates = jnp.where(kept, grad_gates, 0.0)
-    gw_gu = jnp.einsum("td,eth->edh", x_all, ggu, preferred_element_type=F32).astype(BF)
-    gw_dn = jnp.einsum("td,eth->edh", dy_all, hidden_w, preferred_element_type=F32).astype(BF)
-    gw = jnp.concatenate([gw_gu, gw_dn], axis=2)
-    gw = gw.reshape(local_experts, grps, reps, piece, 3 * HID).transpose(2, 1, 3, 0, 4)
-    gw = gw.reshape(reps * grps * piece, EXPERTS // grps * 3 * HID)
-    gw = lax.psum_scatter(gw, "rep", scatter_dimension=0, tiled=True)
-    gw = gw.reshape(grps, piece, local_experts, 3 * HID)
-    gw = lax.all_to_all(gw, "grp", 0, 0, tiled=True)
-    gw = gw.transpose(1, 0, 2, 3).reshape(piece, EXPERTS, 3 * HID)
-    gw = lax.all_gather(gw, "rep", axis=0, tiled=True)
-    grad_gu = gw[:, :, : 2 * HID].astype(F32)
-    grad_dn = gw[:, :, 2 * HID :].astype(F32)
-    out = lax.psum_scatter(out_part, "grp", scatter_dimension=0, tiled=True).astype(F32)
+    out = to_owners(out_part)
     output = (residual + out).astype(BF)
+    if (reps, grps) == (8, 4):
+        grad_gu, grad_dn = expert_grads(x_all, dy_all, ggu, hidden_w)
+    else:
+        grad_gu, grad_dn = expert_grads_general(reps, grps, x_all, dy_all, ggu, hidden_w)
+    grad_gu = grad_gu.reshape(own, EXPERTS, 2 * HID)
+    grad_dn = grad_dn.reshape(own, EXPERTS, HID)
 
     grad_logits = (gates * (grad_gates - jnp.sum(gates * grad_gates, axis=1, keepdims=True))).astype(BF)
     gact = gact + dot(grad_logits, router.T)

time: 1030 us -> 930 us (0.903)
  Pallas kernels: 0 us -> 184 us
  blocking collectives: 230 us -> 92.9 us
  local copies, waits for them, and re-layouts: 154 us -> 73.2 us
  other arithmetic: 70.9 us -> 38.4 us
  matrix products: 89.6 us -> 62.4 us
  waiting for transfers between devices: 454 us -> 442 us
    pallas_call x0 -> x1, Pallas kernels: none -> 184 us  [expert_grads(): pl.pallas_call(lambda *a: grads_kernel(nq, *a), out_shape=(jax.ShapeDtype...]
    all_to_all x2 -> x0, blocking collectives: 140 us -> none  [the longest x1 84.3 us: shards(): gw = lax.all_to_all(gw, 'grp', 0, 0, tiled=True)]
    all_gather x4 -> x5, waiting for transfers between devices: 234 us -> 123 us  [the longest x1 93.2 us: shards(): lax.all_gather(both, 'rep', axis=0, tiled=False, axis_index_groups=same_c...]
    reduce_scatter x3 -> x4, waiting for transfers between devices: 145 us -> 47.6 us  [the longest x2 38.6 us: to_owners(): lax.psum_scatter(v, 'grp', scatter_dimension=0, tiled=True).astype(F32)]
    all_to_all x1 -> x2, waiting for transfers between devices: 5.48 us -> 83.9 us  [the longest x1 78.4 us: shards(): both = lax.all_to_all(both, 'grp', 0, 0, tiled=True)]
    reduce_scatter x1, waiting for transfers between devices: 0.02 us -> 46.4 us  [shards(): lax.psum_scatter(part, 'rep', scatter_dimension=0, tiled=True, axis_index...]
    unnamed x18 -> x22, waiting for transfers between devices: 1.25 us -> 41.2 us
    psum x1, waiting for transfers between devices: 0.03 us -> 38.5 us  [shards(): proj_sum = lax.psum(proj_term.astype(BF), 'grp')]
  transfers between devices with their start and end apart: 18 -> 22, of which waited for: 11 -> 14; matrix products, arithmetic and copies ran while one was open for 19% -> 10% of each run, Pallas kernels for 0% -> 20%
where the time goes in v2:
time: 930 us; the launch traced here: 921 us
  waiting for transfers between devices  442 us (48%)
  Pallas kernels  184 us (20%)
  blocking collectives  92.9 us (10%)
  local copies, waits for them, and re-layouts  73.2 us (8%)
  matrix products  62.4 us (7%)
  other arithmetic  38.4 us (4%)
  between operations  17.5 us (2%)
  starting transfers between devices  10.8 us (1%)
    pallas_call x1, Pallas kernels, expert_grads(): pl.pallas_call(lambda *a: grads_kernel(nq, *a), out_shape=(jax.ShapeDtype...  184 us
    all_gather x1, waiting for transfers between devices, shards(): lax.all_gather(both, 'rep', axis=0, tiled=False, axis_index_groups=same_c...  93.2 us
    all_to_all x1, waiting for transfers between devices, shards(): both = lax.all_to_all(both, 'grp', 0, 0, tiled=True)  78.4 us
    unnamed x100, local copies, waits for them, and re-layouts  51.7 us
    reduce_scatter x1, waiting for transfers between devices, shards(): lax.psum_scatter(part, 'rep', scatter_dimension=0, tiled=True, axis_index...  46.4 us
    unnamed x22, waiting for transfers between devices  41.2 us
    reduce_scatter x2, waiting for transfers between devices, to_owners(): lax.psum_scatter(v, 'grp', scatter_dimension=0, tiled=True).astype(F32)  38.6 us
    psum x1, waiting for transfers between devices, shards(): proj_sum = lax.psum(proj_term.astype(BF), 'grp')  38.5 us
  transfers between devices with their start and end apart: 22, of which 14 were waited for; matrix products, arithmetic and copies ran while one was open for 10% of the time, Pallas kernels for 20%

profile of v2, /device:TPU:0, one launch (start us, length us, event | category | flops | bytes accessed | tf_op | source)
XLA Modules:
  0.0 921.4 jit_solution(8978316099057609998)
XLA Ops:
  11.4 14.9 %all_gather.48 = bf16[1536,18]{0,1:T(8,128)(2,1)S(1)} all-gather(bf16[384,18]{0,1:T(8,128)(2,1)S(1)} %pad_maximum_fusion.14), channel_id=1, replica_groups=mesh['rep'=8,'grp'=4] {'grp'}, dimensions={0}, use_global_device_ids=true | all-gather | bytes 69120 | tf_op jit(solution)/shard_map/all_gather | solution.py:312
  33.2 8.0 all-reduce
  44.4 30.8 %all_gather.50 = bf16[1536,320]{1,0:T(8,128)(2,1)S(1)} all-gather(bf16[384,320]{1,0:T(8,128)(2,1)S(1)} %pad_maximum_fusion.6), channel_id=1, replica_groups=mesh['rep'=8,'grp'=4] {'grp'}, dimensions={0}, use_global_device_ids=true | all-gather | bytes 1228800 | tf_op jit(solution)/shard_map/all_gather | solution.py:323
  85.9 46.4 %reduce-scatter.14.cloned.1.call-done = bf16[128,1536]{1,0:T(8,128)(2,1)} async-done(((bf16[1024,1536]{1,0:T(8,128)(2,1)}), bf16[128,1536]{1,0:T(8,128)(2,1)}) %reduce-scatter.14.cloned.1.call-update) | async-done | bytes 393232 | tf_op jit(solution)/shard_map/reduce_scatter | solution.py:373
  140.9 4.6 all-to-all-start
  146.2 78.4 %all-to-all-done = bf16[4,4,96,768]{3,2,1,0:T(8,128)(2,1)S(1)} async-done(((bf16[4,4,96,768]{3,2,1,0:T(8,128)(2,1)}), bf16[4,4,96,768]{3,2,1,0:T(8,128)(2,1)S(1)}, u32[]{:S(2)}, u32[]{:S(2)}) %all-to-all-start) | async-done | bytes 2359328 | tf_op jit(solution)/shard_map/all_to_all | solution.py:344
  226.8 21.5 %all-gather.18.cloned.1.call-done = bf16[512,1536]{1,0:T(8,128)(2,1)} async-done(((bf16[128,1536]{1,0:T(8,128)(2,1)}), bf16[512,1536]{1,0:T(8,128)(2,1)}) %all-gather.18.cloned.1.call-update) | async-done | bytes 1572880 | tf_op jit(solution)/shard_map/all_gather | solution.py:381
  252.6 93.2 %all-gather.26.cloned.1.call-done = bf16[16,4,96,768]{3,2,1,0:T(8,128)(2,1)} async-done(((bf16[4,4,96,768]{3,2,1,0:T(8,128)(2,1)}), bf16[16,4,96,768]{3,2,1,0:T(8,128)(2,1)}) %all-gather.26.cloned.1.call-update) | async-done | bytes 9437200 | tf_op jit(solution)/shard_map/all_gather | solution.py:345
  345.8 8.3 copy.120
  354.1 5.4 all-gather.16.cloned.1.call-done.a_0_
  359.5 11.7 %fusion.9 = f32[4,1024,512]{2,1,0:T(8,128)} fusion(bf16[4,1536,768]{2,1,0:T(8,128)(2,1)} %bitcast.167, bf16[1024,1536]{1,0:T(8,128)(2,1)} %all-gather.16.cloned.1.call-done.a_0_), kind=kOutput, calls=%fused_computation.21 | convolution fusion | flops 6442450944 | bytes 17825792 | tf_op jit(solution)/shard_map/td,edh->eth/dot_general | solution.py:392
  374.4 10.9 %fusion.5 = (f32[4,1024]{1,0:T(4,128)S(1)}, f32[4,256,1024]{1,2,0:T(8,128)}) fusion(f32[4,1024,512]{2,1,0:T(8,128)} %fusion.9, bf16[4,1536,768]{2,1,0:T(8,128)(2,1)} %bitcast.168, bf16[1024,1536]{1,0:T(8,128)(2,1)} %all-gather.20.cloned.1.call-done.a_1_), kind=kOutput, calls=%fused_computation.11 | convolution fusion | flops 3228561408 | bytes 18890752 | tf_op jit(solution)/shard_map/td,edh->eth/dot_general | solution.py:398
  386.6 9.0 reduce-scatter.28.cloned.1.call-done
  397.2 4.8 all-to-all-start.1
  402.1 5.6 all-to-all-done.1
  407.7 13.1 %all_gather.56 = f32[512,16]{0,1:T(8,128)S(1)} all-gather(f32[128,16]{0,1:T(8,128)S(1)} %get-tuple-element.77), channel_id=1, replica_groups=mesh['rep'=8,'grp'=4] {'grp'}, dimensions={0}, use_global_device_ids=true | all-gather | bytes 40960 | tf_op jit(solution)/shard_map/all_gather | solution.py:381
  422.7 7.1 multiply_convert_fusion.1
  431.8 8.1 bitcast_convert_fusion
  439.9 9.0 reduce-scatter.20.cloned.1.call-done
  449.2 38.6 %reduce-scatter.22.cloned.1.call-done = bf16[128,1536]{1,0:T(8,128)(2,1)} async-done(((bf16[512,1536]{1,0:T(8,128)(2,1)}), bf16[128,1536]{1,0:T(8,128)(2,1)}) %reduce-scatter.22.cloned.1.call-update) | async-done | bytes 393232 | tf_op jit(solution)/shard_map/reduce_scatter | solution.py:386
  492.4 6.7 bitcast_convert_fusion.1
  499.2 24.5 %all-gather.22.cloned.1.call-done = bf16[1024,1536]{1,0:T(8,128)(2,1)} async-done(((bf16[128,1536]{1,0:T(8,128)(2,1)}), bf16[1024,1536]{1,0:T(8,128)(2,1)}) %all-gather.22.cloned.1.call-update) | async-done | bytes 3145744 | tf_op jit(solution)/shard_map/all_gather | solution.py:432
  538.7 3.8 convolution_convert_fusion.3
  543.4 36.8 %reduce-scatter.24.cloned.1.call-done = bf16[128,1536]{1,0:T(8,128)(2,1)} async-done(((bf16[1024,1536]{1,0:T(8,128)(2,1)}), bf16[128,1536]{1,0:T(8,128)(2,1)}) %reduce-scatter.24.cloned.1.call-update) | async-done | bytes 393232 | tf_op jit(solution)/shard_map/reduce_scatter | solution.py:449
  582.4 30.1 %reduce-scatter.30.cloned.1.call-done = bf16[384,320]{1,0:T(8,128)(2,1)} async-done(((bf16[1536,320]{1,0:T(8,128)(2,1)}), bf16[384,320]{1,0:T(8,128)(2,1)}) %reduce-scatter.30.cloned.1.call-update) | async-done | bytes 245776
  614.6 38.5 %all-reduce.6.cloned.1.call-done = bf16[192,1536]{1,0:T(8,128)(2,1)} async-done(((bf16[192,1536]{1,0:T(8,128)(2,1)}), bf16[192,1536]{1,0:T(8,128)(2,1)}) %all-reduce.6.cloned.1.call-update) | async-done | bytes 589840 | tf_op jit(solution)/shard_map/psum | solution.py:459
  653.2 3.9 pad_maximum_fusion.a_2_
  657.1 183.8 %expert_grads.1 = (f32[6144,1024]{1,0:T(8,128)}, f32[6144,512]{1,0:T(8,128)}) custom-call(bf16[1024,1536]{1,0:T(8,128)(2,1)} %all-gather.16.cloned.1.call-done.a_0_, bf16[1024,1536]{1,0:T(8,128)(2,1)} %all-gather.20.cloned.1.call-done.a_1_, bf16[4,1024,512]{2,1,0:T(8,128)(2,1)} %pad_maximum_fusion.a_2_, bf16[4,1024,256]{2,1,0:T(8,128)(2,1)} %get-tuple-element.63.a_3_), custom_call_target="tpu_custom_call" | custom-call | tf_op jit(solution)/shard_map/expert_grads/pallas_call | solution.py:238
  843.6 24.2 %psum.22 = f32[384,18]{0,1:T(8,128)S(1)} all-reduce(f32[384,18]{0,1:T(8,128)} %reduce-scatter.26.cloned.1.call-done), channel_id=1, replica_groups=mesh['rep'=8,'grp'=4] {'rep'}, use_global_device_ids=true, to_apply=%region_25.26 | all-reduce | flops 6912 | bytes 55296 | tf_op jit(solution)/shard_map/psum | solution.py:476
  875.1 5.4 copy.139
  883.5 17.7 %copy.204 = f32[384,16,1024]{2,1,0:T(8,128)} copy(f32[384,16,1024]{2,1,0:T(8,128)} %bitcast.162) | data formatting | bytes 50331648
  901.2 12.4 %copy.205 = f32[384,16,512]{2,1,0:T(8,128)} copy(f32[384,16,512]{2,1,0:T(8,128)} %bitcast.166) | data formatting | bytes 25165824
  (227 shorter events, 86.7 us)
Async XLA Ops:
  8.0 67.4 %all-gather.12.cloned.1.call-start = ((), (), s32[]{:S(2)}) async-start(), calls=%async_computation.11 | async-start | bytes 3538944 | tf_op jit(solution)/shard_map/all_gather | solution.py:353
  28.9 52.4 %all-reduce.4.cloned.1.call-start = ((), (), s32[]{:S(2)}) async-start(), calls=%async_computation.12 | async-start | bytes 1179648 | tf_op jit(solution)/shard_map/psum | solution.py:327
  31.1 101.1 %reduce-scatter.14.cloned.1.call-start = ((), (), s32[]{:S(2)}) async-start(), calls=%async_computation.13 | async-start | bytes 3538944 | tf_op jit(solution)/shard_map/reduce_scatter | solution.py:373
  85.8 46.4 %copy-start.2 = (bf16[128,1536]{1,0:T(8,128)(2,1)S(1)}, bf16[128,1536]{1,0:T(8,128)(2,1)}, u32[]{:S(2)}) copy-start(bf16[128,1536]{1,0:T(8,128)(2,1)} %param.12) | copy-start | bytes 1179652
  85.8 140.2 %all-gather.14.cloned.1.call-start = ((), (), s32[]{:S(2)}) async-start(), calls=%async_computation.14 | async-start | bytes 1966080 | tf_op jit(solution)/shard_map/all_gather | solution.py:381
  140.9 83.6 %all-to-all-start = ((bf16[4,4,96,768]{3,2,1,0:T(8,128)(2,1)}), bf16[4,4,96,768]{3,2,1,0:T(8,128)(2,1)S(1)}, u32[]{:S(2)}, u32[]{:S(2)}) async-start(bf16[4,4,96,768]{3,2,1,0:T(8,128)(2,1)} %bitcast.174), calls=%async_computation.1 | async-start | bytes 4718592 | tf_op jit(solution)/shard_map/all_to_all | solution.py:344
  145.5 103.5 %copy-start.38 = (s32[1,1024]{1,0:T(1,128)S(1)}, s32[1,1024]{1,0:T(1,128)}, u32[]{:S(2)}) copy-start(s32[1,1024]{1,0:T(1,128)} %param.22) | copy-start | bytes 12292
  145.5 104.3 %copy-start.33 = (s32[128,8]{0,1:T(8,128)S(1)}, s32[128,8]{0,1:T(8,128)}, u32[]{:S(2)}) copy-start(s32[128,8]{0,1:T(8,128)} %param.21) | copy-start | bytes 12292
  145.5 102.7 %all-gather.18.cloned.1.call-start = ((), (), s32[]{:S(2)}) async-start(), calls=%async_computation.18 | async-start | bytes 1966080 | tf_op jit(solution)/shard_map/all_gather | solution.py:381
  146.1 199.7 %all-gather.26.cloned.1.call-start = ((), (), s32[]{:S(2)}) async-start(), calls=%async_computation.27 | async-start | bytes 11796480 | tf_op jit(solution)/shard_map/all_gather | solution.py:345
  226.0 133.5 %all-gather.16.cloned.1.call-start = ((), (), s32[]{:S(2)}) async-start(), calls=%async_computation.15 | async-start | bytes 4718592 | tf_op jit(solution)/shard_map/all_gather | solution.py:382
  226.7 147.7 %all-gather.20.cloned.1.call-start = ((), (), s32[]{:S(2)}) async-start(), calls=%async_computation.19 | async-start | bytes 4718592 | tf_op jit(solution)/shard_map/all_gather | solution.py:382
  248.3 147.3 %reduce-scatter.28.cloned.1.call-start = ((), (), s32[]{:S(2)}) async-start(), calls=%async_computation.29 | async-start | bytes 786432
  386.3 45.5 %slice-start = ((s8[9437184]{0:T(1024)(128)(4,1)}), s8[1048576]{0:T(1024)(128)(4,1)S(1)}, s32[]{:S(2)}) async-start(s8[9437184]{0:T(1024)(128)(4,1)} %bitcast.170), calls=%async_computation.31 | async-start | bytes 2097152
  397.2 10.4 %all-to-all-start.1 = ((f32[4,128,4]{1,2,0:T(4,128)}), f32[4,128,4]{1,2,0:T(4,128)S(1)}, u32[]{:S(2)}, u32[]{:S(2)}) async-start(f32[4,128,4]{1,2,0:T(4,128)} %bitcast.23), calls=%async_computation.6 | async-start | bytes 16384 | tf_op jit(solution)/shard_map/all_to_all | solution.py:410
  402.0 46.9 %reduce-scatter.20.cloned.1.call-start = ((), (), s32[]{:S(2)}) async-start(), calls=%async_computation.20 | async-start | bytes 4718592 | tf_op jit(solution)/shard_map/reduce_scatter | solution.py:385
  439.9 47.9 %copy-start.3 = (bf16[128,1536]{1,0:T(8,128)(2,1)S(1)}, bf16[128,1536]{1,0:T(8,128)(2,1)}, u32[]{:S(2)}) copy-start(bf16[128,1536]{1,0:T(8,128)(2,1)} %reduce-scatter.14.cloned.1.call-done) | copy-start | bytes 1179652
  439.9 47.9 %copy-start.35 = (f32[128]{0:T(128)S(1)}, f32[128]{0:T(128)}, u32[]{:S(2)}) copy-start(f32[128]{0:T(128)} %copy-done.34) | copy-start | bytes 1540
  439.9 47.9 %reduce-scatter.22.cloned.1.call-start = ((), (), s32[]{:S(2)}) async-start(), calls=%async_computation.21 | async-start | bytes 1966080 | tf_op jit(solution)/shard_map/reduce_scatter | solution.py:386
  448.9 43.4 %copy-start.5 = (bf16[4,1024,256]{2,1,0:T(8,128)(2,1)S(1)}, bf16[4,1024,256]{2,1,0:T(8,128)(2,1)}, u32[]{:S(2)}) copy-start(bf16[4,1024,256]{2,1,0:T(8,128)(2,1)} %get-tuple-element.63.a_3_) | copy-start | bytes 6291460
  449.0 74.7 %all-gather.22.cloned.1.call-start = ((), (), s32[]{:S(2)}) async-start(), calls=%async_computation.22 | async-start | bytes 3538944 | tf_op jit(solution)/shard_map/all_gather | solution.py:432
  492.3 50.2 %reduce-scatter.16.cloned.1.call-start = ((), (), s32[]{:S(2)}) async-start(), calls=%async_computation.16 | async-start | bytes 4718592 | tf_op jit(solution)/shard_map/reduce_scatter | solution.py:385
  499.1 81.1 %reduce-scatter.24.cloned.1.call-start = ((), (), s32[]{:S(2)}) async-start(), calls=%async_computation.23 | async-start | bytes 3538944 | tf_op jit(solution)/shard_map/reduce_scatter | solution.py:449
  534.1 78.4 %reduce-scatter.30.cloned.1.call-start = ((), (), s32[]{:S(2)}) async-start(), calls=%async_computation.30 | async-start | bytes 1474560
  538.6 114.5 %all-reduce.6.cloned.1.call-start = ((), (), s32[]{:S(2)}) async-start(), calls=%async_computation.25 | async-start | bytes 1179648 | tf_op jit(solution)/shard_map/psum | solution.py:459
  542.4 110.7 %copy-start.7 = (bf16[4,1024,256]{2,1,0:T(8,128)(2,1)S(1)}, bf16[4,1024,256]{2,1,0:T(8,128)(2,1)}, u32[]{:S(2)}) copy-start(bf16[4,1024,256]{2,1,0:T(8,128)(2,1)} %copy-done.6) | copy-start | bytes 6291460
  542.5 298.4 %reduce-scatter.18.cloned.1.call-start = ((), (), s32[]{:S(2)}) async-start(), calls=%async_computation.17 | async-start | bytes 1966080 | tf_op jit(solution)/shard_map/reduce_scatter | solution.py:386
  543.2 300.4 %reduce-scatter.26.cloned.1.call-start = ((), (), s32[]{:S(2)}) async-start(), calls=%async_computation.24 | async-start | bytes 184320 | tf_op jit(solution)/shard_map/reduce_scatter | solution.py:476
  582.3 286.7 %all-gather.28.cloned.1.call-start = ((), (), s32[]{:S(2)}) async-start(), calls=%async_computation.28 | async-start | bytes 2211840 | tf_op jit(solution)/shard_map/all_gather | solution.py:464
  614.3 266.2 %all-gather.24.cloned.1.call-start = ((), (), s32[]{:S(2)}) async-start(), calls=%async_computation.26 | async-start | bytes 5308416 | tf_op jit(solution)/shard_map/all_gather | solution.py:473
  657.1 183.9 %copy-start.10 = (f32[128,1536]{1,0:T(8,128)S(1)}, f32[128,1536]{1,0:T(8,128)}, u32[]{:S(2)}) copy-start(f32[128,1536]{1,0:T(8,128)} %copy-done.9) | copy-start | bytes 2359300
  657.1 183.9 %copy-start.14 = (bf16[128,1536]{1,0:T(8,128)(2,1)S(1)}, bf16[128,1536]{1,0:T(8,128)(2,1)}, u32[]{:S(2)}) copy-start(bf16[128,1536]{1,0:T(8,128)(2,1)} %param.23) | copy-start | bytes 1179652
  (33 other events, 314.7 us)
Sparse Core Ops, SparseCore 0:
  29.0 33.5 all-gather.11
  85.9 46.2 reduce-scatter.13
  492.4 31.1 all-gather.21
  614.4 26.2 all-gather.27
  653.3 49.8 all-gather.23
Sparse Core Ops, SparseCore 1:
  32.3 48.3 all-reduce.3
  135.4 61.4 all-gather.13
  198.4 49.8 all-gather.17
  250.9 94.9 all-gather.25
  347.5 12.0 all-gather.15
  361.1 13.2 all-gather.19
  386.4 9.1 reduce-scatter.27
  440.0 8.9 reduce-scatter.19
  451.2 36.5 reduce-scatter.21
  499.2 9.6 reduce-scatter.15
  534.1 46.1 reduce-scatter.23
  583.3 29.2 reduce-scatter.29
  614.8 38.2 all-reduce.5
  655.5 34.8 reduce-scatter.17
  693.3 18.4 reduce-scatter.25

commit v3 on v2

--- a/solution.py
+++ b/solution.py
@@ -37,14 +37,18 @@
     return jnp.concatenate([a * cos - b * sin, b * cos + a * sin], axis=-1)
 
 
-def routing(expert_ids, priority, logits):
+def choices(expert_ids, priority):
     seq, top = expert_ids.shape
     choose = expert_ids[:, :, None] == jnp.arange(EXPERTS, dtype=jnp.int32)[None, None, :]
     chosen = jnp.any(choose, axis=1)
     rank_of = jnp.sum(jnp.where(choose, priority.reshape(seq, top)[:, :, None], 0), axis=1)
     rank_of = jnp.where(chosen, rank_of, BIG)
     slot = jnp.sum((rank_of[None, :, :] < rank_of[:, None, :]).astype(jnp.int32), axis=1)
-    kept = chosen & (slot < CAP)
+    return chosen, chosen & (slot < CAP)
+
+
+def routing(expert_ids, priority, logits):
+    chosen, kept = choices(expert_ids, priority)
     top_logit = jnp.max(jnp.where(chosen, logits, -jnp.inf), axis=1, keepdims=True)
     gate_exp = jnp.where(chosen, jnp.exp(jnp.where(chosen, logits - top_logit, 0.0)), 0.0)
     gates = gate_exp / jnp.sum(gate_exp, axis=1, keepdims=True)
@@ -260,6 +264,434 @@
     )(xs, dys, ggu, hw)
 
 
+def turn(v, cos, sin):
+    lane = lax.broadcasted_iota(jnp.int32, v.shape, 1)
+    partner = jnp.where(lax.rem(lane, 64) < 32, pltpu.roll(v, 96, 1), pltpu.roll(v, 32, 1))
+    return v * cos + partner * sin
+
+
+def front_kernel(tok, dy, wpiece, qkv_cols, proj, small, masks, prefix, cos_t, sin_t,
+                 o_x, o_dy, o_ggu, o_hw, o_act, o_q, o_k, o_v, o_probs, o_att, o_qkvw, o_projw,
+                 o_small, o_res, o_gates, o_gact, o_gg, o_out,
+                 smalls, qkvw, projw, actp, pre, pr, qs, ks, vs, probs, att, part, sibr, sums, plr,
+                 xall, dyall, wgt, wbuf, ggu, hw, gpart, opart, ggp, gsib, osib, ggsib,
+                 gsum, osum, ggsum, grecv, orecv, ggrecv, res, gates, gact, ggt, outb,
+                 s_small, r_small, s_qkv, r_qkv, s_proj, r_proj, s_wz, r_wz, s_wp, r_wp,
+                 s_act, r_act, s_pre, r_pre, s_actc, r_actc, s_prec, r_prec, s_sib, r_sib, s_pl, r_pl,
+                 s_x, r_x, s_xc, r_xc, s_y, r_y, s_yc, r_yc, s_w, r_w, s_wc, r_wc,
+                 s_g, r_g, s_o, r_o, s_gg, r_gg, s_gc, r_gc, s_oc, r_oc, s_ggc, r_ggc, sl):
+    y, x, c, z = place()
+    half = HID // 2
+
+    def slot(a, b):
+        return flip(y, a * c + b * (1 - c)) * 2 + flip(x, a * (1 - c) + b * c)
+
+    p0, p1, p2, p3 = slot(0, 0), slot(1, 0), slot(0, 1), slot(1, 1)
+    peers = (p1, p2, p3)
+    d1, d2, dsib = (p1 * 2 + c, z), (p2 * 2 + c, z), (p0 * 2 + 1 - c, z)
+    dpl = [(p * 2 + c, z) for p in peers]
+    zk = [lax.rem(z + k, 4) for k in range(4)]
+    zf = [lax.rem(z + 4 - k, 4) for k in range(4)]
+    dz = [(p0 * 2 + c, zz) for zz in zk]
+
+    barrier = pltpu.get_barrier_semaphore()
+    for to in dpl + dz[1:] + [dsib]:
+        pl.semaphore_signal(barrier, 1, device_id=to, device_id_type=MESH)
+    pl.semaphore_wait(barrier, 7)
+
+    def remote(src, dst, s, r, to):
+        return pltpu.make_async_remote_copy(src, dst, s, r, device_id=to, device_id_type=MESH)
+
+    def c_small(k):
+        return remote(small, smalls.at[z], s_small.at[k - 1], r_small.at[k - 1], dz[k])
+
+    def c_qkv(k):
+        return remote(qkv_cols, qkvw.at[pl.ds(pl.multiple_of(z * 384, 384), 384)],
+                      s_qkv.at[k - 1], r_qkv.at[k - 1], dz[k])
+
+    def rows(zz, pp):
+        return pl.ds(pl.multiple_of(zz * 384 + pp * 96, 96), 96)
+
+    def c_wz(k):
+        return remote(wpiece.at[zk[k]], wbuf.at[:, rows(z, p0)], s_wz.at[k - 1], r_wz.at[k - 1], dz[k])
+
+    def c_wp(k, i):
+        zz = zf[k]
+        who, pp = ((d1, p0), (d2, p0), (d2, p1))[i]
+        src = wpiece.at[z] if (k == 0 and i < 2) else wbuf.at[:, rows(zz, pp)]
+        return remote(src, wbuf.at[:, rows(zz, pp)], s_wp.at[k, i], r_wp.at[k, i], who)
+
+    up_ok, down_ok = (z >= p0) & (z < 3), (z <= p0) & (z > 0)
+
+    def c_proj(src, d):
+        return remote(src, projw, s_proj.at[d], r_proj, (p0 * 2 + c, z + 1 if d == 0 else z - 1))
+
+    def c_act(i):
+        return remote(actp.at[c, p0], actp.at[c, p0], s_act.at[i], r_act.at[i], dpl[i])
+
+    def c_pre(i):
+        return remote(pre.at[c, p0], pre.at[c, p0], s_pre.at[i], r_pre.at[i], dpl[i])
+
+    def c_actc(i):
+        p = (p0, p1, p2, p3)[i]
+        return remote(actp.at[c, p], actp.at[c, p], s_actc.at[i], r_actc.at[i], dsib)
+
+    def c_prec(i):
+        p = (p0, p1, p2, p3)[i]
+        return remote(pre.at[c, p], pre.at[c, p], s_prec.at[i], r_prec.at[i], dsib)
+
+    def c_sib():
+        return remote(part, sibr, s_sib, r_sib, dsib)
+
+    def c_pl(i):
+        return remote(sums.at[i], plr.at[i], s_pl.at[i], r_pl.at[i], dpl[i])
+
+    def column(buf, s, r, sc, rc):
+        def along(k):
+            return remote(buf.at[c, z], buf.at[c, z], s.at[k - 1], r.at[k - 1], dz[k])
+
+        def across(k):
+            return remote(buf.at[c, zf[k]], buf.at[c, zf[k]], sc.at[k], rc.at[k], dsib)
+        return along, across
+
+    x_z, x_c = column(xall, s_x, r_x, s_xc, r_xc)
+    y_z, y_c = column(dyall, s_y, r_y, s_yc, r_yc)
+    w_z, w_c = column(wgt, s_w, r_w, s_wc, r_wc)
+
+    def back(src, dst, s, r):
+        return lambda k: remote(src.at[zk[k]], dst.at[k - 1], s.at[k - 1], r.at[k - 1], dz[k])
+
+    g_z, o_z, gg_z = back(gsum, grecv, s_g, r_g), back(osum, orecv, s_o, r_o), back(ggsum, ggrecv, s_gg, r_gg)
+    g_c = remote(gpart, gsib, s_gc, r_gc, dsib)
+    o_c = remote(opart, osib, s_oc, r_oc, dsib)
+    gg_c = remote(ggp.at[1 - c], ggsib, s_ggc, r_ggc, dsib)
+
+    def weights_a(k):
+        if k:
+            c_wz(k).wait_recv()
+        c_wp(k, 0).start()
+
+    def weights_b(k):
+        c_wp(k, 0).wait_recv()
+        c_wp(k, 1).start()
+        c_wp(k, 2).start()
+
+    for k in (1, 2, 3):
+        c_small(k).start()
+    local = [pltpu.make_async_copy(small, smalls.at[z], sl.at[0]),
+             pltpu.make_async_copy(qkv_cols, qkvw.at[pl.ds(pl.multiple_of(z * 384, 384), 384)], sl.at[1]),
+             pltpu.make_async_copy(wpiece.at[z], wbuf.at[:, rows(z, p0)], sl.at[2]),
+             pltpu.make_async_copy(dy, dyall.at[c, z], sl.at[3])]
+    for one in local:
+        one.start()
+    for k in (1, 2, 3):
+        c_qkv(k).start()
+    my_proj = proj.at[pl.ds(pl.multiple_of(c * 192, 192), 192)]
+    own_proj = pltpu.make_async_copy(my_proj, projw, sl.at[4])
+
+    @pl.when(z == p0)
+    def _():
+        own_proj.start()
+
+        @pl.when(z < 3)
+        def _():
+            c_proj(my_proj, 0).start()
+
+        @pl.when(z > 0)
+        def _():
+            c_proj(my_proj, 1).start()
+    weights_a(0)
+    for k in (1, 2, 3):
+        c_wz(k).start()
+
+    tok_f = tok[...].astype(F32)
+    inv1 = lax.rsqrt(jnp.mean(tok_f * tok_f, axis=1, keepdims=True) + EPS)
+    for k in (1, 2, 3):
+        c_small(k).wait_recv()
+    local[0].wait()
+    gain1 = jnp.concatenate([smalls[i, 0:1, :] for i in range(4)], axis=1).astype(F32)
+    actp[c, p0] = (tok_f * inv1 * gain1).astype(BF)
+    pre[c, p0] = prefix[...]
+    for i in range(3):
+        c_act(i).start()
+        c_pre(i).start()
+    c_actc(0).start()
+    c_prec(0).start()
+
+    @pl.when(z == p0)
+    def _():
+        own_proj.wait()
+
+    @pl.when(z != p0)
+    def _():
+        c_proj(projw, 0).wait_recv()
+
+    @pl.when((z > p0) & (z < 3))
+    def _():
+        c_proj(projw, 0).start()
+
+    @pl.when((z < p0) & (z > 0))
+    def _():
+        c_proj(projw, 1).start()
+
+    weights_b(0)
+    for i in range(3):
+        c_act(i).wait_recv()
+        c_pre(i).wait_recv()
+        c_actc(i + 1).start()
+        c_prec(i + 1).start()
+    for k in (1, 2, 3):
+        c_qkv(k).wait_recv()
+    local[1].wait()
+    local[3].wait()
+    for k in (1, 2, 3):
+        y_z(k).start()
+    y_c(0).start()
+
+    row = lax.broadcasted_iota(jnp.int32, (128, 128), 0)
+    col = lax.broadcasted_iota(jnp.int32, (128, 128), 1)
+    causal = col <= row
+    col_f = col.astype(F32)
+
+    def attention(cc):
+        pr[...] = jnp.dot(actp[cc].reshape(512, 1536), qkvw[...], preferred_element_type=F32).reshape(4, 128, 320)
+
+        def one(i, _):
+            lo = turn(pr[i, :, 0:128], cos_t[...], sin_t[...]).astype(BF)
+            hi = turn(pr[i, :, 128:256], cos_t[...], sin_t[...]).astype(BF)
+            qs[cc, i, 0:128] = lo[:, 0:64]
+            qs[cc, i, 128:256] = lo[:, 64:128]
+            qs[cc, i, 256:384] = hi[:, 0:64]
+            ks[cc, i] = hi[:, 64:128]
+            vs[cc, i] = pr[i, :, 256:320].astype(BF)
+            sc = lax.dot_general(qs[cc, i], ks[cc, i], (((1,), (1,)), ((), ())), preferred_element_type=F32)
+            allowed = causal | (col_f < pre[cc, i, 0:1, :])
+            sc = jnp.where(allowed[None], sc.reshape(3, 128, 128) * (64 ** -0.5), -1e30)
+            ex = jnp.exp(sc - jnp.max(sc, axis=-1, keepdims=True))
+            pb = (ex / jnp.sum(ex, axis=-1, keepdims=True)).reshape(384, 128)
+            probs[cc, i] = pb
+            at = jnp.dot(pb.astype(BF), vs[cc, i], preferred_element_type=F32).astype(BF)
+            for h in range(3):
+                att[cc, i, :, h * 64 : (h + 1) * 64] = at[h * 128 : (h + 1) * 128]
+            return 0
+        lax.fori_loop(0, 4, one, 0)
+
+    attention(c)
+    weights_a(1)
+    for i in range(4):
+        c_actc(i).wait_recv()
+        c_prec(i).wait_recv()
+    attention(1 - c)
+
+    def to_sib(i, _):
+        part[i] = jnp.dot(att[1 - c, i], projw[...], preferred_element_type=F32).astype(BF)
+        return 0
+    lax.fori_loop(0, 4, to_sib, 0)
+    c_sib().start()
+    weights_b(1)
+    c_sib().wait_recv()
+    for i in range(3):
+        sums[i] = (jnp.dot(att[c, peers[i]], projw[...], preferred_element_type=F32)
+                   + sibr[peers[i]].astype(F32)).astype(BF)
+        c_pl(i).start()
+    residual = (tok_f + jnp.dot(att[c, p0], projw[...], preferred_element_type=F32) + sibr[p0].astype(F32))
+    weights_a(2)
+    for i in range(3):
+        c_pl(i).wait_recv()
+        residual = residual + plr[i].astype(F32)
+    res[...] = residual
+    inv2 = lax.rsqrt(jnp.mean(residual * residual, axis=1, keepdims=True) + EPS)
+    gain2 = jnp.concatenate([smalls[i, 1:2, :] for i in range(4)], axis=1).astype(F32)
+    act2 = (residual * inv2 * gain2).astype(BF)
+    xall[c, z] = act2
+    for k in (1, 2, 3):
+        x_z(k).start()
+    x_c(0).start()
+    router = jnp.concatenate([smalls[i, 16:32, :] for i in range(4)], axis=1)
+    logits = lax.dot_general(act2, router, (((1,), (1,)), ((), ())), preferred_element_type=F32)
+    chosen, kept = masks[0] > 0.0, masks[1]
+    top = jnp.max(jnp.where(chosen, logits, -1e30), axis=1, keepdims=True)
+    ge = jnp.where(chosen, jnp.exp(jnp.where(chosen, logits - top, 0.0)), 0.0)
+    gt = ge / jnp.sum(ge, axis=1, keepdims=True)
+    gates[...] = gt
+    wgt[c, z] = jnp.concatenate([gt * kept, jnp.zeros((128, 112), F32)], axis=1)
+    for k in (1, 2, 3):
+        w_z(k).start()
+    w_c(0).start()
+    weights_b(2)
+    weights_a(3)
+    for k in (1, 2, 3):
+        y_z(k).wait_recv()
+        y_c(k).start()
+    weights_b(3)
+    for k in (1, 2, 3):
+        x_z(k).wait_recv()
+        x_c(k).start()
+        w_z(k).wait_recv()
+        w_c(k).start()
+    local[2].wait()
+    for k in range(4):
+        c_wp(k, 1).wait_recv()
+        c_wp(k, 2).wait_recv()
+    for k in range(4):
+        x_c(k).wait_recv()
+        y_c(k).wait_recv()
+        w_c(k).wait_recv()
+
+    lane = lax.broadcasted_iota(jnp.int32, (512, 128), 1)
+    ggp[...] = jnp.zeros_like(ggp)
+
+    def expert(n, _):
+        j, t = n // 2, lax.rem(n, 2)
+        gu = jnp.dot(xall[t].reshape(512, 1536), wbuf[j, :, : 2 * half], preferred_element_type=F32)
+        bk = jnp.dot(dyall[t].reshape(512, 1536), wbuf[j, :, 2 * half :], preferred_element_type=F32)
+        mine = lane == z * 4 + j
+        w = jnp.sum(jnp.where(mine, wgt[t].reshape(512, 128), 0.0), axis=1, keepdims=True)
+        g, u = gu[:, :half], gu[:, half:]
+        sg = 1.0 / (1.0 + jnp.exp(-g))
+        silu = g * sg
+        hid = silu * u
+        hw[j, pl.ds(pl.multiple_of(t * 512, 512), 512)] = (hid * w).astype(BF)
+        ggp[t] = ggp[t] + jnp.where(mine, jnp.sum(bk * hid, axis=1, keepdims=True), 0.0).reshape(4, 128, 128)
+        gh = bk * w
+        at = pl.ds(pl.multiple_of(t * 512, 512), 512)
+        ggu[j, at, :half] = (gh * u * sg * (1.0 + g * (1.0 - sg))).astype(BF)
+        ggu[j, at, half:] = (gh * silu).astype(BF)
+        return 0
+    lax.fori_loop(0, 8, expert, 0)
+    saves = []
+
+    def save(src, dst):
+        one = pltpu.make_async_copy(src, dst, sl.at[5 + len(saves)])
+        one.start()
+        saves.append(one)
+    for src, dst in ((xall, o_x), (dyall, o_dy), (ggu, o_ggu), (hw, o_hw), (actp, o_act), (qs, o_q), (ks, o_k),
+                     (vs, o_v), (probs, o_probs), (att, o_att), (qkvw, o_qkvw), (projw, o_projw),
+                     (smalls, o_small), (res, o_res), (gates, o_gates)):
+        save(src, dst)
+
+    def block(grad, t, n):
+        at = pl.ds(pl.multiple_of(t * 512, 512), 512)
+        lanes = pl.ds(pl.multiple_of(n * 256, 256), 256)
+        acc = jnp.zeros((512, 256), F32)
+        for j in range(4):
+            a = ggu[j, at] if grad else hw[j, at]
+            b = wbuf[j, lanes, : 2 * half] if grad else wbuf[j, lanes, 2 * half :]
+            acc = acc + lax.dot_general(a, b, (((1,), (1,)), ((), ())), preferred_element_type=F32)
+        return acc.reshape(4, 128, 256), lanes
+
+    def partial(grad, buf):
+        def one(n, _):
+            v, lanes = block(grad, 1 - c, n)
+            buf[:, :, lanes] = v.astype(BF)
+            return 0
+        lax.fori_loop(0, 6, one, 0)
+
+    def own(grad, sib, dst):
+        def one(n, _):
+            v, lanes = block(grad, c, n)
+            dst[:, :, lanes] = (v + sib[:, :, lanes].astype(F32)).astype(BF)
+            return 0
+        lax.fori_loop(0, 6, one, 0)
+
+    gg_c.start()
+    partial(True, gpart)
+    g_c.start()
+    gg_c.wait_recv()
+    for k in range(4):
+        ggsum[zk[k]] = ggp[c, zk[k]] + ggsib[zk[k]]
+    for k in (1, 2, 3):
+        gg_z(k).start()
+    partial(False, opart)
+    o_c.start()
+    g_c.wait_recv()
+    own(True, gsib, gsum)
+    for k in (1, 2, 3):
+        g_z(k).start()
+    o_c.wait_recv()
+    own(False, osib, osum)
+    for k in (1, 2, 3):
+        o_z(k).start()
+    for k in (1, 2, 3):
+        gg_z(k).wait_recv()
+        g_z(k).wait_recv()
+    ggt[...] = (ggsum[z] + ggrecv[0] + ggrecv[1] + ggrecv[2])[:, :EXPERTS]
+    save(ggt, o_gg)
+    gact[...] = (gsum[z].astype(F32) + grecv[0].astype(F32) + grecv[1].astype(F32) + grecv[2].astype(F32))
+    save(gact, o_gact)
+    for k in (1, 2, 3):
+        o_z(k).wait_recv()
+    outb[...] = (res[...] + osum[z].astype(F32) + orecv[0].astype(F32) + orecv[1].astype(F32)
+                 + orecv[2].astype(F32)).astype(BF)
+    save(outb, o_out)
+
+    for k in (1, 2, 3):
+        for one in (c_small(k), c_qkv(k), c_wz(k), x_z(k), y_z(k), w_z(k), g_z(k), o_z(k), gg_z(k)):
+            one.wait_send()
+    for k in range(4):
+        for i in range(3):
+            c_wp(k, i).wait_send()
+        for one in (c_actc(k), c_prec(k), x_c(k), y_c(k), w_c(k)):
+            one.wait_send()
+    for i in range(3):
+        for one in (c_act(i), c_pre(i), c_pl(i)):
+            one.wait_send()
+    for one in (c_sib(), g_c, o_c, gg_c):
+        one.wait_send()
+
+    @pl.when(up_ok)
+    def _():
+        c_proj(projw, 0).wait_send()
+
+    @pl.when(down_ok)
+    def _():
+        c_proj(projw, 1).wait_send()
+    for one in saves:
+        one.wait()
+
+
+def front(tok, dy, wpiece, qkv_cols, proj, small, masks, prefix, cos_t, sin_t):
+    sem, vm = pltpu.SemaphoreType.DMA, pltpu.VMEM
+    out = lambda shape, kind=BF: jax.ShapeDtypeStruct(shape, kind)
+    outs = (
+        out((2, 4, 128, 1536)), out((2, 4, 128, 1536)), out((4, 1024, 512)), out((4, 1024, 256)),
+        out((2, 4, 128, 1536)), out((2, 4, 384, 64)), out((2, 4, 128, 64)), out((2, 4, 128, 64)),
+        out((2, 4, 384, 128), F32), out((2, 4, 128, 192)), out((1536, 320)), out((192, 1536)),
+        out((4, 32, 384)), out((128, 1536), F32), out((128, 16), F32), out((128, 1536), F32),
+        out((128, 16), F32), out((128, 1536)),
+    )
+    block, quad = vm((2, 4, 128, 1536), BF), vm((4, 128, 1536), BF)
+    three = vm((3, 128, 1536), BF)
+    scratch = [
+        vm((4, 32, 384), BF), vm((1536, 320), BF), vm((192, 1536), BF), block, vm((2, 4, 8, 128), F32),
+        vm((4, 128, 320), F32), vm((2, 4, 384, 64), BF), vm((2, 4, 128, 64), BF), vm((2, 4, 128, 64), BF),
+        vm((2, 4, 384, 128), F32), vm((2, 4, 128, 192), BF), quad, quad, three, three,
+        block, block, vm((2, 4, 128, 128), F32), vm((4, 1536, 768), BF), vm((4, 1024, 512), BF),
+        vm((4, 1024, 256), BF), quad, quad, vm((2, 4, 128, 128), F32), quad, quad, vm((4, 128, 128), F32),
+        quad, quad, vm((4, 128, 128), F32), three, three, vm((3, 128, 128), F32),
+        vm((128, 1536), F32), vm((128, 16), F32), vm((128, 1536), F32), vm((128, 16), F32), vm((128, 1536), BF),
+    ]
+    n3, n4 = sem((3,)), sem((4,))
+    one = sem(())
+    sems = [
+        n3, n3, n3, n3, sem((2,)), one, n3, n3, sem((4, 3)), sem((4, 3)),
+        n3, n3, n3, n3, n4, n4, n4, n4, one, one, n3, n3,
+        n3, n3, n4, n4, n3, n3, n4, n4, n3, n3, n4, n4,
+        n3, n3, n3, n3, n3, n3, one, one, one, one, one, one, sem((24,)),
+    ]
+    vmem, any_ = pl.BlockSpec(memory_space=pltpu.VMEM), pl.BlockSpec(memory_space=pl.ANY)
+    return pl.pallas_call(
+        front_kernel,
+        out_shape=outs,
+        in_specs=[vmem, any_, any_, any_, any_, any_, vmem, vmem, vmem, vmem],
+        out_specs=[any_] * len(outs),
+        scratch_shapes=scratch + sems,
+        compiler_params=pltpu.CompilerParams(
+            collective_id=1, has_side_effects=True, vmem_limit_bytes=62 * 1024 * 1024),
+        name="front",
+    )(tok, dy, wpiece, qkv_cols, proj, small, masks, prefix, cos_t, sin_t)
+
+
 def expert_grads_general(reps, grps, xs, dys, ggu, hw):
     local, half, width = ggu.shape[0], HID // 2, xs.shape[1]
     own = width // grps
@@ -282,7 +714,7 @@
     return gw[:, : 2 * HID], gw[:, 2 * HID :]
 
 
-def shards(
+def shards_general(
     reps,
     grps,
     tokens,
@@ -411,10 +843,7 @@
     grad_gates = jnp.where(kept, grad_gates, 0.0)
     out = to_owners(out_part)
     output = (residual + out).astype(BF)
-    if (reps, grps) == (8, 4):
-        grad_gu, grad_dn = expert_grads(x_all, dy_all, ggu, hidden_w)
-    else:
-        grad_gu, grad_dn = expert_grads_general(reps, grps, x_all, dy_all, ggu, hidden_w)
+    grad_gu, grad_dn = expert_grads_general(reps, grps, x_all, dy_all, ggu, hidden_w)
     grad_gu = grad_gu.reshape(own, EXPERTS, 2 * HID)
     grad_dn = grad_dn.reshape(own, EXPERTS, HID)
 
@@ -472,6 +901,145 @@
     )
     proj_all = lax.all_gather(proj_sum, "rep", axis=0, tiled=True, axis_index_groups=groups)
     grad_proj = lax.dynamic_slice_in_dim(proj_all, grp * own, own, 0).astype(F32)
+    terms = jnp.concatenate([gain_one_term[:, None], gain_two_term[:, None], router_term], axis=1)
+    terms = lax.psum(lax.psum_scatter(terms, "grp", scatter_dimension=0, tiled=True), "rep")
+    return (
+        output,
+        grad_tokens,
+        terms[:, 0],
+        grad_qkv,
+        grad_proj,
+        terms[:, 1],
+        terms[:, 2:],
+        grad_gu,
+        grad_dn,
+    )
+
+
+def shards(
+    tokens,
+    attn_gain,
+    query_key_value_weight,
+    attn_proj,
+    mlp_gain,
+    w_router,
+    w_gate_up,
+    w_down,
+    prefix_len,
+    expert_ids,
+    priority,
+    cotangent,
+):
+    heads, half, own = KEY_VALUE_HEADS, HID // 2, attn_gain.shape[0]
+    qw, hw, q_all = QPK * HEAD_WIDTH, HEAD_WIDTH, QUERY_HEADS * HEAD_WIDTH
+    rep = lax.axis_index("rep")
+    core, chip = lax.rem(rep, 2), rep // 2
+    seq, width = tokens.shape
+    small = jnp.concatenate(
+        [attn_gain[None], mlp_gain[None], jnp.zeros((14, own), BF), w_router.T], axis=0
+    )
+    qkv_cols = jnp.concatenate(
+        [
+            lax.dynamic_slice_in_dim(query_key_value_weight, rep * qw, qw, 1),
+            lax.dynamic_slice_in_dim(query_key_value_weight, q_all + rep * hw, hw, 1),
+            lax.dynamic_slice_in_dim(query_key_value_weight, q_all + heads * hw + rep * hw, hw, 1),
+        ],
+        axis=1,
+    )
+    piece = own // 4
+    gu_piece = lax.dynamic_slice_in_dim(w_gate_up, chip * piece, piece, 0)
+    dn_piece = lax.dynamic_slice_in_dim(w_down, chip * piece, piece, 0)
+    both = jnp.concatenate(
+        [
+            lax.dynamic_slice_in_dim(gu_piece, core * half, half, 2),
+            lax.dynamic_slice_in_dim(gu_piece, HID + core * half, half, 2),
+            lax.dynamic_slice_in_dim(dn_piece, core * half, half, 2),
+        ],
+        axis=2,
+    )
+    wpiece = both.transpose(1, 0, 2).reshape(4, 4, piece, 3 * half)
+    chosen, kept = choices(expert_ids, priority)
+    masks = jnp.stack([chosen, kept]).astype(F32)
+    prefix = jnp.broadcast_to(prefix_len.astype(F32), (8, 128))
+    cos, sin = rope_tables(seq)
+    cos_t, sin_t = jnp.tile(cos, (1, 4)), jnp.tile(jnp.concatenate([-sin, sin], axis=1), (1, 2))
+    (x_all, dy_all, ggu, hidden_w, act_plane, query, key, value, probs, attended, qkv_head, proj_head,
+     smalls, residual, gates, gact, grad_gates, output) = front(
+        tokens, cotangent, wpiece, qkv_cols, attn_proj, small, masks, prefix, cos_t, sin_t)
+    grad_gu, grad_dn = expert_grads(x_all.reshape(1024, width), dy_all.reshape(1024, width), ggu, hidden_w)
+    grad_gu = grad_gu.reshape(own, EXPERTS, 2 * HID)
+    grad_dn = grad_dn.reshape(own, EXPERTS, HID)
+
+    gain_one = smalls[:, 0].reshape(1, width).astype(F32)
+    gain_two = smalls[:, 1].reshape(1, width).astype(F32)
+    router_t = jnp.concatenate([smalls[i, 16:] for i in range(4)], axis=1)
+    tokens_f = tokens.astype(F32)
+    inverse_one = lax.rsqrt(jnp.mean(tokens_f * tokens_f, axis=1, keepdims=True) + EPS)
+    normed_one = tokens_f * inverse_one
+    inverse_two = lax.rsqrt(jnp.mean(residual * residual, axis=1, keepdims=True) + EPS)
+    normed_two = residual * inverse_two
+    act_two = (normed_two * gain_two).astype(BF)
+
+    grad_gates = grad_gates * masks[1]
+    grad_logits = (gates * (grad_gates - jnp.sum(gates * grad_gates, axis=1, keepdims=True))).astype(BF)
+    gact = gact + dot(grad_logits, router_t)
+    router_term = dot(act_two.T, grad_logits)
+    gain_two_term = jnp.sum(gact * normed_two, axis=0)
+    scaled = gact * gain_two
+    dy = cotangent.astype(F32)
+    grad_residual = dy + inverse_two * (
+        scaled - normed_two * jnp.mean(scaled * normed_two, axis=1, keepdims=True)
+    )
+    gres_low = grad_residual.astype(BF)
+
+    def by_core(v):
+        return v.reshape(4, 2, *v.shape[1:]).swapaxes(0, 1)
+
+    gres_plane = by_core(lax.all_gather(gres_low, "rep", axis=0)).reshape(1024, width)
+    query = query.reshape(heads, QPK, seq, hw)
+    key, value = key.reshape(heads, seq, hw), value.reshape(heads, seq, hw)
+    probs = probs.reshape(heads, QPK, seq, seq)
+    attended = attended.reshape(heads * seq, qw)
+    proj_term = dot(attended.T, gres_plane)
+    grad_att = dot(gres_plane, proj_head.T).astype(BF).reshape(heads, seq, QPK, hw)
+    grad_value = jnp.einsum("bgst,bsgd->btd", probs.astype(BF), grad_att, preferred_element_type=F32)
+    grad_probs = jnp.einsum("bsgd,btd->bgst", grad_att, value, preferred_element_type=F32)
+    grad_scores = (
+        probs * (grad_probs - jnp.sum(probs * grad_probs, axis=-1, keepdims=True))
+    ).astype(BF)
+    scale = HEAD_WIDTH ** (-0.5)
+    grad_query = jnp.einsum("bgst,btd->bsgd", grad_scores, key, preferred_element_type=F32) * scale
+    grad_key = jnp.einsum("bgst,bgsd->btd", grad_scores, query, preferred_element_type=F32) * scale
+    turned_back = rotate(
+        jnp.concatenate([grad_query, grad_key[:, :, None]], axis=2),
+        cos[None, :, None, :],
+        -sin[None, :, None, :],
+    )
+    gproj = jnp.concatenate([turned_back, grad_value[:, :, None]], axis=2).astype(BF)
+    gproj = gproj.reshape(heads * seq, qw + 2 * hw)
+    qkv_term = dot(act_plane.reshape(1024, width).T, gproj)
+    gact_one = dot(gproj, qkv_head.T).astype(BF).reshape(2, 4, seq, width).swapaxes(0, 1)
+    gact_one = lax.psum_scatter(
+        gact_one.reshape(1024, width), "rep", scatter_dimension=0, tiled=True
+    ).astype(F32)
+    gain_one_term = jnp.sum(gact_one * normed_one, axis=0)
+    scaled_one = gact_one * gain_one
+    grad_tokens = grad_residual + inverse_one * (
+        scaled_one - normed_one * jnp.mean(scaled_one * normed_one, axis=1, keepdims=True)
+    )
+
+    qkv_own = lax.psum_scatter(qkv_term.astype(BF), "grp", scatter_dimension=0, tiled=True)
+    proj_sum = lax.psum(proj_term.astype(BF), "grp")
+    qkv_own = lax.all_gather(qkv_own, "rep", axis=0, tiled=False).astype(F32)
+    grad_qkv = jnp.concatenate(
+        [
+            qkv_own[:, :, lo:hi].transpose(1, 0, 2).reshape(own, -1)
+            for lo, hi in ((0, qw), (qw, qw + hw), (qw + hw, qw + 2 * hw))
+        ],
+        axis=1,
+    )
+    proj_all = lax.all_gather(proj_sum, "rep", axis=0, tiled=True)
+    grad_proj = lax.dynamic_slice_in_dim(proj_all, lax.axis_index("grp") * own, own, 0).astype(F32)
     terms = jnp.concatenate([gain_one_term[:, None], gain_two_term[:, None], router_term], axis=1)
     terms = lax.psum(lax.psum_scatter(terms, "grp", scatter_dimension=0, tiled=True), "rep")
     return (
@@ -517,6 +1085,8 @@
     reps, grps = mesh.shape["rep"], mesh.shape["grp"]
 
     def body(*args):
-        return shards(reps, grps, *args)
+        if (reps, grps) == (8, 4):
+            return shards(*args)
+        return shards_general(reps, grps, *args)
 
     return jax.shard_map(body, mesh=mesh, in_specs=in_specs, out_specs=out_specs, check_vma=False)

time: 930 us -> 794 us (0.85)
  Pallas kernels: 184 us -> 506 us
  waiting for transfers between devices: 442 us -> 146 us
  blocking collectives: 92.9 us -> 24.2 us
  matrix products: 62.4 us -> 13.5 us
  other arithmetic: 38.4 us -> 25.9 us
  local copies, waits for them, and re-layouts: 73.2 us -> 62.5 us
  starting transfers between devices: 10.8 us -> 0.51 us
    pallas_call x0 -> x1, Pallas kernels: none -> 308 us  [front(): pl.pallas_call(front_kernel, out_shape=outs, in_specs=[vmem, any_, any_,...]
    all_gather x9 -> x3, waiting for transfers between devices: 148 us -> 39.1 us  [the longest x1 39.1 us: shards(): lax.all_gather(gres_low, 'rep', axis=0)]
    reduce_scatter x6 -> x1, waiting for transfers between devices: 131 us -> 37.3 us  [shards(): lax.psum_scatter(gact_one.reshape(1024, width), 'rep', scatter_dimension=...]
    all_to_all x2 -> x0, waiting for transfers between devices: 83.9 us -> none  [the longest x1 78.4 us: shards(): both = lax.all_to_all(both, 'grp', 0, 0, tiled=True)]
    all_gather x4 -> x0, blocking collectives: 60.7 us -> none  [the longest x1 30.8 us: shards(): qkv_head = lax.all_gather(qkv_cols, 'grp', axis=0, tiled=True)]
    dot_general x7 -> x2, matrix products: 38.6 us -> 0.78 us  [the longest x1 0.5 us: shards(): jnp.einsum('bgst,bgsd->btd', grad_scores, query, preferred_element_type=F32)]
    pallas_call x1, Pallas kernels: 184 us -> 198 us  [expert_grads(): pl.pallas_call(lambda *a: grads_kernel(nq, *a), out_shape=(jax.ShapeDtype...]
    unnamed x22 -> x8, waiting for transfers between devices: 41.2 us -> 30.2 us
  transfers between devices with their start and end apart: 22 -> 7, of which waited for: 14 -> 4; matrix products, arithmetic and copies ran while one was open for 10% -> 4% of each run, Pallas kernels for 20% -> 25%
where the time goes in v3:
time: 794 us; the launch traced here: 793 us
  Pallas kernels  506 us (64%)
  waiting for transfers between devices  146 us (18%)
  local copies, waits for them, and re-layouts  62.5 us (8%)
  other arithmetic  25.9 us (3%)
  blocking collectives  24.2 us (3%)
  between operations  15.4 us (2%)
  matrix products  13.5 us (2%)
    pallas_call x1, Pallas kernels, front(): pl.pallas_call(front_kernel, out_shape=outs, in_specs=[vmem, any_, any_,...  308 us
    pallas_call x1, Pallas kernels, expert_grads(): pl.pallas_call(lambda *a: grads_kernel(nq, *a), out_shape=(jax.ShapeDtype...  198 us
    unnamed x49, local copies, waits for them, and re-layouts  41.7 us
    all_gather x1, waiting for transfers between devices, shards(): lax.all_gather(gres_low, 'rep', axis=0)  39.1 us
    psum x1, waiting for transfers between devices, shards(): proj_sum = lax.psum(proj_term.astype(BF), 'grp')  39.1 us
    reduce_scatter x1, waiting for transfers between devices, shards(): lax.psum_scatter(gact_one.reshape(1024, width), 'rep', scatter_dimension=...  37.3 us
    unnamed x8, waiting for transfers between devices  30.2 us
    psum x1, blocking collectives, shards(): lax.psum(lax.psum_scatter(terms, 'grp', scatter_dimension=0, tiled=True),...  24.2 us
  transfers between devices with their start and end apart: 7, of which 4 were waited for; matrix products, arithmetic and copies ran while one was open for 4% of the time, Pallas kernels for 25%

profile of v3, /device:TPU:0, one launch (start us, length us, event | category | flops | bytes accessed | tf_op | source)
XLA Modules:
  0.0 793.1 jit_solution(7813572585336232685)
XLA Ops:
  11.4 1.3 reduce.11
  13.7 2.5 convert_reduce_fusion
  17.9 3.2 constant_dynamic-slice_fusion.5
  21.3 2.1 copy.106
  24.6 1.1 constant_dynamic-slice_fusion.1
  27.8 308.0 %front.1 = (bf16[2,4,128,1536]{3,2,1,0:T(8,128)(2,1)}, bf16[2,4,128,1536]{3,2,1,0:T(8,128)(2,1)}, bf16[4,1024,512]{2,1,0:T(8,128)(2,1)}, bf16[4,1024,256]{2,1,0:...) custom-call(bf16[128,1536]{1,0:T(8,128)(2,1)} %tok.1, ...), custom_call_target="tpu_custom_call" | custom-call | tf_op jit(solution)/shard_map/front/pallas_call | solution.py:683
  335.8 1.5 convert_reduce_fusion.1
  340.0 1.3 multiply_reduce_fusion.2
  341.3 1.8 multiply_reduce_fusion
  344.5 1.9 copy.117
  346.4 39.1 %all-gather.8.cloned.1.call-done = bf16[1024,1536]{1,0:T(8,128)(2,1)} async-done(((bf16[128,1536]{1,0:T(8,128)(2,1)}), bf16[1024,1536]{1,0:T(8,128)(2,1)}) %all-gather.8.cloned.1.call-update) | async-done | bytes 3145744 | tf_op jit(solution)/shard_map/all_gather | solution.py:998
  385.4 2.2 copy.113
  387.6 1.2 fusion.12
  392.2 1.9 convolution_convert_fusion
  394.1 1.9 copy.124
  396.0 3.3 convolution_convert_fusion.1
  399.4 1.4 copy.143
  401.3 3.7 fusion.5
  405.1 37.3 %reduce-scatter.6.cloned.1.call-done = bf16[128,1536]{1,0:T(8,128)(2,1)} async-done(((bf16[1024,1536]{1,0:T(8,128)(2,1)}), bf16[128,1536]{1,0:T(8,128)(2,1)}) %reduce-scatter.6.cloned.1.call-update) | async-done | bytes 393232 | tf_op jit(solution)/shard_map/reduce_scatter | solution.py:1022
  442.4 1.3 fusion.22
  444.5 30.1 %reduce-scatter.10.cloned.1.call-done = bf16[384,320]{1,0:T(8,128)(2,1)} async-done(((bf16[1536,320]{1,0:T(8,128)(2,1)}), bf16[384,320]{1,0:T(8,128)(2,1)}) %reduce-scatter.10.cloned.1.call-update) | async-done | bytes 245776
  474.6 1.8 copy.144
  476.5 39.1 %all-reduce.2.cloned.1.call-done = bf16[192,1536]{1,0:T(8,128)(2,1)} async-done(((bf16[192,1536]{1,0:T(8,128)(2,1)}), bf16[192,1536]{1,0:T(8,128)(2,1)}) %all-reduce.2.cloned.1.call-update) | async-done | bytes 589840 | tf_op jit(solution)/shard_map/psum | solution.py:1032
  515.6 197.6 %expert_grads.1 = (f32[6144,1024]{1,0:T(8,128)}, f32[6144,512]{1,0:T(8,128)}) custom-call(bf16[1024,1536]{1,0:T(8,128)(2,1)} %bitcast.145, bf16[1024,1536]{1,0:T(8,128)(2,1)} %bitcast.146, bf16[4,1024,512]{2,1,0:T(8,128)(2,1)} %get-tuple-element.45.a_2_, bf16[4,1024,256]{2,1,0:T(8,128)(2,1)} %get-tuple-element.46.a_3_), custom_call_target="tpu_custom_call" | custom-call | tf_op jit(solution)/shard_map/expert_grads/pallas_call | solution.py:242
  713.2 2.4 fusion.19
  715.6 24.2 %psum.14 = f32[384,18]{0,1:T(8,128)S(1)} all-reduce(f32[384,18]{0,1:T(8,128)} %reduce-scatter.8.cloned.1.call-done), channel_id=1, replica_groups=mesh['rep'=8,'grp'=4] {'rep'}, use_global_device_ids=true, to_apply=%region_13.14 | all-reduce | flops 6912 | bytes 55296 | tf_op jit(solution)/shard_map/psum | solution.py:1044
  741.0 2.0 convert_element_type.115
  744.8 2.2 pad_maximum_fusion
  747.0 5.4 copy.129
  752.5 3.0 dynamic-slice_convert_fusion
  756.2 17.7 %copy.172 = f32[384,16,1024]{2,1,0:T(8,128)} copy(f32[384,16,1024]{2,1,0:T(8,128)} %bitcast.129) | data formatting | bytes 50331648
  773.9 12.3 %copy.173 = f32[384,16,512]{2,1,0:T(8,128)} copy(f32[384,16,512]{2,1,0:T(8,128)} %bitcast.133) | data formatting | bytes 25165824
  (118 shorter events, 22.1 us)
Async XLA Ops:
  7.2 378.3 %all-gather.8.cloned.1.call-start = ((), (), s32[]{:S(2)}) async-start(), calls=%async_computation.7 | async-start | bytes 3538944 | tf_op jit(solution)/shard_map/all_gather | solution.py:998
  21.3 5.3 copy-start.13
  24.6 313.5 %copy-start.4 = (f32[2,128,16]{2,1,0:T(8,128)S(1)}, f32[2,128,16]{2,1,0:T(8,128)}, u32[]{:S(2)}) copy-start(f32[2,128,16]{2,1,0:T(8,128)} %convert_element_type.90.masks) | copy-start | bytes 49156
  335.8 7.3 copy-start
  335.8 7.3 copy-start.3
  340.0 4.4 copy-start.8
  341.3 5.0 copy-start.14
  343.1 44.5 %copy-start.16 = (f32[128]{0:T(128)}, f32[128]{0:T(128)S(1)}, u32[]{:S(2)}) copy-start(f32[128]{0:T(128)S(1)} %broadcast_multiply_fusion.1) | copy-start | bytes 1540
  344.2 98.2 %reduce-scatter.6.cloned.1.call-start = ((), (), s32[]{:S(2)}) async-start(), calls=%async_computation.3 | async-start | bytes 3538944 | tf_op jit(solution)/shard_map/reduce_scatter | solution.py:1022
  385.4 2.2 copy-start.19
  387.6 1.4 copy-start.1
  387.6 1.7 copy-start.11
  389.3 1.1 copy-start.5
  389.7 1.3 copy-start.10
  391.0 1.3 copy-start.18
  392.0 2.1 copy-start.6
  396.0 78.6 %reduce-scatter.10.cloned.1.call-start = ((), (), s32[]{:S(2)}) async-start(), calls=%async_computation.9 | async-start | bytes 1474560
  399.3 1.5 copy-start.12
  399.3 1.5 copy-start.2
  399.3 1.7 copy-start.9
  399.4 1.7 copy-start.15
  400.8 114.7 %all-reduce.2.cloned.1.call-start = ((), (), s32[]{:S(2)}) async-start(), calls=%async_computation.5 | async-start | bytes 1179648 | tf_op jit(solution)/shard_map/psum | solution.py:1032
  405.1 310.5 %reduce-scatter.8.cloned.1.call-start = ((), (), s32[]{:S(2)}) async-start(), calls=%async_computation.4 | async-start | bytes 184320 | tf_op jit(solution)/shard_map/reduce_scatter | solution.py:1044
  444.5 296.5 %all-gather.10.cloned.1.call-start = ((), (), s32[]{:S(2)}) async-start(), calls=%async_computation.8 | async-start | bytes 2211840 | tf_op jit(solution)/shard_map/all_gather | solution.py:1033
  476.4 276.0 %all-gather.6.cloned.1.call-start = ((), (), s32[]{:S(2)}) async-start(), calls=%async_computation.6 | async-start | bytes 5308416 | tf_op jit(solution)/shard_map/all_gather | solution.py:1041
  515.6 197.6 %copy-start.17 = (f32[128]{0:T(128)S(1)}, f32[128]{0:T(128)}, u32[]{:S(2)}) copy-start(f32[128]{0:T(128)} %copy-done.16) | copy-start | bytes 1540
  752.5 3.0 copy-start.7
Sparse Core Ops, SparseCore 0:
  344.3 41.0 all-gather.7
  396.1 46.2 reduce-scatter.5
  445.4 29.1 reduce-scatter.9
  477.5 37.9 all-reduce.1
  518.3 18.9 reduce-scatter.7
  539.6 33.6 all-gather.9
  575.2 56.4 all-gather.5

commit v4 on v3

--- a/solution.py
+++ b/solution.py
@@ -273,13 +273,13 @@
 def front_kernel(tok, dy, wpiece, qkv_cols, proj, small, masks, prefix, cos_t, sin_t,
                  o_x, o_dy, o_ggu, o_hw, o_act, o_q, o_k, o_v, o_probs, o_att, o_qkvw, o_projw,
                  o_small, o_res, o_gates, o_gact, o_gg, o_out,
-                 smalls, qkvw, projw, actp, pre, pr, qs, ks, vs, probs, att, part, sibr, sums, plr,
-                 xall, dyall, wgt, wbuf, ggu, hw, gpart, opart, ggp, gsib, osib, ggsib,
-                 gsum, osum, ggsum, grecv, orecv, ggrecv, res, gates, gact, ggt, outb,
-                 s_small, r_small, s_qkv, r_qkv, s_proj, r_proj, s_wz, r_wz, s_wp, r_wp,
+                 smalls, qkvw, projw, projq, actp, pre, pr, qs, ks, vs, probs, att, part, sibr, sums, plr,
+                 xall, dyall, wbuf, ggu, hw, gpart, opart, ggp, gsib, osib,
+                 gsum, osum, grecv, orecv, res, gates, gact, ggt, outb,
+                 s_small, r_small, s_qkv, r_qkv, s_pz, r_pz, s_pq, r_pq, s_wz, r_wz, s_wp, r_wp,
                  s_act, r_act, s_pre, r_pre, s_actc, r_actc, s_prec, r_prec, s_sib, r_sib, s_pl, r_pl,
-                 s_x, r_x, s_xc, r_xc, s_y, r_y, s_yc, r_yc, s_w, r_w, s_wc, r_wc,
-                 s_g, r_g, s_o, r_o, s_gg, r_gg, s_gc, r_gc, s_oc, r_oc, s_ggc, r_ggc, sl):
+                 s_x, r_x, s_xc, r_xc, s_y, r_y, s_yc, r_yc,
+                 s_g, r_g, s_o, r_o, s_gc, r_gc, s_oc, r_oc, sl):
     y, x, c, z = place()
     half = HID // 2
 
@@ -305,10 +305,6 @@
     def c_small(k):
         return remote(small, smalls.at[z], s_small.at[k - 1], r_small.at[k - 1], dz[k])
 
-    def c_qkv(k):
-        return remote(qkv_cols, qkvw.at[pl.ds(pl.multiple_of(z * 384, 384), 384)],
-                      s_qkv.at[k - 1], r_qkv.at[k - 1], dz[k])
-
     def rows(zz, pp):
         return pl.ds(pl.multiple_of(zz * 384 + pp * 96, 96), 96)
 
@@ -321,10 +317,18 @@
         src = wpiece.at[z] if (k == 0 and i < 2) else wbuf.at[:, rows(zz, pp)]
         return remote(src, wbuf.at[:, rows(zz, pp)], s_wp.at[k, i], r_wp.at[k, i], who)
 
-    up_ok, down_ok = (z >= p0) & (z < 3), (z <= p0) & (z > 0)
-
-    def c_proj(src, d):
-        return remote(src, projw, s_proj.at[d], r_proj, (p0 * 2 + c, z + 1 if d == 0 else z - 1))
+    def quarter(p):
+        return pl.ds(pl.multiple_of(p * 48, 48), 48)
+
+    def c_pz(k):
+        src = proj.at[pl.ds(pl.multiple_of(c * 192 + p0 * 48, 48), 48)]
+        return remote(src, projq.at[k - 1], s_pz.at[k - 1], r_pz.at[k - 1], dz[k])
+
+    def c_pq(k, owner):
+        return remote(projq.at[k - 1], projw.at[quarter(p0)], s_pq.at[k - 1], r_pq.at[p0], (owner * 2 + c, z))
+
+    def c_pq_in(i):
+        return remote(projq.at[0], projw.at[quarter(peers[i])], s_pq.at[0], r_pq.at[peers[i]], dpl[i])
 
     def c_act(i):
         return remote(actp.at[c, p0], actp.at[c, p0], s_act.at[i], r_act.at[i], dpl[i])
@@ -346,25 +350,75 @@
     def c_pl(i):
         return remote(sums.at[i], plr.at[i], s_pl.at[i], r_pl.at[i], dpl[i])
 
-    def column(buf, s, r, sc, rc):
-        def along(k):
-            return remote(buf.at[c, z], buf.at[c, z], s.at[k - 1], r.at[k - 1], dz[k])
-
-        def across(k):
-            return remote(buf.at[c, zf[k]], buf.at[c, zf[k]], sc.at[k], rc.at[k], dsib)
-        return along, across
-
-    x_z, x_c = column(xall, s_x, r_x, s_xc, r_xc)
-    y_z, y_c = column(dyall, s_y, r_y, s_yc, r_yc)
-    w_z, w_c = column(wgt, s_w, r_w, s_wc, r_wc)
+    def chain(at, s, r, sc=None, rc=None):
+        def hop(h, d, send):
+            block = z - (h - 1) if d == 0 else z + (h - 1)
+            if not send:
+                block = z - h if d == 0 else z + h
+            return remote(at(block), at(block), s.at[d, h - 1], r.at[d, h - 1],
+                          (p0 * 2 + c, z + 1 if d == 0 else z - 1))
+
+        def may(h, d, send):
+            if send:
+                return (z < 3) & (z >= h - 1) if d == 0 else (z > 0) & (z <= 4 - h)
+            return z >= h if d == 0 else z <= 3 - h
+
+        def across(h, d):
+            block = z - h if d == 0 else z + h
+            return remote(at(block), at(block), sc.at[d, h - 1], rc.at[d, h - 1], dsib)
+
+        def over():
+            return remote(at(z), at(z), sc.at[2, 0], rc.at[2, 0], dsib)
+
+        def send(h):
+            for d in range(2):
+                @pl.when(may(h, d, True))
+                def _(d=d):
+                    hop(h, d, True).start()
+            if h == 1 and sc is not None:
+                over().start()
+
+        def recv(h):
+            for d in range(2):
+                @pl.when(may(h, d, False))
+                def _(d=d):
+                    hop(h, d, False).wait_recv()
+                    if sc is not None:
+                        across(h, d).start()
+
+        def finish():
+            over().wait_recv()
+            for h in (1, 2, 3):
+                for d in range(2):
+                    @pl.when(may(h, d, False))
+                    def _(d=d, h=h):
+                        across(h, d).wait_recv()
+
+        def sent():
+            if sc is not None:
+                over().wait_send()
+            for h in (1, 2, 3):
+                for d in range(2):
+                    @pl.when(may(h, d, True))
+                    def _(d=d, h=h):
+                        hop(h, d, True).wait_send()
+                    if sc is not None:
+                        @pl.when(may(h, d, False))
+                        def _(d=d, h=h):
+                            across(h, d).wait_send()
+        return send, recv, finish, sent
+
+    x_send, x_recv, x_finish, x_sent = chain(lambda b: xall.at[c, b], s_x, r_x, s_xc, r_xc)
+    y_send, y_recv, y_finish, y_sent = chain(lambda b: dyall.at[c, b], s_y, r_y, s_yc, r_yc)
+    q_send, q_recv, _, q_sent = chain(
+        lambda b: qkvw.at[pl.ds(pl.multiple_of(b * 384, 384), 384)], s_qkv, r_qkv)
 
     def back(src, dst, s, r):
         return lambda k: remote(src.at[zk[k]], dst.at[k - 1], s.at[k - 1], r.at[k - 1], dz[k])
 
-    g_z, o_z, gg_z = back(gsum, grecv, s_g, r_g), back(osum, orecv, s_o, r_o), back(ggsum, ggrecv, s_gg, r_gg)
+    g_z, o_z = back(gsum, grecv, s_g, r_g), back(osum, orecv, s_o, r_o)
     g_c = remote(gpart, gsib, s_gc, r_gc, dsib)
     o_c = remote(opart, osib, s_oc, r_oc, dsib)
-    gg_c = remote(ggp.at[1 - c], ggsib, s_ggc, r_ggc, dsib)
 
     def weights_a(k):
         if k:
@@ -384,30 +438,19 @@
              pltpu.make_async_copy(dy, dyall.at[c, z], sl.at[3])]
     for one in local:
         one.start()
-    for k in (1, 2, 3):
-        c_qkv(k).start()
-    my_proj = proj.at[pl.ds(pl.multiple_of(c * 192, 192), 192)]
-    own_proj = pltpu.make_async_copy(my_proj, projw, sl.at[4])
+    own_proj = pltpu.make_async_copy(proj.at[pl.ds(pl.multiple_of(c * 192, 192), 192)], projw, sl.at[4])
 
     @pl.when(z == p0)
     def _():
         own_proj.start()
-
-        @pl.when(z < 3)
-        def _():
-            c_proj(my_proj, 0).start()
-
-        @pl.when(z > 0)
-        def _():
-            c_proj(my_proj, 1).start()
-    weights_a(0)
-    for k in (1, 2, 3):
-        c_wz(k).start()
-
     tok_f = tok[...].astype(F32)
     inv1 = lax.rsqrt(jnp.mean(tok_f * tok_f, axis=1, keepdims=True) + EPS)
     for k in (1, 2, 3):
         c_small(k).wait_recv()
+    local[1].wait()
+    q_send(1)
+    for k in (1, 2, 3):
+        c_pz(k).start()
     local[0].wait()
     gain1 = jnp.concatenate([smalls[i, 0:1, :] for i in range(4)], axis=1).astype(F32)
     actp[c, p0] = (tok_f * inv1 * gain1).astype(BF)
@@ -417,36 +460,18 @@
         c_pre(i).start()
     c_actc(0).start()
     c_prec(0).start()
-
-    @pl.when(z == p0)
-    def _():
-        own_proj.wait()
-
-    @pl.when(z != p0)
-    def _():
-        c_proj(projw, 0).wait_recv()
-
-    @pl.when((z > p0) & (z < 3))
-    def _():
-        c_proj(projw, 0).start()
-
-    @pl.when((z < p0) & (z > 0))
-    def _():
-        c_proj(projw, 1).start()
-
-    weights_b(0)
+    q_recv(1)
+    q_send(2)
+    q_recv(2)
+    q_send(3)
     for i in range(3):
         c_act(i).wait_recv()
         c_pre(i).wait_recv()
         c_actc(i + 1).start()
         c_prec(i + 1).start()
-    for k in (1, 2, 3):
-        c_qkv(k).wait_recv()
-    local[1].wait()
+    weights_a(0)
+    q_recv(3)
     local[3].wait()
-    for k in (1, 2, 3):
-        y_z(k).start()
-    y_c(0).start()
 
     row = lax.broadcasted_iota(jnp.int32, (128, 128), 0)
     col = lax.broadcasted_iota(jnp.int32, (128, 128), 1)
@@ -477,25 +502,47 @@
         lax.fori_loop(0, 4, one, 0)
 
     attention(c)
-    weights_a(1)
     for i in range(4):
         c_actc(i).wait_recv()
         c_prec(i).wait_recv()
     attention(1 - c)
+    for k in (1, 2, 3):
+        c_pz(k).wait_recv()
+        owner = zf[k]
+
+        @pl.when(owner != p0)
+        def _(k=k, owner=owner):
+            c_pq(k, owner).start()
+
+        @pl.when(owner == p0)
+        def _(k=k):
+            projw[quarter(p0)] = projq[k - 1]
+
+    for k in (1, 3, 2):
+        c_wz(k).start()
+
+    @pl.when(z == p0)
+    def _():
+        own_proj.wait()
+
+    @pl.when(z != p0)
+    def _():
+        for i in range(3):
+            c_pq_in(i).wait_recv()
+
+    weights_b(0)
 
     def to_sib(i, _):
         part[i] = jnp.dot(att[1 - c, i], projw[...], preferred_element_type=F32).astype(BF)
         return 0
     lax.fori_loop(0, 4, to_sib, 0)
     c_sib().start()
-    weights_b(1)
     c_sib().wait_recv()
     for i in range(3):
         sums[i] = (jnp.dot(att[c, peers[i]], projw[...], preferred_element_type=F32)
                    + sibr[peers[i]].astype(F32)).astype(BF)
         c_pl(i).start()
     residual = (tok_f + jnp.dot(att[c, p0], projw[...], preferred_element_type=F32) + sibr[p0].astype(F32))
-    weights_a(2)
     for i in range(3):
         c_pl(i).wait_recv()
         residual = residual + plr[i].astype(F32)
@@ -503,10 +550,6 @@
     inv2 = lax.rsqrt(jnp.mean(residual * residual, axis=1, keepdims=True) + EPS)
     gain2 = jnp.concatenate([smalls[i, 1:2, :] for i in range(4)], axis=1).astype(F32)
     act2 = (residual * inv2 * gain2).astype(BF)
-    xall[c, z] = act2
-    for k in (1, 2, 3):
-        x_z(k).start()
-    x_c(0).start()
     router = jnp.concatenate([smalls[i, 16:32, :] for i in range(4)], axis=1)
     logits = lax.dot_general(act2, router, (((1,), (1,)), ((), ())), preferred_element_type=F32)
     chosen, kept = masks[0] > 0.0, masks[1]
@@ -514,39 +557,46 @@
     ge = jnp.where(chosen, jnp.exp(jnp.where(chosen, logits - top, 0.0)), 0.0)
     gt = ge / jnp.sum(ge, axis=1, keepdims=True)
     gates[...] = gt
-    wgt[c, z] = jnp.concatenate([gt * kept, jnp.zeros((128, 112), F32)], axis=1)
-    for k in (1, 2, 3):
-        w_z(k).start()
-    w_c(0).start()
+    wide_gates = jnp.concatenate([gt * kept, jnp.zeros((128, 112), F32)], axis=1)
+    gate_hi = wide_gates.astype(BF)
+    xall[c, z, :, :1536] = act2
+    xall[c, z, :, 1536:1664] = gate_hi
+    xall[c, z, :, 1664:] = (wide_gates - gate_hi.astype(F32)).astype(BF)
+    x_send(1)
+    weights_a(1)
+    weights_a(3)
+    weights_b(1)
+    x_recv(1)
+    x_send(2)
+    weights_b(3)
+    weights_a(2)
+    x_recv(2)
+    x_send(3)
+    y_send(1)
     weights_b(2)
-    weights_a(3)
-    for k in (1, 2, 3):
-        y_z(k).wait_recv()
-        y_c(k).start()
-    weights_b(3)
-    for k in (1, 2, 3):
-        x_z(k).wait_recv()
-        x_c(k).start()
-        w_z(k).wait_recv()
-        w_c(k).start()
+    x_recv(3)
+    y_recv(1)
+    y_send(2)
+    y_recv(2)
+    y_send(3)
+    y_recv(3)
     local[2].wait()
     for k in range(4):
         c_wp(k, 1).wait_recv()
         c_wp(k, 2).wait_recv()
-    for k in range(4):
-        x_c(k).wait_recv()
-        y_c(k).wait_recv()
-        w_c(k).wait_recv()
+    x_finish()
+    y_finish()
 
     lane = lax.broadcasted_iota(jnp.int32, (512, 128), 1)
     ggp[...] = jnp.zeros_like(ggp)
 
     def expert(n, _):
         j, t = n // 2, lax.rem(n, 2)
-        gu = jnp.dot(xall[t].reshape(512, 1536), wbuf[j, :, : 2 * half], preferred_element_type=F32)
+        gu = jnp.dot(xall[t, :, :, :1536].reshape(512, 1536), wbuf[j, :, : 2 * half], preferred_element_type=F32)
         bk = jnp.dot(dyall[t].reshape(512, 1536), wbuf[j, :, 2 * half :], preferred_element_type=F32)
         mine = lane == z * 4 + j
-        w = jnp.sum(jnp.where(mine, wgt[t].reshape(512, 128), 0.0), axis=1, keepdims=True)
+        both = (xall[t, :, :, 1536:1664].astype(F32) + xall[t, :, :, 1664:].astype(F32)).reshape(512, 128)
+        w = jnp.sum(jnp.where(mine, both, 0.0), axis=1, keepdims=True)
         g, u = gu[:, :half], gu[:, half:]
         sg = 1.0 / (1.0 + jnp.exp(-g))
         silu = g * sg
@@ -594,30 +644,35 @@
             return 0
         lax.fori_loop(0, 6, one, 0)
 
-    gg_c.start()
+    def put_gate_grads(dst, v):
+        hi = v.astype(BF)
+        dst[:, :, 1536:1664] = hi
+        dst[:, :, 1664:] = (v - hi.astype(F32)).astype(BF)
+
+    def gate_grads(v):
+        return v[..., 1536:1664].astype(F32) + v[..., 1664:].astype(F32)
+
+    put_gate_grads(gpart, ggp[1 - c])
     partial(True, gpart)
     g_c.start()
-    gg_c.wait_recv()
-    for k in range(4):
-        ggsum[zk[k]] = ggp[c, zk[k]] + ggsib[zk[k]]
-    for k in (1, 2, 3):
-        gg_z(k).start()
     partial(False, opart)
     o_c.start()
     g_c.wait_recv()
+    put_gate_grads(gsum, ggp[c] + gate_grads(gsib))
     own(True, gsib, gsum)
     for k in (1, 2, 3):
         g_z(k).start()
     o_c.wait_recv()
     own(False, osib, osum)
     for k in (1, 2, 3):
+        g_z(k).wait_recv()
+    for k in (1, 2, 3):
         o_z(k).start()
-    for k in (1, 2, 3):
-        gg_z(k).wait_recv()
-        g_z(k).wait_recv()
-    ggt[...] = (ggsum[z] + ggrecv[0] + ggrecv[1] + ggrecv[2])[:, :EXPERTS]
+    ggt[...] = (gate_grads(gsum[z]) + gate_grads(grecv[0]) + gate_grads(grecv[1])
+                + gate_grads(grecv[2]))[:, :EXPERTS]
     save(ggt, o_gg)
-    gact[...] = (gsum[z].astype(F32) + grecv[0].astype(F32) + grecv[1].astype(F32) + grecv[2].astype(F32))
+    gact[...] = (gsum[z, :, :1536].astype(F32) + grecv[0, :, :1536].astype(F32)
+                 + grecv[1, :, :1536].astype(F32) + grecv[2, :, :1536].astype(F32))
     save(gact, o_gact)
     for k in (1, 2, 3):
         o_z(k).wait_recv()
@@ -626,26 +681,25 @@
     save(outb, o_out)
 
     for k in (1, 2, 3):
-        for one in (c_small(k), c_qkv(k), c_wz(k), x_z(k), y_z(k), w_z(k), g_z(k), o_z(k), gg_z(k)):
+        for one in (c_small(k), c_pz(k), c_wz(k), g_z(k), o_z(k)):
             one.wait_send()
+
+        @pl.when(zf[k] != p0)
+        def _(k=k):
+            c_pq(k, zf[k]).wait_send()
     for k in range(4):
         for i in range(3):
             c_wp(k, i).wait_send()
-        for one in (c_actc(k), c_prec(k), x_c(k), y_c(k), w_c(k)):
+        for one in (c_actc(k), c_prec(k)):
             one.wait_send()
     for i in range(3):
         for one in (c_act(i), c_pre(i), c_pl(i)):
             one.wait_send()
-    for one in (c_sib(), g_c, o_c, gg_c):
+    for one in (c_sib(), g_c, o_c):
         one.wait_send()
-
-    @pl.when(up_ok)
-    def _():
-        c_proj(projw, 0).wait_send()
-
-    @pl.when(down_ok)
-    def _():
-        c_proj(projw, 1).wait_send()
+    x_sent()
+    y_sent()
+    q_sent()
     for one in saves:
         one.wait()
 
@@ -654,7 +708,7 @@
     sem, vm = pltpu.SemaphoreType.DMA, pltpu.VMEM
     out = lambda shape, kind=BF: jax.ShapeDtypeStruct(shape, kind)
     outs = (
-        out((2, 4, 128, 1536)), out((2, 4, 128, 1536)), out((4, 1024, 512)), out((4, 1024, 256)),
+        out((2, 4, 128, 1792)), out((2, 4, 128, 1536)), out((4, 1024, 512)), out((4, 1024, 256)),
         out((2, 4, 128, 1536)), out((2, 4, 384, 64)), out((2, 4, 128, 64)), out((2, 4, 128, 64)),
         out((2, 4, 384, 128), F32), out((2, 4, 128, 192)), out((1536, 320)), out((192, 1536)),
         out((4, 32, 384)), out((128, 1536), F32), out((128, 16), F32), out((128, 1536), F32),
@@ -662,22 +716,23 @@
     )
     block, quad = vm((2, 4, 128, 1536), BF), vm((4, 128, 1536), BF)
     three = vm((3, 128, 1536), BF)
+    quad_g, three_g = vm((4, 128, 1792), BF), vm((3, 128, 1792), BF)
     scratch = [
-        vm((4, 32, 384), BF), vm((1536, 320), BF), vm((192, 1536), BF), block, vm((2, 4, 8, 128), F32),
+        vm((4, 32, 384), BF), vm((1536, 320), BF), vm((192, 1536), BF), vm((3, 48, 1536), BF),
+        block, vm((2, 4, 8, 128), F32),
         vm((4, 128, 320), F32), vm((2, 4, 384, 64), BF), vm((2, 4, 128, 64), BF), vm((2, 4, 128, 64), BF),
         vm((2, 4, 384, 128), F32), vm((2, 4, 128, 192), BF), quad, quad, three, three,
-        block, block, vm((2, 4, 128, 128), F32), vm((4, 1536, 768), BF), vm((4, 1024, 512), BF),
-        vm((4, 1024, 256), BF), quad, quad, vm((2, 4, 128, 128), F32), quad, quad, vm((4, 128, 128), F32),
-        quad, quad, vm((4, 128, 128), F32), three, three, vm((3, 128, 128), F32),
+        vm((2, 4, 128, 1792), BF), block, vm((4, 1536, 768), BF), vm((4, 1024, 512), BF),
+        vm((4, 1024, 256), BF), quad_g, quad, vm((2, 4, 128, 128), F32), quad_g, quad,
+        quad_g, quad, three_g, three,
         vm((128, 1536), F32), vm((128, 16), F32), vm((128, 1536), F32), vm((128, 16), F32), vm((128, 1536), BF),
     ]
-    n3, n4 = sem((3,)), sem((4,))
-    one = sem(())
+    n3, n4, one = sem((3,)), sem((4,)), sem(())
+    hops = [sem((2, 3)), sem((2, 3)), sem((3, 3)), sem((3, 3))]
     sems = [
-        n3, n3, n3, n3, sem((2,)), one, n3, n3, sem((4, 3)), sem((4, 3)),
+        n3, n3, sem((2, 3)), sem((2, 3)), n3, n3, n3, n4, n3, n3, sem((4, 3)), sem((4, 3)),
         n3, n3, n3, n3, n4, n4, n4, n4, one, one, n3, n3,
-        n3, n3, n4, n4, n3, n3, n4, n4, n3, n3, n4, n4,
-        n3, n3, n3, n3, n3, n3, one, one, one, one, one, one, sem((24,)),
+        *hops, *hops, n3, n3, n3, n3, one, one, one, one, sem((24,)),
     ]
     vmem, any_ = pl.BlockSpec(memory_space=pltpu.VMEM), pl.BlockSpec(memory_space=pl.ANY)
     return pl.pallas_call(
@@ -966,7 +1021,7 @@
     (x_all, dy_all, ggu, hidden_w, act_plane, query, key, value, probs, attended, qkv_head, proj_head,
      smalls, residual, gates, gact, grad_gates, output) = front(
         tokens, cotangent, wpiece, qkv_cols, attn_proj, small, masks, prefix, cos_t, sin_t)
-    grad_gu, grad_dn = expert_grads(x_all.reshape(1024, width), dy_all.reshape(1024, width), ggu, hidden_w)
+    grad_gu, grad_dn = expert_grads(x_all.reshape(1024, 1792), dy_all.reshape(1024, width), ggu, hidden_w)
     grad_gu = grad_gu.reshape(own, EXPERTS, 2 * HID)
     grad_dn = grad_dn.reshape(own, EXPERTS, HID)
 

time: 794 us -> 725 us (0.913)
  Pallas kernels: 506 us -> 440 us
    pallas_call x1, Pallas kernels: 308 us -> 242 us  [front(): pl.pallas_call(front_kernel, out_shape=outs, in_specs=[vmem, any_, any_,...]
  transfers between devices with their start and end apart: 7 -> 7, of which waited for: 4 -> 4; matrix products, arithmetic and copies ran while one was open for 4% -> 4% of each run, Pallas kernels for 25% -> 27%
where the time goes in v4:
time: 725 us; the launch traced here: 724 us
  Pallas kernels  440 us (61%)
  waiting for transfers between devices  142 us (20%)
  local copies, waits for them, and re-layouts  62.5 us (9%)
  other arithmetic  25.9 us (4%)
  blocking collectives  24.1 us (3%)
  between operations  15.4 us (2%)
  matrix products  13.5 us (2%)
    pallas_call x1, Pallas kernels, front(): pl.pallas_call(front_kernel, out_shape=outs, in_specs=[vmem, any_, any_,...  242 us
    pallas_call x1, Pallas kernels, expert_grads(): pl.pallas_call(lambda *a: grads_kernel(nq, *a), out_shape=(jax.ShapeDtype...  198 us
    unnamed x49, local copies, waits for them, and re-layouts  41.7 us
    psum x1, waiting for transfers between devices, shards(): proj_sum = lax.psum(proj_term.astype(BF), 'grp')  39.1 us
    reduce_scatter x1, waiting for transfers between devices, shards(): lax.psum_scatter(gact_one.reshape(1024, width), 'rep', scatter_dimension=...  37.3 us
    all_gather x1, waiting for transfers between devices, shards(): lax.all_gather(gres_low, 'rep', axis=0)  35.3 us
    unnamed x8, waiting for transfers between devices  30.2 us
    psum x1, blocking collectives, shards(): lax.psum(lax.psum_scatter(terms, 'grp', scatter_dimension=0, tiled=True),...  24.1 us
  transfers between devices with their start and end apart: 7, of which 4 were waited for; matrix products, arithmetic and copies ran while one was open for 4% of the time, Pallas kernels for 27%

profile of v4, /device:TPU:0, one launch (start us, length us, event | category | flops | bytes accessed | tf_op | source)
XLA Modules:
  0.0 723.7 jit_solution(7755622972742176011)
XLA Ops:
  11.4 1.3 reduce.11
  13.7 2.5 convert_reduce_fusion
  17.9 3.2 constant_dynamic-slice_fusion.5
  21.3 2.1 copy.106
  24.6 1.1 constant_dynamic-slice_fusion.1
  27.8 242.3 %front.1 = (bf16[2,4,128,1792]{3,2,1,0:T(8,128)(2,1)}, bf16[2,4,128,1536]{3,2,1,0:T(8,128)(2,1)}, bf16[4,1024,512]{2,1,0:T(8,128)(2,1)}, bf16[4,1024,256]{2,1,0:...) custom-call(bf16[128,1536]{1,0:T(8,128)(2,1)} %tok.1, ...), custom_call_target="tpu_custom_call" | custom-call | tf_op jit(solution)/shard_map/front/pallas_call | solution.py:738
  270.2 1.5 convert_reduce_fusion.1
  274.4 1.3 multiply_reduce_fusion.2
  275.7 1.8 multiply_reduce_fusion
  278.8 1.9 copy.117
  280.7 35.3 %all-gather.8.cloned.1.call-done = bf16[1024,1536]{1,0:T(8,128)(2,1)} async-done(((bf16[128,1536]{1,0:T(8,128)(2,1)}), bf16[1024,1536]{1,0:T(8,128)(2,1)}) %all-gather.8.cloned.1.call-update) | async-done | bytes 3145744 | tf_op jit(solution)/shard_map/all_gather | solution.py:1053
  316.0 2.2 copy.113
  318.2 1.2 fusion.12
  322.8 1.9 convolution_convert_fusion
  324.7 1.9 copy.124
  326.6 3.3 convolution_convert_fusion.1
  329.9 1.4 copy.143
  331.9 3.7 fusion.5
  335.7 37.3 %reduce-scatter.6.cloned.1.call-done = bf16[128,1536]{1,0:T(8,128)(2,1)} async-done(((bf16[1024,1536]{1,0:T(8,128)(2,1)}), bf16[128,1536]{1,0:T(8,128)(2,1)}) %reduce-scatter.6.cloned.1.call-update) | async-done | bytes 393232 | tf_op jit(solution)/shard_map/reduce_scatter | solution.py:1077
  373.0 1.3 fusion.22
  375.1 30.1 %reduce-scatter.10.cloned.1.call-done = bf16[384,320]{1,0:T(8,128)(2,1)} async-done(((bf16[1536,320]{1,0:T(8,128)(2,1)}), bf16[384,320]{1,0:T(8,128)(2,1)}) %reduce-scatter.10.cloned.1.call-update) | async-done | bytes 245776
  405.2 1.8 copy.144
  407.0 39.1 %all-reduce.2.cloned.1.call-done = bf16[192,1536]{1,0:T(8,128)(2,1)} async-done(((bf16[192,1536]{1,0:T(8,128)(2,1)}), bf16[192,1536]{1,0:T(8,128)(2,1)}) %all-reduce.2.cloned.1.call-update) | async-done | bytes 589840 | tf_op jit(solution)/shard_map/psum | solution.py:1087
  446.1 197.7 %expert_grads.1 = (f32[6144,1024]{1,0:T(8,128)}, f32[6144,512]{1,0:T(8,128)}) custom-call(bf16[1024,1792]{1,0:T(8,128)(2,1)} %bitcast.139, bf16[1024,1536]{1,0:T(8,128)(2,1)} %bitcast.146, bf16[4,1024,512]{2,1,0:T(8,128)(2,1)} %get-tuple-element.45.a_2_, bf16[4,1024,256]{2,1,0:T(8,128)(2,1)} %get-tuple-element.46.a_3_), custom_call_target="tpu_custom_call" | custom-call | tf_op jit(solution)/shard_map/expert_grads/pallas_call | solution.py:242
  643.8 2.4 fusion.19
  646.3 24.1 %psum.14 = f32[384,18]{0,1:T(8,128)S(1)} all-reduce(f32[384,18]{0,1:T(8,128)} %reduce-scatter.8.cloned.1.call-done), channel_id=1, replica_groups=mesh['rep'=8,'grp'=4] {'rep'}, use_global_device_ids=true, to_apply=%region_13.14 | all-reduce | flops 6912 | bytes 55296 | tf_op jit(solution)/shard_map/psum | solution.py:1099
  671.6 2.0 convert_element_type.115
  675.5 2.2 pad_maximum_fusion
  677.6 5.4 copy.129
  683.1 3.0 dynamic-slice_convert_fusion
  686.9 17.7 %copy.172 = f32[384,16,1024]{2,1,0:T(8,128)} copy(f32[384,16,1024]{2,1,0:T(8,128)} %bitcast.129) | data formatting | bytes 50331648
  704.6 12.3 %copy.173 = f32[384,16,512]{2,1,0:T(8,128)} copy(f32[384,16,512]{2,1,0:T(8,128)} %bitcast.133) | data formatting | bytes 25165824
  (118 shorter events, 22.1 us)
Async XLA Ops:
  7.2 308.8 %all-gather.8.cloned.1.call-start = ((), (), s32[]{:S(2)}) async-start(), calls=%async_computation.7 | async-start | bytes 3538944 | tf_op jit(solution)/shard_map/all_gather | solution.py:1053
  21.3 5.3 copy-start.13
  24.6 247.8 %copy-start.4 = (f32[2,128,16]{2,1,0:T(8,128)S(1)}, f32[2,128,16]{2,1,0:T(8,128)}, u32[]{:S(2)}) copy-start(f32[2,128,16]{2,1,0:T(8,128)} %convert_element_type.90.masks) | copy-start | bytes 49156
  270.1 7.3 %copy-start = (f32[128,1536]{1,0:T(8,128)S(1)}, f32[128,1536]{1,0:T(8,128)}, u32[]{:S(2)}) copy-start(f32[128,1536]{1,0:T(8,128)} %get-tuple-element.30) | copy-start | bytes 2359300
  270.1 7.3 %copy-start.3 = (bf16[128,1536]{1,0:T(8,128)(2,1)S(1)}, bf16[128,1536]{1,0:T(8,128)(2,1)}, u32[]{:S(2)}) copy-start(bf16[128,1536]{1,0:T(8,128)(2,1)} %dy.1) | copy-start | bytes 1179652
  274.4 4.4 copy-start.8
  275.7 5.0 copy-start.14
  277.5 40.7 %copy-start.16 = (f32[128]{0:T(128)}, f32[128]{0:T(128)S(1)}, u32[]{:S(2)}) copy-start(f32[128]{0:T(128)S(1)} %broadcast_multiply_fusion.1) | copy-start | bytes 1540
  278.5 94.4 %reduce-scatter.6.cloned.1.call-start = ((), (), s32[]{:S(2)}) async-start(), calls=%async_computation.3 | async-start | bytes 3538944 | tf_op jit(solution)/shard_map/reduce_scatter | solution.py:1077
  316.0 2.2 copy-start.19
  318.2 1.4 copy-start.1
  318.2 1.7 copy-start.11
  319.9 1.1 copy-start.5
  320.3 1.3 copy-start.10
  321.5 1.3 copy-start.18
  322.6 2.1 copy-start.6
  326.6 78.6 %reduce-scatter.10.cloned.1.call-start = ((), (), s32[]{:S(2)}) async-start(), calls=%async_computation.9 | async-start | bytes 1474560
  329.9 1.5 copy-start.12
  329.9 1.5 copy-start.2
  329.9 1.7 copy-start.9
  329.9 1.7 copy-start.15
  331.4 114.7 %all-reduce.2.cloned.1.call-start = ((), (), s32[]{:S(2)}) async-start(), calls=%async_computation.5 | async-start | bytes 1179648 | tf_op jit(solution)/shard_map/psum | solution.py:1087
  335.6 310.6 %reduce-scatter.8.cloned.1.call-start = ((), (), s32[]{:S(2)}) async-start(), calls=%async_computation.4 | async-start | bytes 184320 | tf_op jit(solution)/shard_map/reduce_scatter | solution.py:1099
  375.0 296.6 %all-gather.10.cloned.1.call-start = ((), (), s32[]{:S(2)}) async-start(), calls=%async_computation.8 | async-start | bytes 2211840 | tf_op jit(solution)/shard_map/all_gather | solution.py:1088
  407.0 276.1 %all-gather.6.cloned.1.call-start = ((), (), s32[]{:S(2)}) async-start(), calls=%async_computation.6 | async-start | bytes 5308416 | tf_op jit(solution)/shard_map/all_gather | solution.py:1096
  446.1 197.7 %copy-start.17 = (f32[128]{0:T(128)S(1)}, f32[128]{0:T(128)}, u32[]{:S(2)}) copy-start(f32[128]{0:T(128)} %copy-done.16) | copy-start | bytes 1540
  683.1 3.0 copy-start.7
Sparse Core Ops, SparseCore 0:
  278.6 37.3 all-gather.7
  326.7 46.2 reduce-scatter.5
  376.0 29.1 reduce-scatter.9
  408.1 37.9 all-reduce.1
  448.9 18.9 reduce-scatter.7
  470.1 33.6 all-gather.9
  505.7 56.5 all-gather.5

commit v5 on v4

--- a/solution.py
+++ b/solution.py
@@ -64,206 +64,6 @@
     return bit + by * (1 - 2 * bit)
 
 
-def grads_kernel(nq, x_ref, dy_ref, ggu_ref, hw_ref, gu_out, dn_out,
-                 gw, recv1, send2, recv2, zs, zr, ag, sb, ib, st,
-                 s1, r1, s2, r2, sz, rz, sa, ra, ss, rs, so):
-    y, x, c, z = place()
-    half = HID // 2
-    wide = 3 * half
-
-    def slot(a, b):
-        return flip(y, a * c + b * (1 - c)) * 2 + flip(x, a * (1 - c) + b * c)
-
-    def dev(p, core, zz):
-        return (p * 2 + core, zz)
-
-    p0 = slot(0, 0)
-    d1, d2, dsib = dev(slot(1, 0), c, z), dev(slot(0, 1), c, z), dev(p0, 1 - c, z)
-    zk = [lax.rem(z + k, 4) for k in range(4)]
-    barrier = pltpu.get_barrier_semaphore()
-    for to in (d1, d2, dsib, dev(p0, c, zk[1]), dev(p0, c, zk[2]), dev(p0, c, zk[3])):
-        pl.semaphore_signal(barrier, 1, device_id=to, device_id_type=MESH)
-    pl.semaphore_wait(barrier, 6)
-
-    def copy1(q, b):
-        return pltpu.make_async_remote_copy(
-            gw.at[q // 2, slot(1, b), q % 2], recv1.at[q, b], s1.at[q, b], r1.at[q, b],
-            device_id=d1, device_id_type=MESH)
-
-    def copy2(q):
-        return pltpu.make_async_remote_copy(
-            send2.at[q % 2], recv2.at[q], s2.at[q], r2.at[q], device_id=d2, device_id_type=MESH)
-
-    def copyz(q, k):
-        return pltpu.make_async_remote_copy(
-            zs.at[q % 2, zk[k]], zr.at[q, z], sz.at[q, k - 1], rz.at[q, k - 1],
-            device_id=dev(p0, c, zk[k]), device_id_type=MESH)
-
-    def copya(q, i):
-        src, dst = ((0, 1), (0, 2), (1, 3))[i]
-        return pltpu.make_async_remote_copy(
-            ag.at[q, src], ag.at[q, dst], sa.at[q, i], ra.at[q, i],
-            device_id=d1 if i == 0 else d2, device_id_type=MESH)
-
-    def copys(q, i):
-        return pltpu.make_async_remote_copy(
-            ag.at[q, i], sb.at[q, i], ss.at[q, i], rs.at[q, i], device_id=dsib, device_id_type=MESH)
-
-    def out_copies(q, k, p, core):
-        rows = 256
-        at = pl.multiple_of(((q // 2) * 128 + p * 32 + (q % 2) * 16) * EXPERTS, rows)
-        lo = pl.multiple_of(core * half, half)
-        hi = pl.multiple_of(HID + core * half, half)
-        pairs = ((gu_out.at[pl.ds(at, rows), pl.ds(lo, half)], 0),
-                 (gu_out.at[pl.ds(at, rows), pl.ds(hi, half)], half),
-                 (dn_out.at[pl.ds(at, rows), pl.ds(lo, half)], 2 * half))
-        return [pltpu.make_async_copy(st.at[k, :, pl.ds(off, half)], ref, so.at[k, i])
-                for i, (ref, off) in enumerate(pairs)]
-
-    def emit(q, k, first, p, core, ref):
-        @pl.when(jnp.logical_not(first))
-        def _():
-            for one in out_copies(q, k, p, core):
-                one.wait()
-        st[k] = ref[...].astype(F32)
-        for one in out_copies(q, k, p, core):
-            one.start()
-
-    def stage1(q):
-        @pl.when(q % 2 == 0)
-        def _():
-            q3 = q // 2
-            xs = jnp.concatenate(
-                [x_ref[:, pl.ds(pl.multiple_of(zz * 384 + q3 * 128, 128), 128)] for zz in range(4)], axis=1)
-            ds_ = jnp.concatenate(
-                [dy_ref[:, pl.ds(pl.multiple_of(zz * 384 + q3 * 128, 128), 128)] for zz in range(4)], axis=1)
-
-            def one(j, _):
-                up = lax.dot_general(xs, ggu_ref[j], (((0,), (0,)), ((), ())),
-                                     preferred_element_type=F32).astype(BF)
-                dn = lax.dot_general(ds_, hw_ref[j], (((0,), (0,)), ((), ())),
-                                     preferred_element_type=F32).astype(BF)
-                for zz in range(4):
-                    for p in range(4):
-                        for h in range(2):
-                            at = zz * 128 + p * 32 + h * 16
-                            gw[q3, p, h, zz, j, :, : 2 * half] = up[at : at + 16]
-                            gw[q3, p, h, zz, j, :, 2 * half :] = dn[at : at + 16]
-                return 0
-            lax.fori_loop(0, 4, one, 0)
-        for b in range(2):
-            copy1(q, b).start()
-
-    def stage2(q):
-        for b in range(2):
-            copy1(q, b).wait_recv()
-
-        def one(zz, _):
-            send2[q % 2, zz] = (gw[q // 2, slot(0, 1), q % 2, zz].astype(F32)
-                                + recv1[q, 1, zz].astype(F32)).astype(BF)
-            return 0
-        lax.fori_loop(0, 4, one, 0)
-        copy2(q).start()
-
-    def stage3(q):
-        copy2(q).wait()
-
-        def one(zz, _):
-            zs[q % 2, zz] = (gw[q // 2, p0, q % 2, zz].astype(F32) + recv1[q, 0, zz].astype(F32)
-                             + recv2[q, zz].astype(F32)).astype(BF)
-            return 0
-        lax.fori_loop(0, 4, one, 0)
-        for k in range(1, 4):
-            copyz(q, k).start()
-        zr[q, z] = zs[q % 2, z]
-
-    def stage4(q):
-        for k in range(1, 4):
-            copyz(q, k).wait()
-        for zz in range(4):
-            for j in range(4):
-                for l in range(wide // 128):
-                    ib[l, pl.ds(zz * 4 + j, 16, stride=EXPERTS), :] = (
-                        zr[q, zz, j, :, l * 128 : (l + 1) * 128].astype(F32))
-        for l in range(wide // 128):
-            ag[q, 0, :, l * 128 : (l + 1) * 128] = ib[l].astype(BF)
-        copya(q, 0).start()
-        copys(q, 0).start()
-
-    def stage5(q):
-        copya(q, 0).wait_recv()
-        copya(q, 1).start()
-        copya(q, 2).start()
-        copys(q, 1).start()
-        emit(q, 0, q == 0, p0, c, ag.at[q, 0])
-        emit(q, 1, q == 0, slot(1, 0), c, ag.at[q, 1])
-
-    def stage6(q):
-        copya(q, 1).wait_recv()
-        copya(q, 2).wait_recv()
-        copys(q, 2).start()
-        copys(q, 3).start()
-        emit(q, 2, q == 0, slot(0, 1), c, ag.at[q, 2])
-        emit(q, 3, q == 0, slot(1, 1), c, ag.at[q, 3])
-
-    def stage7(q):
-        for i in range(4):
-            copys(q, i).wait_recv()
-        for i, p in enumerate((p0, slot(0, 1), slot(1, 0), slot(1, 1))):
-            emit(q, i, False, p, 1 - c, sb.at[q, i])
-        for i in range(4):
-            copys(q, i).wait_send()
-        for i in range(3):
-            copya(q, i).wait_send()
-        for b in range(2):
-            copy1(q, b).wait_send()
-
-    stages = (stage1, stage2, stage3, stage4, stage5, stage6, stage7)
-
-    def step(t, _):
-        for i, stage in enumerate(stages):
-            q = t - i
-
-            @pl.when((q >= 0) & (q < nq))
-            def _(stage=stage, q=q):
-                stage(q)
-        return 0
-
-    lax.fori_loop(0, nq + len(stages) - 1, step, 0)
-    for k in range(4):
-        for one in out_copies(0, k, p0, c):
-            one.wait()
-
-
-def expert_grads(xs, dys, ggu, hw):
-    nq, half, wide = 6, HID // 2, 3 * HID // 2
-    piece = (4, 4, 16, wide)
-    sem = pltpu.SemaphoreType.DMA
-    return pl.pallas_call(
-        lambda *a: grads_kernel(nq, *a),
-        out_shape=(jax.ShapeDtypeStruct((384 * 16, 2 * HID), F32), jax.ShapeDtypeStruct((384 * 16, HID), F32)),
-        in_specs=[pl.BlockSpec(memory_space=pltpu.VMEM)] * 4,
-        out_specs=[pl.BlockSpec(memory_space=pl.ANY)] * 2,
-        scratch_shapes=[
-            pltpu.VMEM((3, 4, 2) + piece, BF),
-            pltpu.VMEM((nq, 2) + piece, BF),
-            pltpu.VMEM((2,) + piece, BF),
-            pltpu.VMEM((nq,) + piece, BF),
-            pltpu.VMEM((2,) + piece, BF),
-            pltpu.VMEM((nq,) + piece, BF),
-            pltpu.VMEM((nq, 4, 256, wide), BF),
-            pltpu.VMEM((nq, 4, 256, wide), BF),
-            pltpu.VMEM((wide // 128, 256, 128), F32),
-            pltpu.VMEM((4, 256, wide), F32),
-            sem((nq, 2)), sem((nq, 2)), sem((nq,)), sem((nq,)), sem((nq, 3)), sem((nq, 3)),
-            sem((nq, 3)), sem((nq, 3)), sem((nq, 4)), sem((nq, 4)), sem((4, 3)),
-        ],
-        compiler_params=pltpu.CompilerParams(
-            collective_id=3, has_side_effects=True, vmem_limit_bytes=62 * 1024 * 1024),
-        name="expert_grads",
-    )(xs, dys, ggu, hw)
-
-
 def turn(v, cos, sin):
     lane = lax.broadcasted_iota(jnp.int32, v.shape, 1)
     partner = jnp.where(lax.rem(lane, 64) < 32, pltpu.roll(v, 96, 1), pltpu.roll(v, 32, 1))
@@ -272,14 +72,14 @@
 
 def front_kernel(tok, dy, wpiece, qkv_cols, proj, small, masks, prefix, cos_t, sin_t,
                  o_x, o_dy, o_ggu, o_hw, o_act, o_q, o_k, o_v, o_probs, o_att, o_qkvw, o_projw,
-                 o_small, o_res, o_gates, o_gact, o_gg, o_out,
+                 o_small, o_res, o_gates, o_gsum, o_osum,
                  smalls, qkvw, projw, projq, actp, pre, pr, qs, ks, vs, probs, att, part, sibr, sums, plr,
                  xall, dyall, wbuf, ggu, hw, gpart, opart, ggp, gsib, osib,
-                 gsum, osum, grecv, orecv, res, gates, gact, ggt, outb,
+                 gsum, osum, res, gates,
                  s_small, r_small, s_qkv, r_qkv, s_pz, r_pz, s_pq, r_pq, s_wz, r_wz, s_wp, r_wp,
                  s_act, r_act, s_pre, r_pre, s_actc, r_actc, s_prec, r_prec, s_sib, r_sib, s_pl, r_pl,
                  s_x, r_x, s_xc, r_xc, s_y, r_y, s_yc, r_yc,
-                 s_g, r_g, s_o, r_o, s_gc, r_gc, s_oc, r_oc, sl):
+                 s_gc, r_gc, s_oc, r_oc, sl):
     y, x, c, z = place()
     half = HID // 2
 
@@ -413,10 +213,6 @@
     q_send, q_recv, _, q_sent = chain(
         lambda b: qkvw.at[pl.ds(pl.multiple_of(b * 384, 384), 384)], s_qkv, r_qkv)
 
-    def back(src, dst, s, r):
-        return lambda k: remote(src.at[zk[k]], dst.at[k - 1], s.at[k - 1], r.at[k - 1], dz[k])
-
-    g_z, o_z = back(gsum, grecv, s_g, r_g), back(osum, orecv, s_o, r_o)
     g_c = remote(gpart, gsib, s_gc, r_gc, dsib)
     o_c = remote(opart, osib, s_oc, r_oc, dsib)
 
@@ -660,28 +456,13 @@
     g_c.wait_recv()
     put_gate_grads(gsum, ggp[c] + gate_grads(gsib))
     own(True, gsib, gsum)
-    for k in (1, 2, 3):
-        g_z(k).start()
+    save(gsum, o_gsum)
     o_c.wait_recv()
     own(False, osib, osum)
+    save(osum, o_osum)
+
     for k in (1, 2, 3):
-        g_z(k).wait_recv()
-    for k in (1, 2, 3):
-        o_z(k).start()
-    ggt[...] = (gate_grads(gsum[z]) + gate_grads(grecv[0]) + gate_grads(grecv[1])
-                + gate_grads(grecv[2]))[:, :EXPERTS]
-    save(ggt, o_gg)
-    gact[...] = (gsum[z, :, :1536].astype(F32) + grecv[0, :, :1536].astype(F32)
-                 + grecv[1, :, :1536].astype(F32) + grecv[2, :, :1536].astype(F32))
-    save(gact, o_gact)
-    for k in (1, 2, 3):
-        o_z(k).wait_recv()
-    outb[...] = (res[...] + osum[z].astype(F32) + orecv[0].astype(F32) + orecv[1].astype(F32)
-                 + orecv[2].astype(F32)).astype(BF)
-    save(outb, o_out)
-
-    for k in (1, 2, 3):
-        for one in (c_small(k), c_pz(k), c_wz(k), g_z(k), o_z(k)):
+        for one in (c_small(k), c_pz(k), c_wz(k)):
             one.wait_send()
 
         @pl.when(zf[k] != p0)
@@ -711,12 +492,12 @@
         out((2, 4, 128, 1792)), out((2, 4, 128, 1536)), out((4, 1024, 512)), out((4, 1024, 256)),
         out((2, 4, 128, 1536)), out((2, 4, 384, 64)), out((2, 4, 128, 64)), out((2, 4, 128, 64)),
         out((2, 4, 384, 128), F32), out((2, 4, 128, 192)), out((1536, 320)), out((192, 1536)),
-        out((4, 32, 384)), out((128, 1536), F32), out((128, 16), F32), out((128, 1536), F32),
-        out((128, 16), F32), out((128, 1536)),
+        out((4, 32, 384)), out((128, 1536), F32), out((128, 16), F32), out((4, 128, 1792)),
+        out((4, 128, 1536)),
     )
     block, quad = vm((2, 4, 128, 1536), BF), vm((4, 128, 1536), BF)
     three = vm((3, 128, 1536), BF)
-    quad_g, three_g = vm((4, 128, 1792), BF), vm((3, 128, 1792), BF)
+    quad_g = vm((4, 128, 1792), BF)
     scratch = [
         vm((4, 32, 384), BF), vm((1536, 320), BF), vm((192, 1536), BF), vm((3, 48, 1536), BF),
         block, vm((2, 4, 8, 128), F32),
@@ -724,15 +505,14 @@
         vm((2, 4, 384, 128), F32), vm((2, 4, 128, 192), BF), quad, quad, three, three,
         vm((2, 4, 128, 1792), BF), block, vm((4, 1536, 768), BF), vm((4, 1024, 512), BF),
         vm((4, 1024, 256), BF), quad_g, quad, vm((2, 4, 128, 128), F32), quad_g, quad,
-        quad_g, quad, three_g, three,
-        vm((128, 1536), F32), vm((128, 16), F32), vm((128, 1536), F32), vm((128, 16), F32), vm((128, 1536), BF),
+        quad_g, quad, vm((128, 1536), F32), vm((128, 16), F32),
     ]
     n3, n4, one = sem((3,)), sem((4,)), sem(())
     hops = [sem((2, 3)), sem((2, 3)), sem((3, 3)), sem((3, 3))]
     sems = [
         n3, n3, sem((2, 3)), sem((2, 3)), n3, n3, n3, n4, n3, n3, sem((4, 3)), sem((4, 3)),
         n3, n3, n3, n3, n4, n4, n4, n4, one, one, n3, n3,
-        *hops, *hops, n3, n3, n3, n3, one, one, one, one, sem((24,)),
+        *hops, *hops, one, one, one, one, sem((24,)),
     ]
     vmem, any_ = pl.BlockSpec(memory_space=pltpu.VMEM), pl.BlockSpec(memory_space=pl.ANY)
     return pl.pallas_call(
@@ -745,6 +525,509 @@
             collective_id=1, has_side_effects=True, vmem_limit_bytes=62 * 1024 * 1024),
         name="front",
     )(tok, dy, wpiece, qkv_cols, proj, small, masks, prefix, cos_t, sin_t)
+
+
+def back_kernel(i_x, i_dy, i_ggu, i_hw, i_act, i_q, i_k, i_v, i_probs, i_att, i_qkvw, i_projw, i_small,
+                i_res, i_gates, i_gsum, i_osum, tok, kept, cos_t, sin_t,
+                o_e, o_gtok, o_qg, o_pg, o_terms, o_op,
+                xb, dyb, ggu, hw, qs, ks, vs, probs, att, qkvw, projw, smalls, res, gates, gown, grecv,
+                gw, recv1, send2, recv2, zs, zr, ib, agv,
+                gres, gresf, gproj, sibr, plr, qgp, qz, qgo, pgp, pgr, pq2, pgo, terms, tz, tsib, tpl, tout, gtok,
+                s1, r1, s2, r2, sz, rz, sa, ra, ss, rs, la,
+                s_g, r_g, s_gr, r_gr, s_grc, r_grc, s_sib, r_sib, s_pl, r_pl, s_qz, r_qz, s_qo, r_qo,
+                s_qoc, r_qoc, s_p1, r_p1, s_p2, r_p2, s_po, r_po, s_poc, r_poc, s_tz, r_tz, s_ts, r_ts,
+                s_tp, r_tp, s_o, r_o, ld, sv):
+    y, x, c, z = place()
+    half = HID // 2
+    wide = 3 * half
+    nq = 6
+
+    def slot(a, b):
+        return flip(y, a * c + b * (1 - c)) * 2 + flip(x, a * (1 - c) + b * c)
+
+    p0, p1, p2, p3 = slot(0, 0), slot(1, 0), slot(0, 1), slot(1, 1)
+    peers = (p1, p2, p3)
+    d1, d2, dsib = (p1 * 2 + c, z), (p2 * 2 + c, z), (p0 * 2 + 1 - c, z)
+    dpl = [(p * 2 + c, z) for p in peers]
+    zk = [lax.rem(z + k, 4) for k in range(4)]
+    dz = [(p0 * 2 + c, zz) for zz in zk]
+
+    loads = {}
+
+    def load(name, src, dst):
+        loads[name] = pltpu.make_async_copy(src, dst, ld.at[len(loads)])
+        loads[name].start()
+    load("x", i_x.at[:, :, :, pl.ds(0, 1536)], xb)
+    load("ggu", i_ggu, ggu)
+    load("dy", i_dy, dyb)
+    load("hw", i_hw, hw)
+    load("gown", i_gsum.at[z], gown)
+    for name, src, dst in (("res", i_res, res), ("gates", i_gates, gates), ("small", i_small, smalls),
+                           ("projw", i_projw, projw), ("probs", i_probs, probs), ("q", i_q, qs), ("k", i_k, ks),
+                           ("v", i_v, vs), ("att", i_att, att), ("qkvw", i_qkvw, qkvw)):
+        load(name, src, dst)
+
+    barrier = pltpu.get_barrier_semaphore()
+    for to in dpl + dz[1:] + [dsib]:
+        pl.semaphore_signal(barrier, 1, device_id=to, device_id_type=MESH)
+    pl.semaphore_wait(barrier, 7)
+
+    def remote(src, dst, s, r, to):
+        return pltpu.make_async_remote_copy(src, dst, s, r, device_id=to, device_id_type=MESH)
+
+    def copy1(q, b):
+        return remote(gw.at[q // 2, slot(1, b), lax.rem(q, 2)], recv1.at[q, b], s1.at[q, b], r1.at[q, b], d1)
+
+    def copy2(q):
+        return remote(send2.at[lax.rem(q, 2)], recv2.at[q], s2.at[q], r2.at[q], d2)
+
+    def copyz(q, k):
+        return remote(zs.at[lax.rem(q, 2), zk[k]], zr.at[q, z], sz.at[q, k - 1], rz.at[q, k - 1], dz[k])
+
+    def rows(q, p):
+        return pl.ds(pl.multiple_of(((q // 2) * 8 + p * 2 + lax.rem(q, 2)) * 256, 256), 256)
+
+    def copya(q, i):
+        p, who = ((p0, d1), (p0, d2), (p1, d2))[i]
+        src = agv.at[lax.rem(q, 2)] if i < 2 else o_e.at[c, rows(q, p)]
+        return remote(src, o_e.at[c, rows(q, p)], sa.at[q, i], ra.at[q, i], who)
+
+    def copys(q, i):
+        p = (p0, p1, p2, p3)[i]
+        src = agv.at[lax.rem(q, 2)] if i == 0 else o_e.at[c, rows(q, p)]
+        return remote(src, o_e.at[c, rows(q, p)], ss.at[q, i], rs.at[q, i], dsib)
+
+    def keep(q):
+        return pltpu.make_async_copy(agv.at[lax.rem(q, 2)], o_e.at[c, rows(q, p0)], la.at[q])
+
+    def c_g(k):
+        return remote(i_gsum.at[zk[k]], grecv.at[k - 1], s_g.at[k - 1], r_g.at[k - 1], dz[k])
+
+    def c_o(k):
+        return remote(i_osum.at[zk[k]], o_op.at[k - 1], s_o.at[k - 1], r_o.at[k - 1], dz[k])
+
+    def c_gr(i):
+        return remote(gres.at[c, p0], gres.at[c, p0], s_gr.at[i], r_gr.at[i], dpl[i])
+
+    def c_grc(i):
+        p = (p0, p1, p2, p3)[i]
+        return remote(gres.at[c, p], gres.at[c, p], s_grc.at[i], r_grc.at[i], dsib)
+
+    def c_sib():
+        return remote(dyb.at[0], sibr, s_sib, r_sib, dsib)
+
+    def c_pl(i):
+        return remote(dyb.at[1, i], plr.at[i], s_pl.at[i], r_pl.at[i], dpl[i])
+
+    def c_qz(k):
+        return remote(qgp.at[zk[k]], qz.at[k - 1], s_qz.at[k - 1], r_qz.at[k - 1], dz[k])
+
+    def c_qo(i):
+        return remote(qgo, o_qg.at[p0 * 2 + c], s_qo.at[i], r_qo.at[i], dpl[i])
+
+    def c_qoc(i):
+        r = (p0, p1, p2, p3)[i] * 2 + c
+        return remote(qgo if i == 0 else o_qg.at[r], o_qg.at[r], s_qoc.at[i], r_qoc.at[i], dsib)
+
+    def c_p1(i):
+        return remote(pgp.at[peers[i]], pgr.at[p0], s_p1.at[i], r_p1.at[i], dpl[i])
+
+    def c_p2(k):
+        return remote(pgr.at[zk[k]], pq2.at[k - 1], s_p2.at[k - 1], r_p2.at[k - 1], dz[k])
+
+    def c_po(i):
+        return remote(pgo, o_pg.at[c, p0], s_po.at[i], r_po.at[i], dpl[i])
+
+    def c_poc(i):
+        p = (p0, p1, p2, p3)[i]
+        return remote(pgo if i == 0 else o_pg.at[c, p], o_pg.at[c, p], s_poc.at[i], r_poc.at[i], dsib)
+
+    def lanes_of(zz):
+        return pl.ds(pl.multiple_of(zz * 384, 384), 384)
+
+    def c_tz(k):
+        return remote(terms.at[:, lanes_of(zk[k])], tz.at[k], s_tz.at[k - 1], r_tz.at[k - 1], dz[k])
+
+    def c_ts():
+        return remote(tz.at[0], tsib, s_ts, r_ts, dsib)
+
+    def c_tp(i):
+        return remote(tpl.at[p0], tpl.at[p0], s_tp.at[i], r_tp.at[i], dpl[i])
+
+    saves = [pltpu.make_async_copy(gtok, o_gtok, sv.at[0]),
+             pltpu.make_async_copy(qgo, o_qg.at[p0 * 2 + c], sv.at[1]),
+             pltpu.make_async_copy(pgo, o_pg.at[c, p0], sv.at[2]),
+             pltpu.make_async_copy(tout, o_terms, sv.at[3])]
+    act_load = pltpu.make_async_copy(i_act, xb, sv.at[4])
+
+    for k in (1, 2, 3):
+        c_g(k).start()
+    loads["x"].wait()
+    loads["ggu"].wait()
+    loads["dy"].wait()
+    loads["hw"].wait()
+
+    def stage1(q):
+        @pl.when(lax.rem(q, 2) == 0)
+        def _():
+            q3 = q // 2
+
+            def side(ref):
+                return jnp.concatenate(
+                    [ref[:, :, :, pl.ds(pl.multiple_of(zz * 384 + q3 * 128, 128), 128)].reshape(1024, 128)
+                     for zz in range(4)], axis=1)
+            xs, ds_ = side(xb), side(dyb)
+
+            def one(j, _):
+                up = lax.dot_general(xs, ggu[j], (((0,), (0,)), ((), ())), preferred_element_type=F32).astype(BF)
+                dn = lax.dot_general(ds_, hw[j], (((0,), (0,)), ((), ())), preferred_element_type=F32).astype(BF)
+                for zz in range(4):
+                    for p in range(4):
+                        for h in range(2):
+                            at = zz * 128 + p * 32 + h * 16
+                            gw[q3, p, h, zz, j, :, : 2 * half] = up[at : at + 16]
+                            gw[q3, p, h, zz, j, :, 2 * half :] = dn[at : at + 16]
+                return 0
+            lax.fori_loop(0, 4, one, 0)
+        for b in range(2):
+            copy1(q, b).start()
+
+    def stage2(q):
+        for b in range(2):
+            copy1(q, b).wait_recv()
+
+        def one(zz, _):
+            send2[lax.rem(q, 2), zz] = (gw[q // 2, p2, lax.rem(q, 2), zz].astype(F32)
+                                        + recv1[q, 1, zz].astype(F32)).astype(BF)
+            return 0
+        lax.fori_loop(0, 4, one, 0)
+        copy2(q).start()
+
+    def stage3(q):
+        copy2(q).wait()
+
+        def one(zz, _):
+            zs[lax.rem(q, 2), zz] = (gw[q // 2, p0, lax.rem(q, 2), zz].astype(F32) + recv1[q, 0, zz].astype(F32)
+                                     + recv2[q, zz].astype(F32)).astype(BF)
+            return 0
+        lax.fori_loop(0, 4, one, 0)
+        for k in range(1, 4):
+            copyz(q, k).start()
+        zr[q, z] = zs[lax.rem(q, 2), z]
+
+    def stage4(q):
+        for k in range(1, 4):
+            copyz(q, k).wait()
+
+        @pl.when(q >= 2)
+        def _():
+            copya(q - 2, 0).wait_send()
+            copya(q - 2, 1).wait_send()
+            copys(q - 2, 0).wait_send()
+            keep(q - 2).wait()
+        for zz in range(4):
+            for j in range(4):
+                for l in range(wide // 128):
+                    ib[l, pl.ds(zz * 4 + j, 16, stride=EXPERTS), :] = (
+                        zr[q, zz, j, :, l * 128 : (l + 1) * 128].astype(F32))
+        for l in range(wide // 128):
+            agv[lax.rem(q, 2), :, l * 128 : (l + 1) * 128] = ib[l].astype(BF)
+        copya(q, 0).start()
+        copys(q, 0).start()
+        keep(q).start()
+
+    def stage5(q):
+        copya(q, 0).wait_recv()
+        copya(q, 1).start()
+        copya(q, 2).start()
+        copys(q, 1).start()
+
+    def stage6(q):
+        copya(q, 1).wait_recv()
+        copya(q, 2).wait_recv()
+        copys(q, 2).start()
+        copys(q, 3).start()
+
+    def stage7(q):
+        for i in range(4):
+            copys(q, i).wait_recv()
+
+    def norm_two():
+        r = res[...]
+        inv = lax.rsqrt(jnp.mean(r * r, axis=1, keepdims=True) + EPS)
+        return inv, r * inv
+
+    def norm_one():
+        t = tok[...].astype(F32)
+        inv = lax.rsqrt(jnp.mean(t * t, axis=1, keepdims=True) + EPS)
+        return inv, t * inv
+
+    def gain(row):
+        return jnp.concatenate([smalls[i, row : row + 1, :] for i in range(4)], axis=1).astype(F32)
+
+    def event_residual():
+        for name in ("gown", "res", "gates", "small"):
+            loads[name].wait()
+        for k in (1, 2, 3):
+            c_g(k).wait_recv()
+        tail = slice(1536, 1664), slice(1664, 1792)
+
+        def gate_part(v):
+            return (v[:, tail[0]].astype(F32) + v[:, tail[1]].astype(F32))[:, :EXPERTS]
+        gg = (gate_part(gown[...]) + gate_part(grecv[0]) + gate_part(grecv[1]) + gate_part(grecv[2])) * kept[...]
+        gt = gates[...]
+        gl = (gt * (gg - jnp.sum(gt * gg, axis=1, keepdims=True))).astype(BF)
+        router_t = jnp.concatenate([smalls[i, 16:32, :] for i in range(4)], axis=1)
+        ga = jnp.dot(gl, router_t, preferred_element_type=F32)
+        ga = ga + gown[:, :1536].astype(F32)
+        for k in range(3):
+            ga = ga + grecv[k, :, :1536].astype(F32)
+        inv, normed = norm_two()
+        terms[8:24, :] = lax.dot_general(gl, xb[c, z], (((0,), (0,)), ((), ())), preferred_element_type=F32)
+        terms[1:2, :] = jnp.sum(ga * normed, axis=0, keepdims=True)
+        scaled = ga * gain(1)
+        gr = dyb[c, z].astype(F32) + inv * (scaled - normed * jnp.mean(scaled * normed, axis=1, keepdims=True))
+        gresf[...] = gr
+        gres[c, p0] = gr.astype(BF)
+        for i in range(3):
+            c_gr(i).start()
+        c_grc(0).start()
+
+    def event_share():
+        for i in range(3):
+            c_gr(i).wait_recv()
+            c_grc(i + 1).start()
+        act_load.start()
+
+    scale = 64 ** -0.5
+
+    def event_attention():
+        for name in ("projw", "probs", "q", "k", "v", "att", "qkvw"):
+            loads[name].wait()
+        for i in range(4):
+            c_grc(i).wait_recv()
+
+        def one(n, _):
+            cc, i = n // 4, lax.rem(n, 4)
+            gb = lax.dot_general(gres[cc, i], projw[...], (((1,), (1,)), ((), ())),
+                                 preferred_element_type=F32).astype(BF)
+            ga = jnp.concatenate([gb[:, h * 64 : (h + 1) * 64] for h in range(3)], axis=0)
+            pb = probs[cc, i]
+            gv = lax.dot_general(pb.astype(BF), ga, (((0,), (0,)), ((), ())), preferred_element_type=F32)
+            gp = lax.dot_general(ga, vs[cc, i], (((1,), (1,)), ((), ())), preferred_element_type=F32)
+            gs = (pb * (gp - jnp.sum(pb * gp, axis=-1, keepdims=True))).astype(BF)
+            gq = jnp.dot(gs, ks[cc, i], preferred_element_type=F32) * scale
+            gk = lax.dot_general(gs, qs[cc, i], (((0,), (0,)), ((), ())), preferred_element_type=F32) * scale
+            lo = jnp.concatenate([gq[0:128], gq[128:256]], axis=1)
+            hi = jnp.concatenate([gq[256:384], gk], axis=1)
+            gproj[cc, i, :, 0:128] = turn(lo, cos_t[...], -sin_t[...]).astype(BF)
+            gproj[cc, i, :, 128:256] = turn(hi, cos_t[...], -sin_t[...]).astype(BF)
+            gproj[cc, i, :, 256:320] = gv.astype(BF)
+            return 0
+        lax.fori_loop(0, 8, one, 0)
+
+        def to_sib(i, _):
+            dyb[0, i] = lax.dot_general(gproj[1 - c, i], qkvw[...], (((1,), (1,)), ((), ())),
+                                        preferred_element_type=F32).astype(BF)
+            return 0
+        lax.fori_loop(0, 4, to_sib, 0)
+        c_sib().start()
+        pg = lax.dot_general(att[...].reshape(1024, 192), gres[...].reshape(1024, 1536), (((0,), (0,)), ((), ())),
+                             preferred_element_type=F32)
+        pgp[...] = pg.astype(BF).reshape(4, 48, 1536)
+        for i in range(3):
+            c_p1(i).start()
+        pgr[p0] = pgp[p0]
+
+    def event_columns():
+        act_load.wait()
+
+        def one(zz, _):
+            a = xb[:, :, :, lanes_of(zz)].reshape(1024, 384)
+            qgp[zz] = lax.dot_general(a, gproj[...].reshape(1024, 320), (((0,), (0,)), ((), ())),
+                                      preferred_element_type=F32).astype(BF)
+            return 0
+        lax.fori_loop(0, 4, one, 0)
+        for k in (1, 2, 3):
+            c_qz(k).start()
+        c_sib().wait()
+
+        def part(p):
+            return lax.dot_general(gproj[c, p], qkvw[...], (((1,), (1,)), ((), ())),
+                                   preferred_element_type=F32) + sibr[p].astype(F32)
+        for i in range(3):
+            dyb[1, i] = part(peers[i]).astype(BF)
+            c_pl(i).start()
+        gtok[...] = part(p0)
+        for i in range(3):
+            c_p1(i).wait_recv()
+        for k in (1, 2, 3):
+            c_p2(k).start()
+
+    def event_tokens():
+        ga = gtok[...]
+        for i in range(3):
+            c_pl(i).wait_recv()
+            ga = ga + plr[i].astype(F32)
+        inv, normed = norm_one()
+        terms[0:1, :] = jnp.sum(ga * normed, axis=0, keepdims=True)
+        scaled = ga * gain(0)
+        gtok[...] = gresf[...] + inv * (scaled - normed * jnp.mean(scaled * normed, axis=1, keepdims=True))
+        saves[0].start()
+        for k in (1, 2, 3):
+            c_tz(k).start()
+        for k in (1, 2, 3):
+            c_qz(k).wait_recv()
+        qgo[...] = (qgp[z].astype(F32) + qz[0].astype(F32) + qz[1].astype(F32) + qz[2].astype(F32)).astype(BF)
+        for i in range(3):
+            c_qo(i).start()
+        c_qoc(0).start()
+        saves[1].start()
+        for k in (1, 2, 3):
+            c_p2(k).wait_recv()
+        pgo[...] = (pgr[z].astype(F32) + pq2[0].astype(F32) + pq2[1].astype(F32) + pq2[2].astype(F32)).astype(BF)
+        for i in range(3):
+            c_po(i).start()
+        c_poc(0).start()
+        saves[2].start()
+        for k in (1, 2, 3):
+            c_o(k).start()
+
+    def event_terms():
+        for k in (1, 2, 3):
+            c_tz(k).wait_recv()
+        tz[0] = terms[:, lanes_of(z)] + tz[1] + tz[2] + tz[3]
+        c_ts().start()
+        for i in range(3):
+            c_qo(i).wait_recv()
+            c_qoc(i + 1).start()
+            c_po(i).wait_recv()
+            c_poc(i + 1).start()
+
+    def event_sums():
+        c_ts().wait()
+        tpl[p0] = tz[0] + tsib[...]
+        for i in range(3):
+            c_tp(i).start()
+
+    def event_last():
+        for i in range(3):
+            c_tp(i).wait_recv()
+        tout[...] = tpl[0] + tpl[1] + tpl[2] + tpl[3]
+        saves[3].start()
+        for i in range(4):
+            c_qoc(i).wait_recv()
+            c_poc(i).wait_recv()
+        for k in (1, 2, 3):
+            c_o(k).wait_recv()
+
+    stages = (stage1, stage2, stage3, stage4, stage5, stage6, stage7)
+    events = {3: event_residual, 4: event_share, 5: event_attention, 6: event_columns, 8: event_tokens,
+              9: event_terms, 10: event_sums, 11: event_last}
+
+    def step(t, _):
+        for i, stage in enumerate(stages):
+            q = t - i
+
+            @pl.when((q >= 0) & (q < nq))
+            def _(stage=stage, q=q):
+                stage(q)
+        for at, event in events.items():
+            @pl.when(t == at)
+            def _(event=event):
+                event()
+        return 0
+
+    lax.fori_loop(0, nq + len(stages) - 1, step, 0)
+
+    def left(q, _):
+        for b in range(2):
+            copy1(q, b).wait_send()
+        for i in range(1, 4):
+            copys(q, i).wait_send()
+        copya(q, 2).wait_send()
+
+        @pl.when(q >= nq - 2)
+        def _():
+            copya(q, 0).wait_send()
+            copya(q, 1).wait_send()
+            copys(q, 0).wait_send()
+            keep(q).wait()
+        return 0
+    lax.fori_loop(0, nq, left, 0)
+    for k in (1, 2, 3):
+        for one in (c_g(k), c_o(k), c_qz(k), c_p2(k), c_tz(k)):
+            one.wait_send()
+    for i in range(3):
+        for one in (c_gr(i), c_pl(i), c_qo(i), c_p1(i), c_po(i), c_tp(i)):
+            one.wait_send()
+    for i in range(4):
+        for one in (c_grc(i), c_qoc(i), c_poc(i)):
+            one.wait_send()
+    for one in saves:
+        one.wait()
+
+
+def back(front_outs, tok, kept, cos_t, sin_t):
+    nq, wide = 6, 3 * HID // 2
+    sem, vm = pltpu.SemaphoreType.DMA, pltpu.VMEM
+    out = lambda shape, kind=BF: jax.ShapeDtypeStruct(shape, kind)
+    piece = (4, 4, 16, wide)
+    outs = (out((2, 6144, wide)), out((128, 1536), F32), out((8, 384, 320)), out((2, 4, 48, 1536)),
+            out((24, 384), F32), out((3, 128, 1536)))
+    block, quad, three = vm((2, 4, 128, 1536), BF), vm((4, 128, 1536), BF), vm((3, 128, 1536), BF)
+    scratch = [
+        block, block, vm((4, 1024, 512), BF), vm((4, 1024, 256), BF), vm((2, 4, 384, 64), BF),
+        vm((2, 4, 128, 64), BF), vm((2, 4, 128, 64), BF), vm((2, 4, 384, 128), F32), vm((2, 4, 128, 192), BF),
+        vm((1536, 320), BF), vm((192, 1536), BF), vm((4, 32, 384), BF), vm((128, 1536), F32), vm((128, 16), F32),
+        vm((128, 1792), BF), vm((3, 128, 1792), BF),
+        vm((3, 4, 2) + piece, BF), vm((nq, 2) + piece, BF), vm((2,) + piece, BF), vm((nq,) + piece, BF),
+        vm((2,) + piece, BF), vm((nq,) + piece, BF), vm((wide // 128, 256, 128), F32), vm((2, 256, wide), BF),
+        block, vm((128, 1536), F32), vm((2, 4, 128, 320), BF), quad, three, vm((4, 384, 320), BF),
+        vm((3, 384, 320), BF), vm((384, 320), BF), vm((4, 48, 1536), BF), vm((4, 48, 1536), BF),
+        vm((3, 48, 1536), BF), vm((48, 1536), BF), vm((24, 1536), F32), vm((4, 24, 384), F32),
+        vm((24, 384), F32), vm((4, 24, 384), F32), vm((24, 384), F32), vm((128, 1536), F32),
+    ]
+    n3, n4, one = sem((3,)), sem((4,)), sem(())
+    sems = [
+        sem((nq, 2)), sem((nq, 2)), sem((nq,)), sem((nq,)), sem((nq, 3)), sem((nq, 3)), sem((nq, 3)), sem((nq, 3)),
+        sem((nq, 4)), sem((nq, 4)), sem((nq,)),
+        n3, n3, n3, n3, n4, n4, one, one, n3, n3, n3, n3, n3, n3,
+        n4, n4, n3, n3, n3, n3, n3, n3, n4, n4, n3, n3, one, one,
+        n3, n3, n3, n3, sem((16,)), sem((5,)),
+    ]
+    vmem, any_ = pl.BlockSpec(memory_space=pltpu.VMEM), pl.BlockSpec(memory_space=pl.ANY)
+    return pl.pallas_call(
+        back_kernel,
+        out_shape=outs,
+        in_specs=[any_] * 17 + [vmem] * 4,
+        out_specs=[any_] * len(outs),
+        scratch_shapes=scratch + sems,
+        compiler_params=pltpu.CompilerParams(
+            collective_id=2, has_side_effects=True, vmem_limit_bytes=62 * 1024 * 1024),
+        name="back",
+    )(*front_outs, tok, kept, cos_t, sin_t)
+
+
+def widen_kernel(v, gu, dn):
+    half = HID // 2
+    for c in range(2):
+        gu[:, c * half : (c + 1) * half] = v[c, :, :half].astype(F32)
+        gu[:, HID + c * half : HID + (c + 1) * half] = v[c, :, half : 2 * half].astype(F32)
+        dn[:, c * half : (c + 1) * half] = v[c, :, 2 * half :].astype(F32)
+
+
+def widen(v):
+    rows, step = v.shape[1], 512
+    return pl.pallas_call(
+        widen_kernel,
+        out_shape=(jax.ShapeDtypeStruct((rows, 2 * HID), F32), jax.ShapeDtypeStruct((rows, HID), F32)),
+        grid=(rows // step,),
+        in_specs=[pl.BlockSpec((2, step, 3 * HID // 2), lambda i: (0, i, 0))],
+        out_specs=[pl.BlockSpec((step, 2 * HID), lambda i: (i, 0)), pl.BlockSpec((step, HID), lambda i: (i, 0))],
+        compiler_params=pltpu.CompilerParams(vmem_limit_bytes=40 * 1024 * 1024),
+        name="widen",
+    )(v)
 
 
 def expert_grads_general(reps, grps, xs, dys, ggu, hw):
@@ -1018,95 +1301,30 @@
     prefix = jnp.broadcast_to(prefix_len.astype(F32), (8, 128))
     cos, sin = rope_tables(seq)
     cos_t, sin_t = jnp.tile(cos, (1, 4)), jnp.tile(jnp.concatenate([-sin, sin], axis=1), (1, 2))
-    (x_all, dy_all, ggu, hidden_w, act_plane, query, key, value, probs, attended, qkv_head, proj_head,
-     smalls, residual, gates, gact, grad_gates, output) = front(
-        tokens, cotangent, wpiece, qkv_cols, attn_proj, small, masks, prefix, cos_t, sin_t)
-    grad_gu, grad_dn = expert_grads(x_all.reshape(1024, 1792), dy_all.reshape(1024, width), ggu, hidden_w)
-    grad_gu = grad_gu.reshape(own, EXPERTS, 2 * HID)
-    grad_dn = grad_dn.reshape(own, EXPERTS, HID)
-
-    gain_one = smalls[:, 0].reshape(1, width).astype(F32)
-    gain_two = smalls[:, 1].reshape(1, width).astype(F32)
-    router_t = jnp.concatenate([smalls[i, 16:] for i in range(4)], axis=1)
-    tokens_f = tokens.astype(F32)
-    inverse_one = lax.rsqrt(jnp.mean(tokens_f * tokens_f, axis=1, keepdims=True) + EPS)
-    normed_one = tokens_f * inverse_one
-    inverse_two = lax.rsqrt(jnp.mean(residual * residual, axis=1, keepdims=True) + EPS)
-    normed_two = residual * inverse_two
-    act_two = (normed_two * gain_two).astype(BF)
-
-    grad_gates = grad_gates * masks[1]
-    grad_logits = (gates * (grad_gates - jnp.sum(gates * grad_gates, axis=1, keepdims=True))).astype(BF)
-    gact = gact + dot(grad_logits, router_t)
-    router_term = dot(act_two.T, grad_logits)
-    gain_two_term = jnp.sum(gact * normed_two, axis=0)
-    scaled = gact * gain_two
-    dy = cotangent.astype(F32)
-    grad_residual = dy + inverse_two * (
-        scaled - normed_two * jnp.mean(scaled * normed_two, axis=1, keepdims=True)
-    )
-    gres_low = grad_residual.astype(BF)
-
-    def by_core(v):
-        return v.reshape(4, 2, *v.shape[1:]).swapaxes(0, 1)
-
-    gres_plane = by_core(lax.all_gather(gres_low, "rep", axis=0)).reshape(1024, width)
-    query = query.reshape(heads, QPK, seq, hw)
-    key, value = key.reshape(heads, seq, hw), value.reshape(heads, seq, hw)
-    probs = probs.reshape(heads, QPK, seq, seq)
-    attended = attended.reshape(heads * seq, qw)
-    proj_term = dot(attended.T, gres_plane)
-    grad_att = dot(gres_plane, proj_head.T).astype(BF).reshape(heads, seq, QPK, hw)
-    grad_value = jnp.einsum("bgst,bsgd->btd", probs.astype(BF), grad_att, preferred_element_type=F32)
-    grad_probs = jnp.einsum("bsgd,btd->bgst", grad_att, value, preferred_element_type=F32)
-    grad_scores = (
-        probs * (grad_probs - jnp.sum(probs * grad_probs, axis=-1, keepdims=True))
-    ).astype(BF)
-    scale = HEAD_WIDTH ** (-0.5)
-    grad_query = jnp.einsum("bgst,btd->bsgd", grad_scores, key, preferred_element_type=F32) * scale
-    grad_key = jnp.einsum("bgst,bgsd->btd", grad_scores, query, preferred_element_type=F32) * scale
-    turned_back = rotate(
-        jnp.concatenate([grad_query, grad_key[:, :, None]], axis=2),
-        cos[None, :, None, :],
-        -sin[None, :, None, :],
-    )
-    gproj = jnp.concatenate([turned_back, grad_value[:, :, None]], axis=2).astype(BF)
-    gproj = gproj.reshape(heads * seq, qw + 2 * hw)
-    qkv_term = dot(act_plane.reshape(1024, width).T, gproj)
-    gact_one = dot(gproj, qkv_head.T).astype(BF).reshape(2, 4, seq, width).swapaxes(0, 1)
-    gact_one = lax.psum_scatter(
-        gact_one.reshape(1024, width), "rep", scatter_dimension=0, tiled=True
-    ).astype(F32)
-    gain_one_term = jnp.sum(gact_one * normed_one, axis=0)
-    scaled_one = gact_one * gain_one
-    grad_tokens = grad_residual + inverse_one * (
-        scaled_one - normed_one * jnp.mean(scaled_one * normed_one, axis=1, keepdims=True)
-    )
-
-    qkv_own = lax.psum_scatter(qkv_term.astype(BF), "grp", scatter_dimension=0, tiled=True)
-    proj_sum = lax.psum(proj_term.astype(BF), "grp")
-    qkv_own = lax.all_gather(qkv_own, "rep", axis=0, tiled=False).astype(F32)
+    parts = front(tokens, cotangent, wpiece, qkv_cols, attn_proj, small, masks, prefix, cos_t, sin_t)
+    residual, out_sum = parts[13], parts[16]
+    wide, grad_tokens, qkv_own, proj_own, terms, out_parts = back(parts, tokens, masks[1], cos_t, sin_t)
+    grad_gu, grad_dn = widen(wide)
+    out = lax.dynamic_index_in_dim(out_sum, lax.axis_index("grp"), 0, False).astype(F32)
+    output = (residual + out + jnp.sum(out_parts.astype(F32), axis=0)).astype(BF)
     grad_qkv = jnp.concatenate(
         [
-            qkv_own[:, :, lo:hi].transpose(1, 0, 2).reshape(own, -1)
+            jnp.concatenate([qkv_own[h, :, lo:hi] for h in range(heads)], axis=1)
             for lo, hi in ((0, qw), (qw, qw + hw), (qw + hw, qw + 2 * hw))
         ],
         axis=1,
-    )
-    proj_all = lax.all_gather(proj_sum, "rep", axis=0, tiled=True)
-    grad_proj = lax.dynamic_slice_in_dim(proj_all, lax.axis_index("grp") * own, own, 0).astype(F32)
-    terms = jnp.concatenate([gain_one_term[:, None], gain_two_term[:, None], router_term], axis=1)
-    terms = lax.psum(lax.psum_scatter(terms, "grp", scatter_dimension=0, tiled=True), "rep")
+    ).astype(F32)
+    grad_proj = proj_own.reshape(own, width).astype(F32)
     return (
         output,
         grad_tokens,
-        terms[:, 0],
+        terms[0],
         grad_qkv,
         grad_proj,
-        terms[:, 1],
-        terms[:, 2:],
-        grad_gu,
-        grad_dn,
+        terms[1],
+        terms[8:].T,
+        grad_gu.reshape(own, EXPERTS, 2 * HID),
+        grad_dn.reshape(own, EXPERTS, HID),
     )
 
 

time: 725 us -> 473 us (0.65)
  waiting for transfers between devices: 142 us -> 0 us
  local copies, waits for them, and re-layouts: 62.5 us -> 19.8 us
  blocking collectives: 24.1 us -> 0 us
  between operations: 15.4 us -> 1.55 us
  matrix products: 13.5 us -> 0 us
  other arithmetic: 25.9 us -> 15.6 us
    pallas_call x1, Pallas kernels: 242 us -> 183 us  [front(): pl.pallas_call(front_kernel, out_shape=outs, in_specs=[vmem, any_, any_,...]
    pallas_call x1 -> x2, Pallas kernels: 198 us -> 250 us  [the longest x1 229 us: back(): pl.pallas_call(back_kernel, out_shape=outs, in_specs=[any_] * 17 + [vmem]...]
    unnamed x49 -> x14, local copies, waits for them, and re-layouts: 41.7 us -> 1.42 us
    psum x1 -> x0, waiting for transfers between devices: 39.1 us -> none  [shards(): proj_sum = lax.psum(proj_term.astype(BF), 'grp')]
    reduce_scatter x2 -> x0, waiting for transfers between devices: 37.3 us -> none  [the longest x1 37.3 us: shards(): lax.psum_scatter(gact_one.reshape(1024, width), 'rep', scatter_dimension=...]
    all_gather x3 -> x0, waiting for transfers between devices: 35.3 us -> none  [the longest x1 35.3 us: shards(): lax.all_gather(gres_low, 'rep', axis=0)]
    unnamed x8 -> x0, waiting for transfers between devices: 30.2 us -> none
    psum x1 -> x0, blocking collectives: 24.1 us -> none  [shards(): lax.psum(lax.psum_scatter(terms, 'grp', scatter_dimension=0, tiled=True),...]
  transfers between devices with their start and end apart: 7 -> 0, of which waited for: 4 -> 0; matrix products, arithmetic and copies ran while one was open for 4% -> 0% of each run, Pallas kernels for 27% -> 0%
where the time goes in v5:
time: 473 us; the launch traced here: 470 us
  Pallas kernels  433 us (92%)
  local copies, waits for them, and re-layouts  19.8 us (4%)
  other arithmetic  15.6 us (3%)
    pallas_call x1, Pallas kernels, back(): pl.pallas_call(back_kernel, out_shape=outs, in_specs=[any_] * 17 + [vmem]...  229 us
    pallas_call x1, Pallas kernels, front(): pl.pallas_call(front_kernel, out_shape=outs, in_specs=[vmem, any_, any_,...  183 us
    pallas_call x1, Pallas kernels, widen(): pl.pallas_call(widen_kernel, out_shape=(jax.ShapeDtypeStruct((rows, 2 * H...  20.6 us

profile of v5, /device:TPU:0, one launch (start us, length us, event | category | flops | bytes accessed | tf_op | source)
XLA Modules:
  0.0 469.6 jit_solution(6110573426936967237)
XLA Ops:
  1.4 0.7 broadcast_in_dim.38
  2.1 0.7 broadcast_in_dim.39
  2.8 0.7 fusion.2
  3.5 0.5 broadcast.59
  4.0 1.3 reduce.7
  5.4 0.6 broadcast_in_dim.45.prefix
  6.0 1.4 pad_maximum_fusion.2.small
  7.3 0.1 fusion.5
  7.5 0.7 copy.44.sin_t
  8.4 0.7 select_reduce_fusion
  9.2 2.5 convert_reduce_fusion.1
  11.8 0.1 copy.42
  12.0 0.7 copy.43.cos_t
  12.7 0.7 slice_bitcast_fusion.24.kept
  13.4 1.1 constant_dynamic-slice_fusion.1
  14.5 1.1 constant_dynamic-slice_fusion.2
  15.6 0.8 pad_maximum_fusion.qkv_cols
  16.4 3.2 constant_dynamic-slice_fusion.5
  19.6 0.2 maximum_bitcast_fusion
  19.8 2.1 copy.38
  21.9 182.7 %front.1 = (bf16[2,4,128,1792]{3,2,1,0:T(8,128)(2,1)}, bf16[2,4,128,1536]{3,2,1,0:T(8,128)(2,1)}, bf16[4,1024,512]{2,1,0:T(8,128)(2,1)}, bf16[4,1024,256]{2,1,0:...) custom-call(bf16[128,1536]{1,0:T(8,128)(2,1)} %tok.3, ...), custom_call_target="tpu_custom_call" | custom-call | tf_op jit(solution)/shard_map/front/pallas_call | solution.py:518
  204.6 229.5 %back.1 = (bf16[2,6144,768]{2,1,0:T(8,128)(2,1)}, f32[128,1536]{1,0:T(8,128)}, bf16[8,384,320]{2,1,0:T(8,128)(2,1)}, bf16[2,4,48,1536]{3,2,1,0:T(8,128)(2,1)}, f...) custom-call(bf16[2,4,128,1792]{3,2,1,0:T(8,128)(2,1)} %get-tuple-element.36.i_x, ...), custom_call_target="tpu_custom_call" | custom-call | tf_op jit(solution)/shard_map/back/pallas_call | solution.py:1000
  434.1 1.7 convert_reduce_fusion
  435.8 1.9 fusion.1
  437.7 0.6 slice_reduce_fusion
  438.3 0.6 slice_bitcast_fusion.25
  439.0 1.3 slice_bitcast_fusion.8
  440.3 3.6 concatenate.19
  443.9 2.4 convert_element_type.40
  446.4 1.8 bitcast_convert_fusion
  448.1 20.6 %widen.1 = (f32[6144,1024]{1,0:T(8,128)}, f32[6144,512]{1,0:T(8,128)}) custom-call(bf16[2,6144,768]{2,1,0:T(8,128)(2,1)} %get-tuple-element.56.v), custom_call_target="tpu_custom_call" | custom-call | tf_op jit(solution)/shard_map/widen/pallas_call | solution.py:1022
  468.7 0.9 copy.49
  (27 shorter events, 0.5 us)
Async XLA Ops:
  12.7 6.9 %copy-start.3 = (f32[2,128,16]{2,1,0:T(8,128)}, f32[2,128,16]{2,1,0:T(8,128)S(1)}, u32[]{:S(2)}) copy-start(f32[2,128,16]{2,1,0:T(8,128)S(1)} %convert_element_type.33.masks) | copy-start | bytes 49156
  204.6 231.2 %copy-start.1 = (f32[128,1536]{1,0:T(8,128)S(1)}, f32[128,1536]{1,0:T(8,128)}, u32[]{:S(2)}) copy-start(f32[128,1536]{1,0:T(8,128)} %get-tuple-element.34.i_res) | copy-start | bytes 2359300
  434.1 3.6 copy-start.5
  434.1 4.8 %copy-start = (bf16[8,384,320]{2,1,0:T(8,128)(2,1)S(1)}, bf16[8,384,320]{2,1,0:T(8,128)(2,1)}, u32[]{:S(2)}) copy-start(bf16[8,384,320]{2,1,0:T(8,128)(2,1)} %get-tuple-element.54) | copy-start | bytes 5898244
  443.9 2.4 copy-start.2
  448.1 20.6 %copy-start.4 = (f32[128,1536]{1,0:T(8,128)S(1)}, f32[128,1536]{1,0:T(8,128)}, u32[]{:S(2)}) copy-start(f32[128,1536]{1,0:T(8,128)} %get-tuple-element.103) | copy-start | bytes 2359300

commit v6 on v5

--- a/solution.py
+++ b/solution.py
@@ -1,5 +1,6 @@
 import jax
 import jax.numpy as jnp
+import numpy as np
 from jax import lax
 from jax.experimental import pallas as pl
 from jax.experimental.pallas import tpu as pltpu
@@ -70,12 +71,12 @@
     return v * cos + partner * sin
 
 
-def front_kernel(tok, dy, wpiece, qkv_cols, proj, small, masks, prefix, cos_t, sin_t,
+def front_kernel(tok, dy, w_gu, w_dn, qkv, proj, small, ids, prio, prefix, cos_t, sin_t,
                  o_x, o_dy, o_ggu, o_hw, o_act, o_q, o_k, o_v, o_probs, o_att, o_qkvw, o_projw,
-                 o_small, o_res, o_gates, o_gsum, o_osum,
+                 o_small, o_res, o_gates, o_kept, o_gsum, o_osum,
                  smalls, qkvw, projw, projq, actp, pre, pr, qs, ks, vs, probs, att, part, sibr, sums, plr,
-                 xall, dyall, wbuf, ggu, hw, gpart, opart, ggp, gsib, osib,
-                 gsum, osum, res, gates,
+                 xall, dyall, wbuf, ggu, hw, gpart, ggp, gsib,
+                 gsum, res, gates, kept, qwin, wst, wcol, wpiece,
                  s_small, r_small, s_qkv, r_qkv, s_pz, r_pz, s_pq, r_pq, s_wz, r_wz, s_wp, r_wp,
                  s_act, r_act, s_pre, r_pre, s_actc, r_actc, s_prec, r_prec, s_sib, r_sib, s_pl, r_pl,
                  s_x, r_x, s_xc, r_xc, s_y, r_y, s_yc, r_yc,
@@ -213,6 +214,7 @@
     q_send, q_recv, _, q_sent = chain(
         lambda b: qkvw.at[pl.ds(pl.multiple_of(b * 384, 384), 384)], s_qkv, r_qkv)
 
+    opart, osib, osum = part, sibr, sums
     g_c = remote(gpart, gsib, s_gc, r_gc, dsib)
     o_c = remote(opart, osib, s_oc, r_oc, dsib)
 
@@ -229,21 +231,38 @@
     for k in (1, 2, 3):
         c_small(k).start()
     local = [pltpu.make_async_copy(small, smalls.at[z], sl.at[0]),
-             pltpu.make_async_copy(qkv_cols, qkvw.at[pl.ds(pl.multiple_of(z * 384, 384), 384)], sl.at[1]),
-             pltpu.make_async_copy(wpiece.at[z], wbuf.at[:, rows(z, p0)], sl.at[2]),
              pltpu.make_async_copy(dy, dyall.at[c, z], sl.at[3])]
-    for one in local:
+
+    def window(off, width, at, n):
+        src = qkv.at[:, pl.ds(pl.multiple_of(off, 128), width)]
+        return pltpu.make_async_copy(src, qwin.at[:, pl.ds(at, width)], sl.at[n])
+    mine = p0 * 96
+    windows = [window(384 * p0 + 128 * c, 256, 0, 1), window(1536 + 128 * p0, 128, 256, 2),
+               window(2048 + 128 * p0, 128, 384, 24)]
+    pieces = [pltpu.make_async_copy(
+        ref.at[pl.ds(pl.multiple_of(mine, 96), 96), :, pl.ds(pl.multiple_of(off, half), half)],
+        wst.at[:, :, pl.ds(i * half, half)], sl.at[25 + i])
+        for i, (ref, off) in enumerate(((w_gu, c * half), (w_gu, HID + c * half), (w_dn, c * half)))]
+    for one in local + windows + pieces:
         one.start()
     own_proj = pltpu.make_async_copy(proj.at[pl.ds(pl.multiple_of(c * 192, 192), 192)], projw, sl.at[4])
 
     @pl.when(z == p0)
     def _():
         own_proj.start()
+    for one in windows:
+        one.wait()
+    cols = qwin[...].astype(F32)
+    own_rows = pl.ds(pl.multiple_of(z * 384, 384), 384)
+    for at, lo, width in ((0, 0, 256), (192, 256, 128), (256, 384, 128)):
+        part_ = cols[:, lo : lo + width]
+        part_ = jnp.where(c == 0, part_, pltpu.roll(part_, width - 64, 1)).astype(BF)
+        qkvw[own_rows, at : at + (192 if at == 0 else 64)] = part_[:, : 192 if at == 0 else 64]
+
     tok_f = tok[...].astype(F32)
     inv1 = lax.rsqrt(jnp.mean(tok_f * tok_f, axis=1, keepdims=True) + EPS)
     for k in (1, 2, 3):
         c_small(k).wait_recv()
-    local[1].wait()
     q_send(1)
     for k in (1, 2, 3):
         c_pz(k).start()
@@ -256,8 +275,37 @@
         c_pre(i).start()
     c_actc(0).start()
     c_prec(0).start()
+    chosen_f = jnp.zeros((128, 128), F32)
+    rank_of = jnp.zeros((128, 128), F32)
+    lane_e = lax.broadcasted_iota(jnp.int32, (128, 128), 1)
+    for k in range(8):
+        hit = ids[:, k : k + 1] == lane_e
+        chosen_f = jnp.where(hit, 1.0, chosen_f)
+        rank_of = jnp.where(hit, prio[:, k : k + 1].astype(F32), rank_of)
+    rank_of = jnp.where(chosen_f > 0.0, rank_of, 65536.0)
+    rank_t = rank_of.T
+    slots = jnp.zeros((128, 128), F32)
+    for e in range(EXPERTS):
+        before = jnp.sum((rank_t[e : e + 1, :] < rank_of[:, e : e + 1]).astype(F32), axis=1, keepdims=True)
+        slots = jnp.where(lane_e == e, before, slots)
+    kept_f = jnp.where(slots < CAP, chosen_f, 0.0)
+    kept[...] = kept_f[:, :EXPERTS]
     q_recv(1)
     q_send(2)
+
+    for one in pieces:
+        one.wait()
+
+    def expert_rows(l, _):
+        wcol[...] = wst[:, :, pl.ds(pl.multiple_of(l * 128, 128), 128)].astype(F32).reshape(1536, 128)
+        for e in range(EXPERTS):
+            wpiece[e // 4, e % 4, :, pl.ds(pl.multiple_of(l * 128, 128), 128)] = (
+                wcol[pl.ds(e, 96, stride=EXPERTS), :].astype(BF))
+        return 0
+    lax.fori_loop(0, 6, expert_rows, 0)
+    own_piece = pltpu.make_async_copy(wpiece.at[z], wbuf.at[:, rows(z, p0)], sl.at[28])
+    own_piece.start()
+    weights_a(0)
     q_recv(2)
     q_send(3)
     for i in range(3):
@@ -265,9 +313,8 @@
         c_pre(i).wait_recv()
         c_actc(i + 1).start()
         c_prec(i + 1).start()
-    weights_a(0)
     q_recv(3)
-    local[3].wait()
+    local[1].wait()
 
     row = lax.broadcasted_iota(jnp.int32, (128, 128), 0)
     col = lax.broadcasted_iota(jnp.int32, (128, 128), 1)
@@ -348,12 +395,12 @@
     act2 = (residual * inv2 * gain2).astype(BF)
     router = jnp.concatenate([smalls[i, 16:32, :] for i in range(4)], axis=1)
     logits = lax.dot_general(act2, router, (((1,), (1,)), ((), ())), preferred_element_type=F32)
-    chosen, kept = masks[0] > 0.0, masks[1]
+    chosen = chosen_f[:, :EXPERTS] > 0.0
     top = jnp.max(jnp.where(chosen, logits, -1e30), axis=1, keepdims=True)
     ge = jnp.where(chosen, jnp.exp(jnp.where(chosen, logits - top, 0.0)), 0.0)
     gt = ge / jnp.sum(ge, axis=1, keepdims=True)
     gates[...] = gt
-    wide_gates = jnp.concatenate([gt * kept, jnp.zeros((128, 112), F32)], axis=1)
+    wide_gates = jnp.concatenate([gt * kept[...], jnp.zeros((128, 112), F32)], axis=1)
     gate_hi = wide_gates.astype(BF)
     xall[c, z, :, :1536] = act2
     xall[c, z, :, 1536:1664] = gate_hi
@@ -376,7 +423,7 @@
     y_recv(2)
     y_send(3)
     y_recv(3)
-    local[2].wait()
+    own_piece.wait()
     for k in range(4):
         c_wp(k, 1).wait_recv()
         c_wp(k, 2).wait_recv()
@@ -413,7 +460,7 @@
         saves.append(one)
     for src, dst in ((xall, o_x), (dyall, o_dy), (ggu, o_ggu), (hw, o_hw), (actp, o_act), (qs, o_q), (ks, o_k),
                      (vs, o_v), (probs, o_probs), (att, o_att), (qkvw, o_qkvw), (projw, o_projw),
-                     (smalls, o_small), (res, o_res), (gates, o_gates)):
+                     (smalls, o_small), (res, o_res), (gates, o_gates), (kept, o_kept)):
         save(src, dst)
 
     def block(grad, t, n):
@@ -448,6 +495,9 @@
     def gate_grads(v):
         return v[..., 1536:1664].astype(F32) + v[..., 1664:].astype(F32)
 
+    c_sib().wait_send()
+    for i in range(3):
+        c_pl(i).wait_send()
     put_gate_grads(gpart, ggp[1 - c])
     partial(True, gpart)
     g_c.start()
@@ -474,9 +524,9 @@
         for one in (c_actc(k), c_prec(k)):
             one.wait_send()
     for i in range(3):
-        for one in (c_act(i), c_pre(i), c_pl(i)):
+        for one in (c_act(i), c_pre(i)):
             one.wait_send()
-    for one in (c_sib(), g_c, o_c):
+    for one in (g_c, o_c):
         one.wait_send()
     x_sent()
     y_sent()
@@ -485,14 +535,14 @@
         one.wait()
 
 
-def front(tok, dy, wpiece, qkv_cols, proj, small, masks, prefix, cos_t, sin_t):
+def front(*args):
     sem, vm = pltpu.SemaphoreType.DMA, pltpu.VMEM
     out = lambda shape, kind=BF: jax.ShapeDtypeStruct(shape, kind)
     outs = (
         out((2, 4, 128, 1792)), out((2, 4, 128, 1536)), out((4, 1024, 512)), out((4, 1024, 256)),
         out((2, 4, 128, 1536)), out((2, 4, 384, 64)), out((2, 4, 128, 64)), out((2, 4, 128, 64)),
         out((2, 4, 384, 128), F32), out((2, 4, 128, 192)), out((1536, 320)), out((192, 1536)),
-        out((4, 32, 384)), out((128, 1536), F32), out((128, 16), F32), out((4, 128, 1792)),
+        out((4, 32, 384)), out((128, 1536), F32), out((128, 16), F32), out((128, 16), F32), out((4, 128, 1792)),
         out((4, 128, 1536)),
     )
     block, quad = vm((2, 4, 128, 1536), BF), vm((4, 128, 1536), BF)
@@ -502,35 +552,36 @@
         vm((4, 32, 384), BF), vm((1536, 320), BF), vm((192, 1536), BF), vm((3, 48, 1536), BF),
         block, vm((2, 4, 8, 128), F32),
         vm((4, 128, 320), F32), vm((2, 4, 384, 64), BF), vm((2, 4, 128, 64), BF), vm((2, 4, 128, 64), BF),
-        vm((2, 4, 384, 128), F32), vm((2, 4, 128, 192), BF), quad, quad, three, three,
+        vm((2, 4, 384, 128), F32), vm((2, 4, 128, 192), BF), quad, quad, quad, three,
         vm((2, 4, 128, 1792), BF), block, vm((4, 1536, 768), BF), vm((4, 1024, 512), BF),
-        vm((4, 1024, 256), BF), quad_g, quad, vm((2, 4, 128, 128), F32), quad_g, quad,
-        quad_g, quad, vm((128, 1536), F32), vm((128, 16), F32),
+        vm((4, 1024, 256), BF), quad_g, vm((2, 4, 128, 128), F32), quad_g,
+        quad_g, vm((128, 1536), F32), vm((128, 16), F32), vm((128, 16), F32),
+        vm((384, 512), BF), vm((96, 16, 768), BF), vm((1536, 128), F32), vm((4, 4, 96, 768), BF),
     ]
     n3, n4, one = sem((3,)), sem((4,)), sem(())
     hops = [sem((2, 3)), sem((2, 3)), sem((3, 3)), sem((3, 3))]
     sems = [
         n3, n3, sem((2, 3)), sem((2, 3)), n3, n3, n3, n4, n3, n3, sem((4, 3)), sem((4, 3)),
         n3, n3, n3, n3, n4, n4, n4, n4, one, one, n3, n3,
-        *hops, *hops, one, one, one, one, sem((24,)),
+        *hops, *hops, one, one, one, one, sem((29,)),
     ]
     vmem, any_ = pl.BlockSpec(memory_space=pltpu.VMEM), pl.BlockSpec(memory_space=pl.ANY)
     return pl.pallas_call(
         front_kernel,
         out_shape=outs,
-        in_specs=[vmem, any_, any_, any_, any_, any_, vmem, vmem, vmem, vmem],
+        in_specs=[vmem, any_, any_, any_, any_, any_, any_, vmem, vmem, vmem, vmem, vmem],
         out_specs=[any_] * len(outs),
         scratch_shapes=scratch + sems,
         compiler_params=pltpu.CompilerParams(
             collective_id=1, has_side_effects=True, vmem_limit_bytes=62 * 1024 * 1024),
         name="front",
-    )(tok, dy, wpiece, qkv_cols, proj, small, masks, prefix, cos_t, sin_t)
+    )(*args)
 
 
 def back_kernel(i_x, i_dy, i_ggu, i_hw, i_act, i_q, i_k, i_v, i_probs, i_att, i_qkvw, i_projw, i_small,
-                i_res, i_gates, i_gsum, i_osum, tok, kept, cos_t, sin_t,
+                i_res, i_gates, i_kept, i_gsum, i_osum, tok, cos_t, sin_t,
                 o_e, o_gtok, o_qg, o_pg, o_terms, o_op,
-                xb, dyb, ggu, hw, qs, ks, vs, probs, att, qkvw, projw, smalls, res, gates, gown, grecv,
+                xb, dyb, ggu, hw, qs, ks, vs, probs, att, qkvw, projw, smalls, res, gates, kept, gown, grecv,
                 gw, recv1, send2, recv2, zs, zr, ib, agv,
                 gres, gresf, gproj, sibr, plr, qgp, qz, qgo, pgp, pgr, pq2, pgo, terms, tz, tsib, tpl, tout, gtok,
                 s1, r1, s2, r2, sz, rz, sa, ra, ss, rs, la,
@@ -562,7 +613,8 @@
     load("dy", i_dy, dyb)
     load("hw", i_hw, hw)
     load("gown", i_gsum.at[z], gown)
-    for name, src, dst in (("res", i_res, res), ("gates", i_gates, gates), ("small", i_small, smalls),
+    for name, src, dst in (("res", i_res, res), ("gates", i_gates, gates), ("kept", i_kept, kept),
+                           ("small", i_small, smalls),
                            ("projw", i_projw, projw), ("probs", i_probs, probs), ("q", i_q, qs), ("k", i_k, ks),
                            ("v", i_v, vs), ("att", i_att, att), ("qkvw", i_qkvw, qkvw)):
         load(name, src, dst)
@@ -604,7 +656,7 @@
         return remote(i_gsum.at[zk[k]], grecv.at[k - 1], s_g.at[k - 1], r_g.at[k - 1], dz[k])
 
     def c_o(k):
-        return remote(i_osum.at[zk[k]], o_op.at[k - 1], s_o.at[k - 1], r_o.at[k - 1], dz[k])
+        return remote(i_osum.at[zk[k]], o_op.at[k], s_o.at[k - 1], r_o.at[k - 1], dz[k])
 
     def c_gr(i):
         return remote(gres.at[c, p0], gres.at[c, p0], s_gr.at[i], r_gr.at[i], dpl[i])
@@ -658,6 +710,8 @@
              pltpu.make_async_copy(qgo, o_qg.at[p0 * 2 + c], sv.at[1]),
              pltpu.make_async_copy(pgo, o_pg.at[c, p0], sv.at[2]),
              pltpu.make_async_copy(tout, o_terms, sv.at[3])]
+    own_out = pltpu.make_async_copy(i_osum.at[z], o_op.at[0], sv.at[5])
+    own_out.start()
     act_load = pltpu.make_async_copy(i_act, xb, sv.at[4])
 
     for k in (1, 2, 3):
@@ -668,8 +722,7 @@
     loads["hw"].wait()
 
     def stage1(q):
-        @pl.when(lax.rem(q, 2) == 0)
-        def _():
+        def multiply():
             q3 = q // 2
 
             def side(ref):
@@ -689,6 +742,11 @@
                             gw[q3, p, h, zz, j, :, 2 * half :] = dn[at : at + 16]
                 return 0
             lax.fori_loop(0, 4, one, 0)
+        if isinstance(q, int):
+            if q % 2 == 0:
+                multiply()
+        else:
+            pl.when(lax.rem(q, 2) == 0)(multiply)
         for b in range(2):
             copy1(q, b).start()
 
@@ -766,7 +824,7 @@
         return jnp.concatenate([smalls[i, row : row + 1, :] for i in range(4)], axis=1).astype(F32)
 
     def event_residual():
-        for name in ("gown", "res", "gates", "small"):
+        for name in ("gown", "res", "gates", "kept", "small"):
             loads[name].wait()
         for k in (1, 2, 3):
             c_g(k).wait_recv()
@@ -922,12 +980,16 @@
             c_o(k).wait_recv()
 
     stages = (stage1, stage2, stage3, stage4, stage5, stage6, stage7)
-    events = {3: event_residual, 4: event_share, 5: event_attention, 6: event_columns, 8: event_tokens,
-              9: event_terms, 10: event_sums, 11: event_last}
+    lead = 1
+    events = {2: event_residual, 3: event_share, 4: event_attention, 5: event_columns, 7: event_tokens,
+              8: event_terms, 9: event_sums, 10: event_last}
+
+    for q in range(lead):
+        stage1(q)
 
     def step(t, _):
         for i, stage in enumerate(stages):
-            q = t - i
+            q = t + lead if i == 0 else t + 1 - i
 
             @pl.when((q >= 0) & (q < nq))
             def _(stage=stage, q=q):
@@ -938,7 +1000,7 @@
                 event()
         return 0
 
-    lax.fori_loop(0, nq + len(stages) - 1, step, 0)
+    lax.fori_loop(0, nq + len(stages) - 2, step, 0)
 
     def left(q, _):
         for b in range(2):
@@ -964,22 +1026,22 @@
     for i in range(4):
         for one in (c_grc(i), c_qoc(i), c_poc(i)):
             one.wait_send()
-    for one in saves:
+    for one in saves + [own_out]:
         one.wait()
 
 
-def back(front_outs, tok, kept, cos_t, sin_t):
+def back(front_outs, tok, cos_t, sin_t):
     nq, wide = 6, 3 * HID // 2
     sem, vm = pltpu.SemaphoreType.DMA, pltpu.VMEM
     out = lambda shape, kind=BF: jax.ShapeDtypeStruct(shape, kind)
     piece = (4, 4, 16, wide)
     outs = (out((2, 6144, wide)), out((128, 1536), F32), out((8, 384, 320)), out((2, 4, 48, 1536)),
-            out((24, 384), F32), out((3, 128, 1536)))
+            out((24, 384), F32), out((4, 128, 1536)))
     block, quad, three = vm((2, 4, 128, 1536), BF), vm((4, 128, 1536), BF), vm((3, 128, 1536), BF)
     scratch = [
         block, block, vm((4, 1024, 512), BF), vm((4, 1024, 256), BF), vm((2, 4, 384, 64), BF),
         vm((2, 4, 128, 64), BF), vm((2, 4, 128, 64), BF), vm((2, 4, 384, 128), F32), vm((2, 4, 128, 192), BF),
-        vm((1536, 320), BF), vm((192, 1536), BF), vm((4, 32, 384), BF), vm((128, 1536), F32), vm((128, 16), F32),
+        vm((1536, 320), BF), vm((192, 1536), BF), vm((4, 32, 384), BF), vm((128, 1536), F32), vm((128, 16), F32), vm((128, 16), F32),
         vm((128, 1792), BF), vm((3, 128, 1792), BF),
         vm((3, 4, 2) + piece, BF), vm((nq, 2) + piece, BF), vm((2,) + piece, BF), vm((nq,) + piece, BF),
         vm((2,) + piece, BF), vm((nq,) + piece, BF), vm((wide // 128, 256, 128), F32), vm((2, 256, wide), BF),
@@ -994,40 +1056,62 @@
         sem((nq, 4)), sem((nq, 4)), sem((nq,)),
         n3, n3, n3, n3, n4, n4, one, one, n3, n3, n3, n3, n3, n3,
         n4, n4, n3, n3, n3, n3, n3, n3, n4, n4, n3, n3, one, one,
-        n3, n3, n3, n3, sem((16,)), sem((5,)),
+        n3, n3, n3, n3, sem((16,)), sem((6,)),
     ]
     vmem, any_ = pl.BlockSpec(memory_space=pltpu.VMEM), pl.BlockSpec(memory_space=pl.ANY)
     return pl.pallas_call(
         back_kernel,
         out_shape=outs,
-        in_specs=[any_] * 17 + [vmem] * 4,
+        in_specs=[any_] * 18 + [vmem] * 3,
         out_specs=[any_] * len(outs),
         scratch_shapes=scratch + sems,
         compiler_params=pltpu.CompilerParams(
             collective_id=2, has_side_effects=True, vmem_limit_bytes=62 * 1024 * 1024),
         name="back",
-    )(*front_outs, tok, kept, cos_t, sin_t)
-
-
-def widen_kernel(v, gu, dn):
+    )(*front_outs, tok, cos_t, sin_t)
+
+
+def finish_kernel(v, qkv, proj, res, parts, gu, dn, g_qkv, g_proj, out):
     half = HID // 2
     for c in range(2):
         gu[:, c * half : (c + 1) * half] = v[c, :, :half].astype(F32)
         gu[:, HID + c * half : HID + (c + 1) * half] = v[c, :, half : 2 * half].astype(F32)
         dn[:, c * half : (c + 1) * half] = v[c, :, 2 * half :].astype(F32)
-
-
-def widen(v):
-    rows, step = v.shape[1], 512
+    heads = range(qkv.shape[0])
+    g_qkv[...] = jnp.concatenate(
+        [qkv[h, :, lo:hi].astype(F32) for lo, hi in ((0, 192), (192, 256), (256, 320)) for h in heads], axis=1)
+    g_proj[...] = proj[...].astype(F32)
+
+    @pl.when(pl.program_id(0) == 0)
+    def _():
+        total = res[...]
+        for k in range(4):
+            total = total + parts[k].astype(F32)
+        out[...] = total.astype(BF)
+
+
+def finish(v, qkv, proj, res, parts):
+    steps, own, width = 24, proj.shape[0], proj.shape[1]
+    row, some = v.shape[1] // steps, own // steps
+    once = lambda n: (lambda i: (0,) * n)
     return pl.pallas_call(
-        widen_kernel,
-        out_shape=(jax.ShapeDtypeStruct((rows, 2 * HID), F32), jax.ShapeDtypeStruct((rows, HID), F32)),
-        grid=(rows // step,),
-        in_specs=[pl.BlockSpec((2, step, 3 * HID // 2), lambda i: (0, i, 0))],
-        out_specs=[pl.BlockSpec((step, 2 * HID), lambda i: (i, 0)), pl.BlockSpec((step, HID), lambda i: (i, 0))],
+        finish_kernel,
+        grid=(steps,),
+        out_shape=(
+            jax.ShapeDtypeStruct((v.shape[1], 2 * HID), F32), jax.ShapeDtypeStruct((v.shape[1], HID), F32),
+            jax.ShapeDtypeStruct((own, 2560), F32), jax.ShapeDtypeStruct((own, width), F32),
+            jax.ShapeDtypeStruct(res.shape, BF)),
+        in_specs=[
+            pl.BlockSpec((2, row, v.shape[2]), lambda i: (0, i, 0)),
+            pl.BlockSpec((8, some, 320), lambda i: (0, i, 0)), pl.BlockSpec((some, width), lambda i: (i, 0)),
+            pl.BlockSpec(res.shape, once(2)), pl.BlockSpec(parts.shape, once(3))],
+        out_specs=[
+            pl.BlockSpec((row, 2 * HID), lambda i: (i, 0)), pl.BlockSpec((row, HID), lambda i: (i, 0)),
+            pl.BlockSpec((some, 2560), lambda i: (i, 0)), pl.BlockSpec((some, width), lambda i: (i, 0)),
+            pl.BlockSpec(res.shape, once(2))],
         compiler_params=pltpu.CompilerParams(vmem_limit_bytes=40 * 1024 * 1024),
-        name="widen",
-    )(v)
+        name="finish",
+    )(v, qkv, proj, res, parts)
 
 
 def expert_grads_general(reps, grps, xs, dys, ggu, hw):
@@ -1268,53 +1352,23 @@
     priority,
     cotangent,
 ):
-    heads, half, own = KEY_VALUE_HEADS, HID // 2, attn_gain.shape[0]
-    qw, hw, q_all = QPK * HEAD_WIDTH, HEAD_WIDTH, QUERY_HEADS * HEAD_WIDTH
-    rep = lax.axis_index("rep")
-    core, chip = lax.rem(rep, 2), rep // 2
-    seq, width = tokens.shape
+    own, width = attn_gain.shape[0], tokens.shape[1]
     small = jnp.concatenate(
         [attn_gain[None], mlp_gain[None], jnp.zeros((14, own), BF), w_router.T], axis=0
     )
-    qkv_cols = jnp.concatenate(
-        [
-            lax.dynamic_slice_in_dim(query_key_value_weight, rep * qw, qw, 1),
-            lax.dynamic_slice_in_dim(query_key_value_weight, q_all + rep * hw, hw, 1),
-            lax.dynamic_slice_in_dim(query_key_value_weight, q_all + heads * hw + rep * hw, hw, 1),
-        ],
-        axis=1,
-    )
-    piece = own // 4
-    gu_piece = lax.dynamic_slice_in_dim(w_gate_up, chip * piece, piece, 0)
-    dn_piece = lax.dynamic_slice_in_dim(w_down, chip * piece, piece, 0)
-    both = jnp.concatenate(
-        [
-            lax.dynamic_slice_in_dim(gu_piece, core * half, half, 2),
-            lax.dynamic_slice_in_dim(gu_piece, HID + core * half, half, 2),
-            lax.dynamic_slice_in_dim(dn_piece, core * half, half, 2),
-        ],
-        axis=2,
-    )
-    wpiece = both.transpose(1, 0, 2).reshape(4, 4, piece, 3 * half)
-    chosen, kept = choices(expert_ids, priority)
-    masks = jnp.stack([chosen, kept]).astype(F32)
     prefix = jnp.broadcast_to(prefix_len.astype(F32), (8, 128))
-    cos, sin = rope_tables(seq)
-    cos_t, sin_t = jnp.tile(cos, (1, 4)), jnp.tile(jnp.concatenate([-sin, sin], axis=1), (1, 2))
-    parts = front(tokens, cotangent, wpiece, qkv_cols, attn_proj, small, masks, prefix, cos_t, sin_t)
-    residual, out_sum = parts[13], parts[16]
-    wide, grad_tokens, qkv_own, proj_own, terms, out_parts = back(parts, tokens, masks[1], cos_t, sin_t)
-    grad_gu, grad_dn = widen(wide)
-    out = lax.dynamic_index_in_dim(out_sum, lax.axis_index("grp"), 0, False).astype(F32)
-    output = (residual + out + jnp.sum(out_parts.astype(F32), axis=0)).astype(BF)
-    grad_qkv = jnp.concatenate(
-        [
-            jnp.concatenate([qkv_own[h, :, lo:hi] for h in range(heads)], axis=1)
-            for lo, hi in ((0, qw), (qw, qw + hw), (qw + hw, qw + 2 * hw))
-        ],
-        axis=1,
-    ).astype(F32)
-    grad_proj = proj_own.reshape(own, width).astype(F32)
+    half = HEAD_WIDTH // 2
+    inverse_freq = np.float32(10000.0) ** (-np.arange(half, dtype=np.float32) * np.float32(2.0 / HEAD_WIDTH))
+    angles = np.arange(tokens.shape[0], dtype=np.float32)[:, None] * inverse_freq[None, :]
+    cos_t = jnp.asarray(np.tile(np.cos(angles), (1, 4)), F32)
+    sin = np.sin(angles)
+    sin_t = jnp.asarray(np.tile(np.concatenate([-sin, sin], axis=1), (1, 2)), F32)
+    parts = front(
+        tokens, cotangent, w_gate_up, w_down, query_key_value_weight, attn_proj, small, expert_ids,
+        priority.reshape(expert_ids.shape), prefix, cos_t, sin_t)
+    wide, grad_tokens, qkv_own, proj_own, terms, out_parts = back(parts, tokens, cos_t, sin_t)
+    grad_gu, grad_dn, grad_qkv, grad_proj, output = finish(
+        wide, qkv_own, proj_own.reshape(own, width), parts[13], out_parts)
     return (
         output,
         grad_tokens,

time: 473 us -> 458 us (0.968)
  other arithmetic: 15.6 us -> 2.73 us
  local copies, waits for them, and re-layouts: 19.8 us -> 12.6 us
  Pallas kernels: 433 us -> 438 us
    convert_element_type x4 -> x0, other arithmetic: 6.06 us -> none  [the longest x1 2.41 us: shards(): grad_qkv = jnp.concatenate([jnp.concatenate([qkv_own[h, :, lo:hi] for h i...]
    unnamed x14 -> x13, local copies, waits for them, and re-layouts: 1.42 us -> 7.16 us
    dynamic_slice x3 -> x0, local copies, waits for them, and re-layouts: 5.36 us -> none  [the longest x1 3.21 us: shards(): lax.dynamic_slice_in_dim(gu_piece, core * half, half, 2)]
    pallas_call x2, Pallas kernels: 250 us -> 255 us  [the longest x1 229 us: back(): pl.pallas_call(back_kernel, out_shape=outs, in_specs=[any_] * 18 + [vmem]...]
    reduce_sum x3 -> x0, other arithmetic: 4.92 us -> none  [the longest x1 2.52 us: choices(): jnp.sum((rank_of[None, :, :] < rank_of[:, None, :]).astype(jnp.int32), ax...]
where the time goes in v6:
time: 458 us; the launch traced here: 455 us
  Pallas kernels  438 us (96%)
  local copies, waits for them, and re-layouts  12.6 us (3%)
    pallas_call x1, Pallas kernels, back(): pl.pallas_call(back_kernel, out_shape=outs, in_specs=[any_] * 18 + [vmem]...  229 us
    pallas_call x1, Pallas kernels, front(): pl.pallas_call(front_kernel, out_shape=outs, in_specs=[vmem, any_, any_,...  183 us
    pallas_call x1, Pallas kernels, finish(): pl.pallas_call(finish_kernel, grid=(steps,), out_shape=(jax.ShapeDtypeStr...  25.9 us

profile of v6, /device:TPU:0, one launch (start us, length us, event | category | flops | bytes accessed | tf_op | source)
XLA Modules:
  0.0 454.5 jit_solution(17154752466263427492)
XLA Ops:
  1.3 0.1 pad.2.clone
  1.4 0.7 broadcast_in_dim.14
  2.1 0.7 broadcast_in_dim.15
  2.7 0.5 broadcast.10
  3.3 1.3 reduce.7
  4.6 0.6 broadcast_in_dim.17.prefix
  5.2 1.4 pad_maximum_fusion.small
  6.6 0.7 reshape.31.prio
  7.3 1.4 copy.24.ids
  8.7 182.6 %front.1 = (bf16[2,4,128,1792]{3,2,1,0:T(8,128)(2,1)}, bf16[2,4,128,1536]{3,2,1,0:T(8,128)(2,1)}, bf16[4,1024,512]{2,1,0:T(8,128)(2,1)}, bf16[4,1024,256]{2,1,0:...) custom-call(bf16[128,1536]{1,0:T(8,128)(2,1)} %tok.3, ...), custom_call_target="tpu_custom_call" | custom-call | tf_op jit(solution)/shard_map/front/pallas_call | solution.py:569
  191.4 0.0 copy-start
  191.4 229.2 %back.1 = (bf16[2,6144,768]{2,1,0:T(8,128)(2,1)}, f32[128,1536]{1,0:T(8,128)}, bf16[8,384,320]{2,1,0:T(8,128)(2,1)}, bf16[2,4,48,1536]{3,2,1,0:T(8,128)(2,1)}, f...) custom-call(bf16[2,4,128,1792]{3,2,1,0:T(8,128)(2,1)} %get-tuple-element.38.i_x, ...), custom_call_target="tpu_custom_call" | custom-call | tf_op jit(solution)/shard_map/back/pallas_call | solution.py:1062
  420.6 1.4 slice_reduce_fusion
  422.0 1.3 slice_bitcast_fusion
  423.3 0.0 copy-done
  423.3 0.0 copy-start.1
  423.3 1.7 copy-done.1
  425.0 0.0 copy-start.2
  425.0 1.4 copy-done.2
  426.4 0.0 copy-start.3
  426.4 1.3 copy-done.3
  427.7 0.0 copy-start.4
  427.7 25.9 %finish.1 = (f32[6144,1024]{1,0:T(8,128)}, f32[6144,512]{1,0:T(8,128)}, f32[384,2560]{1,0:T(8,128)}, f32[384,1536]{1,0:T(8,128)}, bf16[128,1536]{1,0:T(8,128)(2,1)}) custom-call(bf16[2,6144,768]{2,1,0:T(8,128)(2,1)} %get-tuple-element.56.v, bf16[8,384,320]{2,1,0:T(8,128)(2,1)S(1)} %copy-done.1, bf16[384,1536]{1,0:T(8,128)(2,1)S(1)} %bitcast.7, ...), custom_call_target="tpu_custom_call" | custom-call | tf_op jit(solution)/shard_map/finish/pallas_call | solution.py:1097
  453.6 0.0 copy-done.4
  453.6 0.9 copy.27
  (1 shorter events, 0.0 us)
Async XLA Ops:
  191.4 232.0 %copy-start = (f32[128,1536]{1,0:T(8,128)S(1)}, f32[128,1536]{1,0:T(8,128)}, u32[]{:S(2)}) copy-start(f32[128,1536]{1,0:T(8,128)} %get-tuple-element.51.i_res.res) | copy-start | bytes 2359300
  423.3 1.7 copy-start.1
  425.0 1.4 copy-start.2
  426.4 1.3 copy-start.3
  427.7 25.9 %copy-start.4 = (f32[128,1536]{1,0:T(8,128)S(1)}, f32[128,1536]{1,0:T(8,128)}, u32[]{:S(2)}) copy-start(f32[128,1536]{1,0:T(8,128)} %get-tuple-element.79) | copy-start | bytes 2359300

commit v7 on v6

--- a/solution.py
+++ b/solution.py
@@ -71,16 +71,38 @@
     return v * cos + partner * sin
 
 
+def gradient_rows(q3, x, dy, ggu, hw, gw):
+    half = HID // 2
+
+    def side(ref):
+        return jnp.concatenate(
+            [ref[:, :, :, pl.ds(pl.multiple_of(zz * 384 + q3 * 128, 128), 128)].reshape(1024, 128)
+             for zz in range(4)], axis=1)
+    xs, ds = side(x), side(dy)
+
+    def one(j, _):
+        up = lax.dot_general(xs, ggu[j], (((0,), (0,)), ((), ())), preferred_element_type=F32).astype(BF)
+        dn = lax.dot_general(ds, hw[j], (((0,), (0,)), ((), ())), preferred_element_type=F32).astype(BF)
+        for zz in range(4):
+            for p in range(4):
+                for h in range(2):
+                    at = zz * 128 + p * 32 + h * 16
+                    gw[p, h, zz, j, :, : 2 * half] = up[at : at + 16]
+                    gw[p, h, zz, j, :, 2 * half :] = dn[at : at + 16]
+        return 0
+    lax.fori_loop(0, 4, one, 0)
+
+
 def front_kernel(tok, dy, w_gu, w_dn, qkv, proj, small, ids, prio, prefix, cos_t, sin_t,
                  o_x, o_dy, o_ggu, o_hw, o_act, o_q, o_k, o_v, o_probs, o_att, o_qkvw, o_projw,
-                 o_small, o_res, o_gates, o_kept, o_gsum, o_osum,
+                 o_small, o_res, o_gates, o_kept, o_gsum, o_osum, o_gw, o_r1,
                  smalls, qkvw, projw, projq, actp, pre, pr, qs, ks, vs, probs, att, part, sibr, sums, plr,
                  xall, dyall, wbuf, ggu, hw, gpart, ggp, gsib,
-                 gsum, res, gates, kept, qwin, wst, wcol, wpiece,
+                 gsum, res, gates, kept, qwin, wst, wcol, wpiece, gw, recv1,
                  s_small, r_small, s_qkv, r_qkv, s_pz, r_pz, s_pq, r_pq, s_wz, r_wz, s_wp, r_wp,
                  s_act, r_act, s_pre, r_pre, s_actc, r_actc, s_prec, r_prec, s_sib, r_sib, s_pl, r_pl,
                  s_x, r_x, s_xc, r_xc, s_y, r_y, s_yc, r_yc,
-                 s_gc, r_gc, s_oc, r_oc, sl):
+                 s_gc, r_gc, s_oc, r_oc, s1, r1, sl):
     y, x, c, z = place()
     half = HID // 2
 
@@ -132,10 +154,12 @@
         return remote(projq.at[0], projw.at[quarter(peers[i])], s_pq.at[0], r_pq.at[peers[i]], dpl[i])
 
     def c_act(i):
-        return remote(actp.at[c, p0], actp.at[c, p0], s_act.at[i], r_act.at[i], dpl[i])
+        blk = actp.at[c, p1 if i == 2 else p0]
+        return remote(blk, blk, s_act.at[i], r_act.at[i], d1 if i == 0 else d2)
 
     def c_pre(i):
-        return remote(pre.at[c, p0], pre.at[c, p0], s_pre.at[i], r_pre.at[i], dpl[i])
+        blk = pre.at[c, p1 if i == 2 else p0]
+        return remote(blk, blk, s_pre.at[i], r_pre.at[i], d1 if i == 0 else d2)
 
     def c_actc(i):
         p = (p0, p1, p2, p3)[i]
@@ -149,7 +173,7 @@
         return remote(part, sibr, s_sib, r_sib, dsib)
 
     def c_pl(i):
-        return remote(sums.at[i], plr.at[i], s_pl.at[i], r_pl.at[i], dpl[i])
+        return remote(sums.at[i], plr.at[i], s_pl.at[i], r_pl.at[i], d2 if i == 1 else d1)
 
     def chain(at, s, r, sc=None, rc=None):
         def hop(h, d, send):
@@ -215,6 +239,9 @@
         lambda b: qkvw.at[pl.ds(pl.multiple_of(b * 384, 384), 384)], s_qkv, r_qkv)
 
     opart, osib, osum = part, sibr, sums
+
+    def copy1(h, b):
+        return remote(gw.at[slot(1, b), h], recv1.at[h, b], s1.at[h, b], r1.at[h, b], d1)
     g_c = remote(gpart, gsib, s_gc, r_gc, dsib)
     o_c = remote(opart, osib, s_oc, r_oc, dsib)
 
@@ -238,10 +265,10 @@
         return pltpu.make_async_copy(src, qwin.at[:, pl.ds(at, width)], sl.at[n])
     mine = p0 * 96
     windows = [window(384 * p0 + 128 * c, 256, 0, 1), window(1536 + 128 * p0, 128, 256, 2),
-               window(2048 + 128 * p0, 128, 384, 24)]
+               window(2048 + 128 * p0, 128, 384, 5)]
     pieces = [pltpu.make_async_copy(
         ref.at[pl.ds(pl.multiple_of(mine, 96), 96), :, pl.ds(pl.multiple_of(off, half), half)],
-        wst.at[:, :, pl.ds(i * half, half)], sl.at[25 + i])
+        wst.at[:, :, pl.ds(i * half, half)], sl.at[6 + i])
         for i, (ref, off) in enumerate(((w_gu, c * half), (w_gu, HID + c * half), (w_dn, c * half)))]
     for one in local + windows + pieces:
         one.start()
@@ -270,7 +297,7 @@
     gain1 = jnp.concatenate([smalls[i, 0:1, :] for i in range(4)], axis=1).astype(F32)
     actp[c, p0] = (tok_f * inv1 * gain1).astype(BF)
     pre[c, p0] = prefix[...]
-    for i in range(3):
+    for i in range(2):
         c_act(i).start()
         c_pre(i).start()
     c_actc(0).start()
@@ -303,7 +330,7 @@
                 wcol[pl.ds(e, 96, stride=EXPERTS), :].astype(BF))
         return 0
     lax.fori_loop(0, 6, expert_rows, 0)
-    own_piece = pltpu.make_async_copy(wpiece.at[z], wbuf.at[:, rows(z, p0)], sl.at[28])
+    own_piece = pltpu.make_async_copy(wpiece.at[z], wbuf.at[:, rows(z, p0)], sl.at[30])
     own_piece.start()
     weights_a(0)
     q_recv(2)
@@ -311,9 +338,14 @@
     for i in range(3):
         c_act(i).wait_recv()
         c_pre(i).wait_recv()
+        if i == 0:
+            c_act(2).start()
+            c_pre(2).start()
         c_actc(i + 1).start()
         c_prec(i + 1).start()
     q_recv(3)
+    for k in (1, 3, 2):
+        c_wz(k).start()
     local[1].wait()
 
     row = lax.broadcasted_iota(jnp.int32, (128, 128), 0)
@@ -361,9 +393,6 @@
         def _(k=k):
             projw[quarter(p0)] = projq[k - 1]
 
-    for k in (1, 3, 2):
-        c_wz(k).start()
-
     @pl.when(z == p0)
     def _():
         own_proj.wait()
@@ -372,8 +401,6 @@
     def _():
         for i in range(3):
             c_pq_in(i).wait_recv()
-
-    weights_b(0)
 
     def to_sib(i, _):
         part[i] = jnp.dot(att[1 - c, i], projw[...], preferred_element_type=F32).astype(BF)
@@ -381,12 +408,18 @@
     lax.fori_loop(0, 4, to_sib, 0)
     c_sib().start()
     c_sib().wait_recv()
-    for i in range(3):
-        sums[i] = (jnp.dot(att[c, peers[i]], projw[...], preferred_element_type=F32)
-                   + sibr[peers[i]].astype(F32)).astype(BF)
+    def mixed(p):
+        return jnp.dot(att[c, p], projw[...], preferred_element_type=F32) + sibr[p].astype(F32)
+
+    for i in (2, 0):
+        sums[i] = mixed(peers[i]).astype(BF)
         c_pl(i).start()
-    residual = (tok_f + jnp.dot(att[c, p0], projw[...], preferred_element_type=F32) + sibr[p0].astype(F32))
-    for i in range(3):
+    to_second = mixed(p2)
+    residual = tok_f + mixed(p0)
+    c_pl(2).wait_recv()
+    sums[1] = (to_second + plr[2].astype(F32)).astype(BF)
+    c_pl(1).start()
+    for i in range(2):
         c_pl(i).wait_recv()
         residual = residual + plr[i].astype(F32)
     res[...] = residual
@@ -406,6 +439,7 @@
     xall[c, z, :, 1536:1664] = gate_hi
     xall[c, z, :, 1664:] = (wide_gates - gate_hi.astype(F32)).astype(BF)
     x_send(1)
+    weights_b(0)
     weights_a(1)
     weights_a(3)
     weights_b(1)
@@ -452,10 +486,15 @@
         ggu[j, at, half:] = (gh * silu).astype(BF)
         return 0
     lax.fori_loop(0, 8, expert, 0)
+
+    gradient_rows(0, xall, dyall, ggu, hw, gw)
+    for h in range(2):
+        for b in range(2):
+            copy1(h, b).start()
     saves = []
 
     def save(src, dst):
-        one = pltpu.make_async_copy(src, dst, sl.at[5 + len(saves)])
+        one = pltpu.make_async_copy(src, dst, sl.at[9 + len(saves)])
         one.start()
         saves.append(one)
     for src, dst in ((xall, o_x), (dyall, o_dy), (ggu, o_ggu), (hw, o_hw), (actp, o_act), (qs, o_q), (ks, o_k),
@@ -510,6 +549,11 @@
     o_c.wait_recv()
     own(False, osib, osum)
     save(osum, o_osum)
+    save(gw, o_gw)
+    for h in range(2):
+        for b in range(2):
+            copy1(h, b).wait()
+    save(recv1, o_r1)
 
     for k in (1, 2, 3):
         for one in (c_small(k), c_pz(k), c_wz(k)):
@@ -543,7 +587,7 @@
         out((2, 4, 128, 1536)), out((2, 4, 384, 64)), out((2, 4, 128, 64)), out((2, 4, 128, 64)),
         out((2, 4, 384, 128), F32), out((2, 4, 128, 192)), out((1536, 320)), out((192, 1536)),
         out((4, 32, 384)), out((128, 1536), F32), out((128, 16), F32), out((128, 16), F32), out((4, 128, 1792)),
-        out((4, 128, 1536)),
+        out((4, 128, 1536)), out((4, 2, 4, 4, 16, 768)), out((2, 2, 4, 4, 16, 768)),
     )
     block, quad = vm((2, 4, 128, 1536), BF), vm((4, 128, 1536), BF)
     three = vm((3, 128, 1536), BF)
@@ -557,13 +601,14 @@
         vm((4, 1024, 256), BF), quad_g, vm((2, 4, 128, 128), F32), quad_g,
         quad_g, vm((128, 1536), F32), vm((128, 16), F32), vm((128, 16), F32),
         vm((384, 512), BF), vm((96, 16, 768), BF), vm((1536, 128), F32), vm((4, 4, 96, 768), BF),
+        vm((4, 2, 4, 4, 16, 768), BF), vm((2, 2, 4, 4, 16, 768), BF),
     ]
     n3, n4, one = sem((3,)), sem((4,)), sem(())
     hops = [sem((2, 3)), sem((2, 3)), sem((3, 3)), sem((3, 3))]
     sems = [
         n3, n3, sem((2, 3)), sem((2, 3)), n3, n3, n3, n4, n3, n3, sem((4, 3)), sem((4, 3)),
         n3, n3, n3, n3, n4, n4, n4, n4, one, one, n3, n3,
-        *hops, *hops, one, one, one, one, sem((29,)),
+        *hops, *hops, one, one, one, one, sem((2, 2)), sem((2, 2)), sem((31,)),
     ]
     vmem, any_ = pl.BlockSpec(memory_space=pltpu.VMEM), pl.BlockSpec(memory_space=pl.ANY)
     return pl.pallas_call(
@@ -579,7 +624,7 @@
 
 
 def back_kernel(i_x, i_dy, i_ggu, i_hw, i_act, i_q, i_k, i_v, i_probs, i_att, i_qkvw, i_projw, i_small,
-                i_res, i_gates, i_kept, i_gsum, i_osum, tok, cos_t, sin_t,
+                i_res, i_gates, i_kept, i_gsum, i_osum, i_gw, i_r1, tok, cos_t, sin_t,
                 o_e, o_gtok, o_qg, o_pg, o_terms, o_op,
                 xb, dyb, ggu, hw, qs, ks, vs, probs, att, qkvw, projw, smalls, res, gates, kept, gown, grecv,
                 gw, recv1, send2, recv2, zs, zr, ib, agv,
@@ -608,6 +653,8 @@
     def load(name, src, dst):
         loads[name] = pltpu.make_async_copy(src, dst, ld.at[len(loads)])
         loads[name].start()
+    load("gw", i_gw, gw.at[0])
+    load("r1", i_r1, recv1.at[pl.ds(0, 2)])
     load("x", i_x.at[:, :, :, pl.ds(0, 1536)], xb)
     load("ggu", i_ggu, ggu)
     load("dy", i_dy, dyb)
@@ -659,7 +706,8 @@
         return remote(i_osum.at[zk[k]], o_op.at[k], s_o.at[k - 1], r_o.at[k - 1], dz[k])
 
     def c_gr(i):
-        return remote(gres.at[c, p0], gres.at[c, p0], s_gr.at[i], r_gr.at[i], dpl[i])
+        blk = gres.at[c, p1 if i == 2 else p0]
+        return remote(blk, blk, s_gr.at[i], r_gr.at[i], d1 if i == 0 else d2)
 
     def c_grc(i):
         p = (p0, p1, p2, p3)[i]
@@ -669,13 +717,14 @@
         return remote(dyb.at[0], sibr, s_sib, r_sib, dsib)
 
     def c_pl(i):
-        return remote(dyb.at[1, i], plr.at[i], s_pl.at[i], r_pl.at[i], dpl[i])
+        return remote(dyb.at[1, i], plr.at[i], s_pl.at[i], r_pl.at[i], d2 if i == 1 else d1)
 
     def c_qz(k):
         return remote(qgp.at[zk[k]], qz.at[k - 1], s_qz.at[k - 1], r_qz.at[k - 1], dz[k])
 
     def c_qo(i):
-        return remote(qgo, o_qg.at[p0 * 2 + c], s_qo.at[i], r_qo.at[i], dpl[i])
+        dst = o_qg.at[(p1 if i == 2 else p0) * 2 + c]
+        return remote(dst if i == 2 else qgo, dst, s_qo.at[i], r_qo.at[i], d1 if i == 0 else d2)
 
     def c_qoc(i):
         r = (p0, p1, p2, p3)[i] * 2 + c
@@ -688,7 +737,8 @@
         return remote(pgr.at[zk[k]], pq2.at[k - 1], s_p2.at[k - 1], r_p2.at[k - 1], dz[k])
 
     def c_po(i):
-        return remote(pgo, o_pg.at[c, p0], s_po.at[i], r_po.at[i], dpl[i])
+        dst = o_pg.at[c, p1 if i == 2 else p0]
+        return remote(dst if i == 2 else pgo, dst, s_po.at[i], r_po.at[i], d1 if i == 0 else d2)
 
     def c_poc(i):
         p = (p0, p1, p2, p3)[i]
@@ -716,43 +766,25 @@
 
     for k in (1, 2, 3):
         c_g(k).start()
+    loads["gw"].wait()
+    loads["r1"].wait()
     loads["x"].wait()
     loads["ggu"].wait()
     loads["dy"].wait()
     loads["hw"].wait()
 
     def stage1(q):
-        def multiply():
-            q3 = q // 2
-
-            def side(ref):
-                return jnp.concatenate(
-                    [ref[:, :, :, pl.ds(pl.multiple_of(zz * 384 + q3 * 128, 128), 128)].reshape(1024, 128)
-                     for zz in range(4)], axis=1)
-            xs, ds_ = side(xb), side(dyb)
-
-            def one(j, _):
-                up = lax.dot_general(xs, ggu[j], (((0,), (0,)), ((), ())), preferred_element_type=F32).astype(BF)
-                dn = lax.dot_general(ds_, hw[j], (((0,), (0,)), ((), ())), preferred_element_type=F32).astype(BF)
-                for zz in range(4):
-                    for p in range(4):
-                        for h in range(2):
-                            at = zz * 128 + p * 32 + h * 16
-                            gw[q3, p, h, zz, j, :, : 2 * half] = up[at : at + 16]
-                            gw[q3, p, h, zz, j, :, 2 * half :] = dn[at : at + 16]
-                return 0
-            lax.fori_loop(0, 4, one, 0)
-        if isinstance(q, int):
-            if q % 2 == 0:
-                multiply()
-        else:
-            pl.when(lax.rem(q, 2) == 0)(multiply)
+        @pl.when(lax.rem(q, 2) == 0)
+        def _():
+            gradient_rows(q // 2, xb, dyb, ggu, hw, gw.at[q // 2])
         for b in range(2):
             copy1(q, b).start()
 
     def stage2(q):
-        for b in range(2):
-            copy1(q, b).wait_recv()
+        @pl.when(q >= 2)
+        def _():
+            for b in range(2):
+                copy1(q, b).wait_recv()
 
         def one(zz, _):
             send2[lax.rem(q, 2), zz] = (gw[q // 2, p2, lax.rem(q, 2), zz].astype(F32)
@@ -847,13 +879,15 @@
         gr = dyb[c, z].astype(F32) + inv * (scaled - normed * jnp.mean(scaled * normed, axis=1, keepdims=True))
         gresf[...] = gr
         gres[c, p0] = gr.astype(BF)
-        for i in range(3):
+        for i in range(2):
             c_gr(i).start()
         c_grc(0).start()
 
     def event_share():
         for i in range(3):
             c_gr(i).wait_recv()
+            if i == 0:
+                c_gr(2).start()
             c_grc(i + 1).start()
         act_load.start()
 
@@ -913,18 +947,24 @@
         def part(p):
             return lax.dot_general(gproj[c, p], qkvw[...], (((1,), (1,)), ((), ())),
                                    preferred_element_type=F32) + sibr[p].astype(F32)
-        for i in range(3):
+        for i in (2, 0):
             dyb[1, i] = part(peers[i]).astype(BF)
             c_pl(i).start()
+        dyb[1, 1] = part(p2).astype(BF)
         gtok[...] = part(p0)
         for i in range(3):
             c_p1(i).wait_recv()
         for k in (1, 2, 3):
             c_p2(k).start()
 
+    def event_second():
+        c_pl(2).wait_recv()
+        dyb[1, 1] = (dyb[1, 1].astype(F32) + plr[2].astype(F32)).astype(BF)
+        c_pl(1).start()
+
     def event_tokens():
         ga = gtok[...]
-        for i in range(3):
+        for i in range(2):
             c_pl(i).wait_recv()
             ga = ga + plr[i].astype(F32)
         inv, normed = norm_one()
@@ -937,14 +977,14 @@
         for k in (1, 2, 3):
             c_qz(k).wait_recv()
         qgo[...] = (qgp[z].astype(F32) + qz[0].astype(F32) + qz[1].astype(F32) + qz[2].astype(F32)).astype(BF)
-        for i in range(3):
+        for i in range(2):
             c_qo(i).start()
         c_qoc(0).start()
         saves[1].start()
         for k in (1, 2, 3):
             c_p2(k).wait_recv()
         pgo[...] = (pgr[z].astype(F32) + pq2[0].astype(F32) + pq2[1].astype(F32) + pq2[2].astype(F32)).astype(BF)
-        for i in range(3):
+        for i in range(2):
             c_po(i).start()
         c_poc(0).start()
         saves[2].start()
@@ -958,8 +998,12 @@
         c_ts().start()
         for i in range(3):
             c_qo(i).wait_recv()
+            if i == 0:
+                c_qo(2).start()
             c_qoc(i + 1).start()
             c_po(i).wait_recv()
+            if i == 0:
+                c_po(2).start()
             c_poc(i + 1).start()
 
     def event_sums():
@@ -980,12 +1024,11 @@
             c_o(k).wait_recv()
 
     stages = (stage1, stage2, stage3, stage4, stage5, stage6, stage7)
-    lead = 1
-    events = {2: event_residual, 3: event_share, 4: event_attention, 5: event_columns, 7: event_tokens,
-              8: event_terms, 9: event_sums, 10: event_last}
-
-    for q in range(lead):
-        stage1(q)
+    lead = 4
+    for q in (2, 3):
+        stage1(jnp.int32(q))
+    events = {2: event_residual, 3: event_share, 4: event_attention, 5: event_columns, 6: event_second,
+              7: event_tokens, 8: event_terms, 9: event_sums, 10: event_last}
 
     def step(t, _):
         for i, stage in enumerate(stages):
@@ -1003,8 +1046,10 @@
     lax.fori_loop(0, nq + len(stages) - 2, step, 0)
 
     def left(q, _):
-        for b in range(2):
-            copy1(q, b).wait_send()
+        @pl.when(q >= 2)
+        def _():
+            for b in range(2):
+                copy1(q, b).wait_send()
         for i in range(1, 4):
             copys(q, i).wait_send()
         copya(q, 2).wait_send()
@@ -1056,13 +1101,13 @@
         sem((nq, 4)), sem((nq, 4)), sem((nq,)),
         n3, n3, n3, n3, n4, n4, one, one, n3, n3, n3, n3, n3, n3,
         n4, n4, n3, n3, n3, n3, n3, n3, n4, n4, n3, n3, one, one,
-        n3, n3, n3, n3, sem((16,)), sem((6,)),
+        n3, n3, n3, n3, sem((18,)), sem((6,)),
     ]
     vmem, any_ = pl.BlockSpec(memory_space=pltpu.VMEM), pl.BlockSpec(memory_space=pl.ANY)
     return pl.pallas_call(
         back_kernel,
         out_shape=outs,
-        in_specs=[any_] * 18 + [vmem] * 3,
+        in_specs=[any_] * 20 + [vmem] * 3,
         out_specs=[any_] * len(outs),
         scratch_shapes=scratch + sems,
         compiler_params=pltpu.CompilerParams(
@@ -1071,7 +1116,7 @@
     )(*front_outs, tok, cos_t, sin_t)
 
 
-def finish_kernel(v, qkv, proj, res, parts, gu, dn, g_qkv, g_proj, out):
+def finish_kernel(v, qkv, proj, res, parts, terms, gu, dn, g_qkv, g_proj, out, g_router):
     half = HID // 2
     for c in range(2):
         gu[:, c * half : (c + 1) * half] = v[c, :, :half].astype(F32)
@@ -1088,10 +1133,11 @@
         for k in range(4):
             total = total + parts[k].astype(F32)
         out[...] = total.astype(BF)
-
-
-def finish(v, qkv, proj, res, parts):
-    steps, own, width = 24, proj.shape[0], proj.shape[1]
+        g_router[...] = terms[8:, :]
+
+
+def finish(v, qkv, proj, res, parts, terms):
+    steps, own, width = 8, proj.shape[0], proj.shape[1]
     row, some = v.shape[1] // steps, own // steps
     once = lambda n: (lambda i: (0,) * n)
     return pl.pallas_call(
@@ -1100,18 +1146,19 @@
         out_shape=(
             jax.ShapeDtypeStruct((v.shape[1], 2 * HID), F32), jax.ShapeDtypeStruct((v.shape[1], HID), F32),
             jax.ShapeDtypeStruct((own, 2560), F32), jax.ShapeDtypeStruct((own, width), F32),
-            jax.ShapeDtypeStruct(res.shape, BF)),
+            jax.ShapeDtypeStruct(res.shape, BF), jax.ShapeDtypeStruct((EXPERTS, own), F32)),
         in_specs=[
             pl.BlockSpec((2, row, v.shape[2]), lambda i: (0, i, 0)),
             pl.BlockSpec((8, some, 320), lambda i: (0, i, 0)), pl.BlockSpec((some, width), lambda i: (i, 0)),
-            pl.BlockSpec(res.shape, once(2)), pl.BlockSpec(parts.shape, once(3))],
+            pl.BlockSpec(res.shape, once(2)), pl.BlockSpec(parts.shape, once(3)),
+            pl.BlockSpec(terms.shape, once(2))],
         out_specs=[
             pl.BlockSpec((row, 2 * HID), lambda i: (i, 0)), pl.BlockSpec((row, HID), lambda i: (i, 0)),
             pl.BlockSpec((some, 2560), lambda i: (i, 0)), pl.BlockSpec((some, width), lambda i: (i, 0)),
-            pl.BlockSpec(res.shape, once(2))],
-        compiler_params=pltpu.CompilerParams(vmem_limit_bytes=40 * 1024 * 1024),
+            pl.BlockSpec(res.shape, once(2)), pl.BlockSpec((EXPERTS, own), once(2))],
+        compiler_params=pltpu.CompilerParams(vmem_limit_bytes=62 * 1024 * 1024),
         name="finish",
-    )(v, qkv, proj, res, parts)
+    )(v, qkv, proj, res, parts, terms)
 
 
 def expert_grads_general(reps, grps, xs, dys, ggu, hw):
@@ -1367,8 +1414,8 @@
         tokens, cotangent, w_gate_up, w_down, query_key_value_weight, attn_proj, small, expert_ids,
         priority.reshape(expert_ids.shape), prefix, cos_t, sin_t)
     wide, grad_tokens, qkv_own, proj_own, terms, out_parts = back(parts, tokens, cos_t, sin_t)
-    grad_gu, grad_dn, grad_qkv, grad_proj, output = finish(
-        wide, qkv_own, proj_own.reshape(own, width), parts[13], out_parts)
+    grad_gu, grad_dn, grad_qkv, grad_proj, output, grad_router = finish(
+        wide, qkv_own, proj_own.reshape(own, width), parts[13], out_parts, terms)
     return (
         output,
         grad_tokens,
@@ -1376,7 +1423,7 @@
         grad_qkv,
         grad_proj,
         terms[1],
-        terms[8:].T,
+        grad_router.T,
         grad_gu.reshape(own, EXPERTS, 2 * HID),
         grad_dn.reshape(own, EXPERTS, HID),
     )

time: 458 us -> 435 us (0.950)
  Pallas kernels: 438 us -> 423 us
  local copies, waits for them, and re-layouts: 12.6 us -> 6.95 us
    pallas_call x1, Pallas kernels: 229 us -> 206 us  [back(): pl.pallas_call(back_kernel, out_shape=outs, in_specs=[any_] * 20 + [vmem]...]
    pallas_call x1, Pallas kernels: 183 us -> 193 us  [front(): pl.pallas_call(front_kernel, out_shape=outs, in_specs=[vmem, any_, any_,...]
where the time goes in v7:
time: 435 us; the launch traced here: 434 us
  Pallas kernels  423 us (97%)
  local copies, waits for them, and re-layouts  6.95 us (2%)
    pallas_call x1, Pallas kernels, back(): pl.pallas_call(back_kernel, out_shape=outs, in_specs=[any_] * 20 + [vmem]...  206 us
    pallas_call x1, Pallas kernels, front(): pl.pallas_call(front_kernel, out_shape=outs, in_specs=[vmem, any_, any_,...  193 us
    pallas_call x1, Pallas kernels, finish(): pl.pallas_call(finish_kernel, grid=(steps,), out_shape=(jax.ShapeDtypeStr...  24.3 us

profile of v7, /device:TPU:0, one launch (start us, length us, event | category | flops | bytes accessed | tf_op | source)
XLA Modules:
  0.0 434.4 jit_solution(11293735169953378376)
XLA Ops:
  0.6 0.5 broadcast.10
  1.2 1.3 reduce.7
  2.5 0.7 reshape.31.prio
  3.2 1.4 copy.24.ids
  4.6 0.7 broadcast_in_dim.14
  5.3 0.7 broadcast_in_dim.15
  6.0 0.1 pad.2.clone
  6.1 1.4 pad_maximum_fusion.small
  8.1 0.6 broadcast_in_dim.17.prefix
  8.7 192.8 %front.1 = (bf16[2,4,128,1792]{3,2,1,0:T(8,128)(2,1)}, bf16[2,4,128,1536]{3,2,1,0:T(8,128)(2,1)}, bf16[4,1024,512]{2,1,0:T(8,128)(2,1)}, bf16[4,1024,256]{2,1,0:...) custom-call(bf16[128,1536]{1,0:T(8,128)(2,1)} %tok.3, ...), custom_call_target="tpu_custom_call" | custom-call | tf_op jit(solution)/shard_map/front/pallas_call | solution.py:614
  201.6 206.2 %back.1 = (bf16[2,6144,768]{2,1,0:T(8,128)(2,1)}, f32[128,1536]{1,0:T(8,128)}, bf16[8,384,320]{2,1,0:T(8,128)(2,1)}, bf16[2,4,48,1536]{3,2,1,0:T(8,128)(2,1)}, f...) custom-call(bf16[2,4,128,1792]{3,2,1,0:T(8,128)(2,1)} %get-tuple-element.41.i_x, ...), custom_call_target="tpu_custom_call" | custom-call | tf_op jit(solution)/shard_map/back/pallas_call | solution.py:1107
  407.8 0.0 copy-start
  407.8 24.3 %finish.1 = (f32[6144,1024]{1,0:T(8,128)}, f32[6144,512]{1,0:T(8,128)}, f32[384,2560]{1,0:T(8,128)}, f32[384,1536]{1,0:T(8,128)}, bf16[128,1536]{1,0:T(8,128)(2,1)}, /*index=5*/f32[16,384]{1,0:T(8,128)}) custom-call(bf16[2,6144,768]{2,1,0:T(8,128)(2,1)} %get-tuple-element.61.v, bf16[8,384,320]{2,1,0:T(8,128)(2,1)} %get-tuple-element.62.qkv, ...), custom_call_target="tpu_custom_call" | custom-call | tf_op jit(solution)/shard_map/finish/pallas_call | solution.py:1143
  432.2 1.4 slice_reduce_fusion
  433.6 0.0 copy-done
  433.6 0.9 copy.27
  (1 shorter events, 0.0 us)
Async XLA Ops:
  407.8 25.7 %copy-start = (f32[128,1536]{1,0:T(8,128)S(1)}, f32[128,1536]{1,0:T(8,128)}, u32[]{:S(2)}) copy-start(f32[128,1536]{1,0:T(8,128)} %get-tuple-element.85) | copy-start | bytes 2359300

commit v8 on v7

--- a/solution.py
+++ b/solution.py
@@ -291,8 +291,6 @@
     for k in (1, 2, 3):
         c_small(k).wait_recv()
     q_send(1)
-    for k in (1, 2, 3):
-        c_pz(k).start()
     local[0].wait()
     gain1 = jnp.concatenate([smalls[i, 0:1, :] for i in range(4)], axis=1).astype(F32)
     actp[c, p0] = (tok_f * inv1 * gain1).astype(BF)
@@ -335,6 +333,8 @@
     weights_a(0)
     q_recv(2)
     q_send(3)
+    for k in (1, 2, 3):
+        c_pz(k).start()
     for i in range(3):
         c_act(i).wait_recv()
         c_pre(i).wait_recv()
@@ -344,8 +344,6 @@
         c_actc(i + 1).start()
         c_prec(i + 1).start()
     q_recv(3)
-    for k in (1, 3, 2):
-        c_wz(k).start()
     local[1].wait()
 
     row = lax.broadcasted_iota(jnp.int32, (128, 128), 0)
@@ -377,6 +375,8 @@
         lax.fori_loop(0, 4, one, 0)
 
     attention(c)
+    for k in (1, 3, 2):
+        c_wz(k).start()
     for i in range(4):
         c_actc(i).wait_recv()
         c_prec(i).wait_recv()
@@ -439,23 +439,23 @@
     xall[c, z, :, 1536:1664] = gate_hi
     xall[c, z, :, 1664:] = (wide_gates - gate_hi.astype(F32)).astype(BF)
     x_send(1)
+    y_send(1)
     weights_b(0)
     weights_a(1)
     weights_a(3)
     weights_b(1)
     x_recv(1)
     x_send(2)
+    y_recv(1)
+    y_send(2)
     weights_b(3)
     weights_a(2)
     x_recv(2)
     x_send(3)
-    y_send(1)
+    y_recv(2)
+    y_send(3)
     weights_b(2)
     x_recv(3)
-    y_recv(1)
-    y_send(2)
-    y_recv(2)
-    y_send(3)
     y_recv(3)
     own_piece.wait()
     for k in range(4):
@@ -884,6 +884,8 @@
         c_grc(0).start()
 
     def event_share():
+        for k in (1, 2, 3):
+            c_o(k).start()
         for i in range(3):
             c_gr(i).wait_recv()
             if i == 0:
@@ -988,8 +990,6 @@
             c_po(i).start()
         c_poc(0).start()
         saves[2].start()
-        for k in (1, 2, 3):
-            c_o(k).start()
 
     def event_terms():
         for k in (1, 2, 3):
@@ -1027,12 +1027,14 @@
     lead = 4
     for q in (2, 3):
         stage1(jnp.int32(q))
+    for q in range(1):
+        stage2(jnp.int32(q))
     events = {2: event_residual, 3: event_share, 4: event_attention, 5: event_columns, 6: event_second,
               7: event_tokens, 8: event_terms, 9: event_sums, 10: event_last}
 
     def step(t, _):
         for i, stage in enumerate(stages):
-            q = t + lead if i == 0 else t + 1 - i
+            q = t + lead if i == 0 else t + 2 - i
 
             @pl.when((q >= 0) & (q < nq))
             def _(stage=stage, q=q):

time: 435 us -> 420 us (0.966)
  Pallas kernels: 423 us -> 409 us
    pallas_call x1, Pallas kernels: 193 us -> 179 us  [front(): pl.pallas_call(front_kernel, out_shape=outs, in_specs=[vmem, any_, any_,...]
where the time goes in v8:
time: 420 us
  Pallas kernels  409 us (97%)
  local copies, waits for them, and re-layouts  6.95 us (2%)
    pallas_call x1, Pallas kernels, back(): pl.pallas_call(back_kernel, out_shape=outs, in_specs=[any_] * 20 + [vmem]...  205 us
    pallas_call x1, Pallas kernels, front(): pl.pallas_call(front_kernel, out_shape=outs, in_specs=[vmem, any_, any_,...  179 us
    pallas_call x1, Pallas kernels, finish(): pl.pallas_call(finish_kernel, grid=(steps,), out_shape=(jax.ShapeDtypeStr...  24.3 us

profile of v8, /device:TPU:0, one launch (start us, length us, event | category | flops | bytes accessed | tf_op | source)
XLA Modules:
  0.0 419.5 jit_solution(5832522305576199808)
XLA Ops:
  0.6 0.5 broadcast.10
  1.2 1.3 reduce.7
  2.5 0.7 reshape.31.prio
  3.2 1.4 copy.24.ids
  4.6 0.7 broadcast_in_dim.14
  5.3 0.7 broadcast_in_dim.15
  6.0 0.1 pad.2.clone
  6.1 1.4 pad_maximum_fusion.small
  8.1 0.6 broadcast_in_dim.17.prefix
  8.7 179.3 %front.1 = (bf16[2,4,128,1792]{3,2,1,0:T(8,128)(2,1)}, bf16[2,4,128,1536]{3,2,1,0:T(8,128)(2,1)}, bf16[4,1024,512]{2,1,0:T(8,128)(2,1)}, bf16[4,1024,256]{2,1,0:...) custom-call(bf16[128,1536]{1,0:T(8,128)(2,1)} %tok.3, ...), custom_call_target="tpu_custom_call" | custom-call | tf_op jit(solution)/shard_map/front/pallas_call | solution.py:614
  188.0 204.9 %back.1 = (bf16[2,6144,768]{2,1,0:T(8,128)(2,1)}, f32[128,1536]{1,0:T(8,128)}, bf16[8,384,320]{2,1,0:T(8,128)(2,1)}, bf16[2,4,48,1536]{3,2,1,0:T(8,128)(2,1)}, f...) custom-call(bf16[2,4,128,1792]{3,2,1,0:T(8,128)(2,1)} %get-tuple-element.41.i_x, ...), custom_call_target="tpu_custom_call" | custom-call | tf_op jit(solution)/shard_map/back/pallas_call | solution.py:1109
  392.9 0.0 copy-start
  392.9 24.3 %finish.1 = (f32[6144,1024]{1,0:T(8,128)}, f32[6144,512]{1,0:T(8,128)}, f32[384,2560]{1,0:T(8,128)}, f32[384,1536]{1,0:T(8,128)}, bf16[128,1536]{1,0:T(8,128)(2,1)}, /*index=5*/f32[16,384]{1,0:T(8,128)}) custom-call(bf16[2,6144,768]{2,1,0:T(8,128)(2,1)} %get-tuple-element.61.v, bf16[8,384,320]{2,1,0:T(8,128)(2,1)} %get-tuple-element.62.qkv, ...), custom_call_target="tpu_custom_call" | custom-call | tf_op jit(solution)/shard_map/finish/pallas_call | solution.py:1145
  417.3 1.4 slice_reduce_fusion
  418.6 0.0 copy-done
  418.6 0.9 copy.27
  (1 shorter events, 0.0 us)
Async XLA Ops:
  392.9 25.7 %copy-start = (f32[128,1536]{1,0:T(8,128)S(1)}, f32[128,1536]{1,0:T(8,128)}, u32[]{:S(2)}) copy-start(f32[128,1536]{1,0:T(8,128)} %get-tuple-element.85) | copy-start | bytes 2359300

commit v9 on v8

--- a/solution.py
+++ b/solution.py
@@ -93,12 +93,12 @@
     lax.fori_loop(0, 4, one, 0)
 
 
-def front_kernel(tok, dy, w_gu, w_dn, qkv, proj, small, ids, prio, prefix, cos_t, sin_t,
+def front_kernel(tok, dy, w_gu, w_dn, qkv, proj, small, ids_t, prio, prefix, cos_t, sin_t,
                  o_x, o_dy, o_ggu, o_hw, o_act, o_q, o_k, o_v, o_probs, o_att, o_qkvw, o_projw,
                  o_small, o_res, o_gates, o_kept, o_gsum, o_osum, o_gw, o_r1,
                  smalls, qkvw, projw, projq, actp, pre, pr, qs, ks, vs, probs, att, part, sibr, sums, plr,
                  xall, dyall, wbuf, ggu, hw, gpart, ggp, gsib,
-                 gsum, res, gates, kept, qwin, wst, wcol, wpiece, gw, recv1,
+                 gsum, res, gates, kept, qwin, wst, wcol, wpiece, gw,
                  s_small, r_small, s_qkv, r_qkv, s_pz, r_pz, s_pq, r_pq, s_wz, r_wz, s_wp, r_wp,
                  s_act, r_act, s_pre, r_pre, s_actc, r_actc, s_prec, r_prec, s_sib, r_sib, s_pl, r_pl,
                  s_x, r_x, s_xc, r_xc, s_y, r_y, s_yc, r_yc,
@@ -241,7 +241,7 @@
     opart, osib, osum = part, sibr, sums
 
     def copy1(h, b):
-        return remote(gw.at[slot(1, b), h], recv1.at[h, b], s1.at[h, b], r1.at[h, b], d1)
+        return remote(gw.at[slot(1, b), h], o_r1.at[h, b], s1.at[h, b], r1.at[h, b], d1)
     g_c = remote(gpart, gsib, s_gc, r_gc, dsib)
     o_c = remote(opart, osib, s_oc, r_oc, dsib)
 
@@ -249,10 +249,13 @@
         if k:
             c_wz(k).wait_recv()
         c_wp(k, 0).start()
+        if k == 0:
+            c_wp(0, 1).start()
 
     def weights_b(k):
         c_wp(k, 0).wait_recv()
-        c_wp(k, 1).start()
+        if k:
+            c_wp(k, 1).start()
         c_wp(k, 2).start()
 
     for k in (1, 2, 3):
@@ -303,8 +306,9 @@
     chosen_f = jnp.zeros((128, 128), F32)
     rank_of = jnp.zeros((128, 128), F32)
     lane_e = lax.broadcasted_iota(jnp.int32, (128, 128), 1)
+    ids = ids_t[...].astype(F32).T
     for k in range(8):
-        hit = ids[:, k : k + 1] == lane_e
+        hit = ids[:, k : k + 1] == lane_e.astype(F32)
         chosen_f = jnp.where(hit, 1.0, chosen_f)
         rank_of = jnp.where(hit, prio[:, k : k + 1].astype(F32), rank_of)
     rank_of = jnp.where(chosen_f > 0.0, rank_of, 65536.0)
@@ -344,6 +348,7 @@
         c_actc(i + 1).start()
         c_prec(i + 1).start()
     q_recv(3)
+    weights_b(0)
     local[1].wait()
 
     row = lax.broadcasted_iota(jnp.int32, (128, 128), 0)
@@ -433,28 +438,27 @@
     ge = jnp.where(chosen, jnp.exp(jnp.where(chosen, logits - top, 0.0)), 0.0)
     gt = ge / jnp.sum(ge, axis=1, keepdims=True)
     gates[...] = gt
-    wide_gates = jnp.concatenate([gt * kept[...], jnp.zeros((128, 112), F32)], axis=1)
-    gate_hi = wide_gates.astype(BF)
+    kept_gates = gt * kept[...]
+    gate_hi = kept_gates.astype(BF)
+    gate_lo = (kept_gates - gate_hi.astype(F32)).astype(BF)
     xall[c, z, :, :1536] = act2
-    xall[c, z, :, 1536:1664] = gate_hi
-    xall[c, z, :, 1664:] = (wide_gates - gate_hi.astype(F32)).astype(BF)
+    xall[c, z, :, 1536:] = jnp.concatenate([gate_hi, gate_lo, jnp.zeros((128, 96), BF)], axis=1)
     x_send(1)
     y_send(1)
-    weights_b(0)
     weights_a(1)
     weights_a(3)
     weights_b(1)
+    weights_b(3)
     x_recv(1)
     x_send(2)
+    weights_a(2)
     y_recv(1)
     y_send(2)
-    weights_b(3)
-    weights_a(2)
     x_recv(2)
     x_send(3)
+    weights_b(2)
     y_recv(2)
     y_send(3)
-    weights_b(2)
     x_recv(3)
     y_recv(3)
     own_piece.wait()
@@ -472,8 +476,8 @@
         gu = jnp.dot(xall[t, :, :, :1536].reshape(512, 1536), wbuf[j, :, : 2 * half], preferred_element_type=F32)
         bk = jnp.dot(dyall[t].reshape(512, 1536), wbuf[j, :, 2 * half :], preferred_element_type=F32)
         mine = lane == z * 4 + j
-        both = (xall[t, :, :, 1536:1664].astype(F32) + xall[t, :, :, 1664:].astype(F32)).reshape(512, 128)
-        w = jnp.sum(jnp.where(mine, both, 0.0), axis=1, keepdims=True)
+        both = xall[t, :, :, 1536:].astype(F32).reshape(512, 128)
+        w = jnp.sum(jnp.where(mine | (lane == EXPERTS + z * 4 + j), both, 0.0), axis=1, keepdims=True)
         g, u = gu[:, :half], gu[:, half:]
         sg = 1.0 / (1.0 + jnp.exp(-g))
         silu = g * sg
@@ -527,12 +531,13 @@
         lax.fori_loop(0, 6, one, 0)
 
     def put_gate_grads(dst, v):
-        hi = v.astype(BF)
-        dst[:, :, 1536:1664] = hi
-        dst[:, :, 1664:] = (v - hi.astype(F32)).astype(BF)
+        hi = v.astype(BF).astype(F32)
+        lo = pltpu.roll((v - hi).reshape(512, 128), EXPERTS, 1)
+        dst[:, :, 1536:] = jnp.where(lane < EXPERTS, hi.reshape(512, 128), lo).astype(BF).reshape(4, 128, 128)
 
     def gate_grads(v):
-        return v[..., 1536:1664].astype(F32) + v[..., 1664:].astype(F32)
+        both = v[..., 1536:].astype(F32).reshape(512, 128)
+        return jnp.where(lane < EXPERTS, both + pltpu.roll(both, 128 - EXPERTS, 1), 0.0).reshape(4, 128, 128)
 
     c_sib().wait_send()
     for i in range(3):
@@ -553,7 +558,6 @@
     for h in range(2):
         for b in range(2):
             copy1(h, b).wait()
-    save(recv1, o_r1)
 
     for k in (1, 2, 3):
         for one in (c_small(k), c_pz(k), c_wz(k)):
@@ -583,25 +587,25 @@
     sem, vm = pltpu.SemaphoreType.DMA, pltpu.VMEM
     out = lambda shape, kind=BF: jax.ShapeDtypeStruct(shape, kind)
     outs = (
-        out((2, 4, 128, 1792)), out((2, 4, 128, 1536)), out((4, 1024, 512)), out((4, 1024, 256)),
+        out((2, 4, 128, 1664)), out((2, 4, 128, 1536)), out((4, 1024, 512)), out((4, 1024, 256)),
         out((2, 4, 128, 1536)), out((2, 4, 384, 64)), out((2, 4, 128, 64)), out((2, 4, 128, 64)),
         out((2, 4, 384, 128), F32), out((2, 4, 128, 192)), out((1536, 320)), out((192, 1536)),
-        out((4, 32, 384)), out((128, 1536), F32), out((128, 16), F32), out((128, 16), F32), out((4, 128, 1792)),
+        out((4, 32, 384)), out((128, 1536), F32), out((128, 16), F32), out((128, 16), F32), out((4, 128, 1664)),
         out((4, 128, 1536)), out((4, 2, 4, 4, 16, 768)), out((2, 2, 4, 4, 16, 768)),
     )
     block, quad = vm((2, 4, 128, 1536), BF), vm((4, 128, 1536), BF)
     three = vm((3, 128, 1536), BF)
-    quad_g = vm((4, 128, 1792), BF)
+    quad_g = vm((4, 128, 1664), BF)
     scratch = [
         vm((4, 32, 384), BF), vm((1536, 320), BF), vm((192, 1536), BF), vm((3, 48, 1536), BF),
         block, vm((2, 4, 8, 128), F32),
         vm((4, 128, 320), F32), vm((2, 4, 384, 64), BF), vm((2, 4, 128, 64), BF), vm((2, 4, 128, 64), BF),
         vm((2, 4, 384, 128), F32), vm((2, 4, 128, 192), BF), quad, quad, quad, three,
-        vm((2, 4, 128, 1792), BF), block, vm((4, 1536, 768), BF), vm((4, 1024, 512), BF),
+        vm((2, 4, 128, 1664), BF), block, vm((4, 1536, 768), BF), vm((4, 1024, 512), BF),
         vm((4, 1024, 256), BF), quad_g, vm((2, 4, 128, 128), F32), quad_g,
         quad_g, vm((128, 1536), F32), vm((128, 16), F32), vm((128, 16), F32),
         vm((384, 512), BF), vm((96, 16, 768), BF), vm((1536, 128), F32), vm((4, 4, 96, 768), BF),
-        vm((4, 2, 4, 4, 16, 768), BF), vm((2, 2, 4, 4, 16, 768), BF),
+        vm((4, 2, 4, 4, 16, 768), BF),
     ]
     n3, n4, one = sem((3,)), sem((4,)), sem(())
     hops = [sem((2, 3)), sem((2, 3)), sem((3, 3)), sem((3, 3))]
@@ -860,10 +864,9 @@
             loads[name].wait()
         for k in (1, 2, 3):
             c_g(k).wait_recv()
-        tail = slice(1536, 1664), slice(1664, 1792)
 
         def gate_part(v):
-            return (v[:, tail[0]].astype(F32) + v[:, tail[1]].astype(F32))[:, :EXPERTS]
+            return v[:, 1536 : 1536 + EXPERTS].astype(F32) + v[:, 1536 + EXPERTS : 1536 + 2 * EXPERTS].astype(F32)
         gg = (gate_part(gown[...]) + gate_part(grecv[0]) + gate_part(grecv[1]) + gate_part(grecv[2])) * kept[...]
         gt = gates[...]
         gl = (gt * (gg - jnp.sum(gt * gg, axis=1, keepdims=True))).astype(BF)
@@ -963,19 +966,6 @@
         c_pl(2).wait_recv()
         dyb[1, 1] = (dyb[1, 1].astype(F32) + plr[2].astype(F32)).astype(BF)
         c_pl(1).start()
-
-    def event_tokens():
-        ga = gtok[...]
-        for i in range(2):
-            c_pl(i).wait_recv()
-            ga = ga + plr[i].astype(F32)
-        inv, normed = norm_one()
-        terms[0:1, :] = jnp.sum(ga * normed, axis=0, keepdims=True)
-        scaled = ga * gain(0)
-        gtok[...] = gresf[...] + inv * (scaled - normed * jnp.mean(scaled * normed, axis=1, keepdims=True))
-        saves[0].start()
-        for k in (1, 2, 3):
-            c_tz(k).start()
         for k in (1, 2, 3):
             c_qz(k).wait_recv()
         qgo[...] = (qgp[z].astype(F32) + qz[0].astype(F32) + qz[1].astype(F32) + qz[2].astype(F32)).astype(BF)
@@ -991,22 +981,33 @@
         c_poc(0).start()
         saves[2].start()
 
+    def event_tokens():
+        ga = gtok[...]
+        for i in range(2):
+            c_pl(i).wait_recv()
+            ga = ga + plr[i].astype(F32)
+        inv, normed = norm_one()
+        terms[0:1, :] = jnp.sum(ga * normed, axis=0, keepdims=True)
+        scaled = ga * gain(0)
+        gtok[...] = gresf[...] + inv * (scaled - normed * jnp.mean(scaled * normed, axis=1, keepdims=True))
+        saves[0].start()
+        for k in (1, 2, 3):
+            c_tz(k).start()
+        for copy, over in ((c_qo, c_qoc), (c_po, c_poc)):
+            copy(0).wait_recv()
+            copy(2).start()
+            over(1).start()
+            copy(1).wait_recv()
+            over(2).start()
+
     def event_terms():
         for k in (1, 2, 3):
             c_tz(k).wait_recv()
         tz[0] = terms[:, lanes_of(z)] + tz[1] + tz[2] + tz[3]
         c_ts().start()
-        for i in range(3):
-            c_qo(i).wait_recv()
-            if i == 0:
-                c_qo(2).start()
-            c_qoc(i + 1).start()
-            c_po(i).wait_recv()
-            if i == 0:
-                c_po(2).start()
-            c_poc(i + 1).start()
-
-    def event_sums():
+        for copy, over in ((c_qo, c_qoc), (c_po, c_poc)):
+            copy(2).wait_recv()
+            over(3).start()
         c_ts().wait()
         tpl[p0] = tz[0] + tsib[...]
         for i in range(3):
@@ -1030,7 +1031,7 @@
     for q in range(1):
         stage2(jnp.int32(q))
     events = {2: event_residual, 3: event_share, 4: event_attention, 5: event_columns, 6: event_second,
-              7: event_tokens, 8: event_terms, 9: event_sums, 10: event_last}
+              7: event_tokens, 8: event_terms, 9: event_last}
 
     def step(t, _):
         for i, stage in enumerate(stages):
@@ -1089,7 +1090,7 @@
         block, block, vm((4, 1024, 512), BF), vm((4, 1024, 256), BF), vm((2, 4, 384, 64), BF),
         vm((2, 4, 128, 64), BF), vm((2, 4, 128, 64), BF), vm((2, 4, 384, 128), F32), vm((2, 4, 128, 192), BF),
         vm((1536, 320), BF), vm((192, 1536), BF), vm((4, 32, 384), BF), vm((128, 1536), F32), vm((128, 16), F32), vm((128, 16), F32),
-        vm((128, 1792), BF), vm((3, 128, 1792), BF),
+        vm((128, 1664), BF), vm((3, 128, 1664), BF),
         vm((3, 4, 2) + piece, BF), vm((nq, 2) + piece, BF), vm((2,) + piece, BF), vm((nq,) + piece, BF),
         vm((2,) + piece, BF), vm((nq,) + piece, BF), vm((wide // 128, 256, 128), F32), vm((2, 256, wide), BF),
         block, vm((128, 1536), F32), vm((2, 4, 128, 320), BF), quad, three, vm((4, 384, 320), BF),
@@ -1413,7 +1414,7 @@
     sin = np.sin(angles)
     sin_t = jnp.asarray(np.tile(np.concatenate([-sin, sin], axis=1), (1, 2)), F32)
     parts = front(
-        tokens, cotangent, w_gate_up, w_down, query_key_value_weight, attn_proj, small, expert_ids,
+        tokens, cotangent, w_gate_up, w_down, query_key_value_weight, attn_proj, small, expert_ids.T,
         priority.reshape(expert_ids.shape), prefix, cos_t, sin_t)
     wide, grad_tokens, qkv_own, proj_own, terms, out_parts = back(parts, tokens, cos_t, sin_t)
     grad_gu, grad_dn, grad_qkv, grad_proj, output, grad_router = finish(

time: 420 us -> 416 us (level)
  no operation moved by 1% of the time
where the time goes in v9:
time: 416 us
  Pallas kernels  406 us (98%)
  local copies, waits for them, and re-layouts  5.53 us (1%)
    pallas_call x1, Pallas kernels, back(): pl.pallas_call(back_kernel, out_shape=outs, in_specs=[any_] * 20 + [vmem]...  204 us
    pallas_call x1, Pallas kernels, front(): pl.pallas_call(front_kernel, out_shape=outs, in_specs=[vmem, any_, any_,...  178 us
    pallas_call x1, Pallas kernels, finish(): pl.pallas_call(finish_kernel, grid=(steps,), out_shape=(jax.ShapeDtypeStr...  24.3 us

profile of v9, /device:TPU:0, one launch (start us, length us, event | category | flops | bytes accessed | tf_op | source)
XLA Modules:
  0.0 415.6 jit_solution(5498064565388382326)
XLA Ops:
  0.6 0.5 broadcast.10
  1.2 1.3 reduce.7
  2.5 0.7 reshape.31.prio
  3.2 0.7 broadcast_in_dim.14
  3.9 0.7 broadcast_in_dim.15
  4.6 0.1 pad.2.clone
  4.7 1.4 pad_maximum_fusion.small
  6.7 0.6 broadcast_in_dim.17.prefix
  7.3 177.5 %front.1 = (bf16[2,4,128,1664]{3,2,1,0:T(8,128)(2,1)}, bf16[2,4,128,1536]{3,2,1,0:T(8,128)(2,1)}, bf16[4,1024,512]{2,1,0:T(8,128)(2,1)}, bf16[4,1024,256]{2,1,0:...) custom-call(bf16[128,1536]{1,0:T(8,128)(2,1)} %tok.3, ...), custom_call_target="tpu_custom_call" | custom-call | tf_op jit(solution)/shard_map/front/pallas_call | solution.py:618
  184.8 204.1 %back.1 = (bf16[2,6144,768]{2,1,0:T(8,128)(2,1)}, f32[128,1536]{1,0:T(8,128)}, bf16[8,384,320]{2,1,0:T(8,128)(2,1)}, bf16[2,4,48,1536]{3,2,1,0:T(8,128)(2,1)}, f...) custom-call(bf16[2,4,128,1664]{3,2,1,0:T(8,128)(2,1)} %get-tuple-element.41.i_x, ...), custom_call_target="tpu_custom_call" | custom-call | tf_op jit(solution)/shard_map/back/pallas_call | solution.py:1110
  389.0 0.0 copy-start
  389.0 24.3 %finish.1 = (f32[6144,1024]{1,0:T(8,128)}, f32[6144,512]{1,0:T(8,128)}, f32[384,2560]{1,0:T(8,128)}, f32[384,1536]{1,0:T(8,128)}, bf16[128,1536]{1,0:T(8,128)(2,1)}, /*index=5*/f32[16,384]{1,0:T(8,128)}) custom-call(bf16[2,6144,768]{2,1,0:T(8,128)(2,1)} %get-tuple-element.61.v, bf16[8,384,320]{2,1,0:T(8,128)(2,1)} %get-tuple-element.62.qkv, ...), custom_call_target="tpu_custom_call" | custom-call | tf_op jit(solution)/shard_map/finish/pallas_call | solution.py:1146
  413.3 1.4 slice_reduce_fusion
  414.7 0.0 copy-done
  414.7 0.9 copy.25
  (1 shorter events, 0.0 us)
Async XLA Ops:
  389.0 25.7 %copy-start = (f32[128,1536]{1,0:T(8,128)S(1)}, f32[128,1536]{1,0:T(8,128)}, u32[]{:S(2)}) copy-start(f32[128,1536]{1,0:T(8,128)} %get-tuple-element.85) | copy-start | bytes 2359300

commit v10 on v9

--- a/solution.py
+++ b/solution.py
@@ -297,7 +297,7 @@
     local[0].wait()
     gain1 = jnp.concatenate([smalls[i, 0:1, :] for i in range(4)], axis=1).astype(F32)
     actp[c, p0] = (tok_f * inv1 * gain1).astype(BF)
-    pre[c, p0] = prefix[...]
+    pre[c, p0] = jnp.full((8, 128), prefix[0], jnp.int32).astype(F32)
     for i in range(2):
         c_act(i).start()
         c_pre(i).start()
@@ -307,10 +307,15 @@
     rank_of = jnp.zeros((128, 128), F32)
     lane_e = lax.broadcasted_iota(jnp.int32, (128, 128), 1)
     ids = ids_t[...].astype(F32).T
+    spread = jnp.concatenate(
+        [jnp.broadcast_to(prio[i : i + 1, :].astype(F32), (16, 128)) for i in range(8)], axis=0)
+    token = lax.broadcasted_iota(jnp.int32, (128, 128), 0)
+    spread = jnp.where(lane_e // 8 == lax.rem(token, 16), spread, 0.0)
     for k in range(8):
         hit = ids[:, k : k + 1] == lane_e.astype(F32)
         chosen_f = jnp.where(hit, 1.0, chosen_f)
-        rank_of = jnp.where(hit, prio[:, k : k + 1].astype(F32), rank_of)
+        own_prio = jnp.sum(jnp.where(lax.rem(lane_e, 8) == k, spread, 0.0), axis=1, keepdims=True)
+        rank_of = jnp.where(hit, own_prio, rank_of)
     rank_of = jnp.where(chosen_f > 0.0, rank_of, 65536.0)
     rank_t = rank_of.T
     slots = jnp.zeros((128, 128), F32)
@@ -618,7 +623,8 @@
     return pl.pallas_call(
         front_kernel,
         out_shape=outs,
-        in_specs=[vmem, any_, any_, any_, any_, any_, any_, vmem, vmem, vmem, vmem, vmem],
+        in_specs=[vmem, any_, any_, any_, any_, any_, any_, vmem, vmem,
+                  pl.BlockSpec(memory_space=pltpu.SMEM), vmem, vmem],
         out_specs=[any_] * len(outs),
         scratch_shapes=scratch + sems,
         compiler_params=pltpu.CompilerParams(
@@ -1140,7 +1146,7 @@
 
 
 def finish(v, qkv, proj, res, parts, terms):
-    steps, own, width = 8, proj.shape[0], proj.shape[1]
+    steps, own, width = 3, proj.shape[0], proj.shape[1]
     row, some = v.shape[1] // steps, own // steps
     once = lambda n: (lambda i: (0,) * n)
     return pl.pallas_call(
@@ -1406,7 +1412,6 @@
     small = jnp.concatenate(
         [attn_gain[None], mlp_gain[None], jnp.zeros((14, own), BF), w_router.T], axis=0
     )
-    prefix = jnp.broadcast_to(prefix_len.astype(F32), (8, 128))
     half = HEAD_WIDTH // 2
     inverse_freq = np.float32(10000.0) ** (-np.arange(half, dtype=np.float32) * np.float32(2.0 / HEAD_WIDTH))
     angles = np.arange(tokens.shape[0], dtype=np.float32)[:, None] * inverse_freq[None, :]
@@ -1415,7 +1420,7 @@
     sin_t = jnp.asarray(np.tile(np.concatenate([-sin, sin], axis=1), (1, 2)), F32)
     parts = front(
         tokens, cotangent, w_gate_up, w_down, query_key_value_weight, attn_proj, small, expert_ids.T,
-        priority.reshape(expert_ids.shape), prefix, cos_t, sin_t)
+        priority.reshape(8, 128), prefix_len, cos_t, sin_t)
     wide, grad_tokens, qkv_own, proj_own, terms, out_parts = back(parts, tokens, cos_t, sin_t)
     grad_gu, grad_dn, grad_qkv, grad_proj, output, grad_router = finish(
         wide, qkv_own, proj_own.reshape(own, width), parts[13], out_parts, terms)

time: 416 us -> 410 us (0.986)
  no operation moved by 1% of the time
where the time goes in v10:
time: 410 us
  Pallas kernels  403 us (98%)
    pallas_call x1, Pallas kernels, back(): pl.pallas_call(back_kernel, out_shape=outs, in_specs=[any_] * 20 + [vmem]...  204 us
    pallas_call x1, Pallas kernels, front(): pl.pallas_call(front_kernel, out_shape=outs, in_specs=[vmem, any_, any_,...  178 us
    pallas_call x1, Pallas kernels, finish(): pl.pallas_call(finish_kernel, grid=(steps,), out_shape=(jax.ShapeDtypeStr...  21.3 us

profile of v10, /device:TPU:0, one launch (start us, length us, event | category | flops | bytes accessed | tf_op | source)
XLA Modules:
  0.0 409.5 jit_solution(1014717980823898825)
XLA Ops:
  0.6 0.7 broadcast_in_dim.10
  1.3 0.7 broadcast_in_dim.9
  2.0 0.1 pad.2.clone
  2.1 1.4 pad_maximum_fusion.small
  4.1 177.7 %front.1 = (bf16[2,4,128,1664]{3,2,1,0:T(8,128)(2,1)}, bf16[2,4,128,1536]{3,2,1,0:T(8,128)(2,1)}, bf16[4,1024,512]{2,1,0:T(8,128)(2,1)}, bf16[4,1024,256]{2,1,0:...) custom-call(bf16[128,1536]{1,0:T(8,128)(2,1)} %tok.3, ...), custom_call_target="tpu_custom_call" | custom-call | tf_op jit(solution)/shard_map/front/pallas_call | solution.py:623
  181.8 204.1 %back.1 = (bf16[2,6144,768]{2,1,0:T(8,128)(2,1)}, f32[128,1536]{1,0:T(8,128)}, bf16[8,384,320]{2,1,0:T(8,128)(2,1)}, bf16[2,4,48,1536]{3,2,1,0:T(8,128)(2,1)}, f...) custom-call(bf16[2,4,128,1664]{3,2,1,0:T(8,128)(2,1)} %get-tuple-element.41.i_x, ...), custom_call_target="tpu_custom_call" | custom-call | tf_op jit(solution)/shard_map/back/pallas_call | solution.py:1116
  385.9 0.0 copy-start
  385.9 21.3 %finish.1 = (f32[6144,1024]{1,0:T(8,128)}, f32[6144,512]{1,0:T(8,128)}, f32[384,2560]{1,0:T(8,128)}, f32[384,1536]{1,0:T(8,128)}, bf16[128,1536]{1,0:T(8,128)(2,1)}, /*index=5*/f32[16,384]{1,0:T(8,128)}) custom-call(bf16[2,6144,768]{2,1,0:T(8,128)(2,1)} %get-tuple-element.61.v, bf16[8,384,320]{2,1,0:T(8,128)(2,1)} %get-tuple-element.62.qkv, ...), custom_call_target="tpu_custom_call" | custom-call | tf_op jit(solution)/shard_map/finish/pallas_call | solution.py:1152
  407.3 1.4 slice_reduce_fusion
  408.6 0.0 copy-done
  408.6 0.9 copy.25
  (1 shorter events, 0.0 us)
Async XLA Ops:
  385.9 22.7 %copy-start = (f32[128,1536]{1,0:T(8,128)S(1)}, f32[128,1536]{1,0:T(8,128)}, u32[]{:S(2)}) copy-start(f32[128,1536]{1,0:T(8,128)} %get-tuple-element.85) | copy-start | bytes 2359300

commit v11 on v10

--- a/solution.py
+++ b/solution.py
@@ -506,7 +506,7 @@
         one = pltpu.make_async_copy(src, dst, sl.at[9 + len(saves)])
         one.start()
         saves.append(one)
-    for src, dst in ((xall, o_x), (dyall, o_dy), (ggu, o_ggu), (hw, o_hw), (actp, o_act), (qs, o_q), (ks, o_k),
+    for src, dst in ((gw, o_gw), (xall, o_x), (dyall, o_dy), (ggu, o_ggu), (hw, o_hw), (actp, o_act), (qs, o_q), (ks, o_k),
                      (vs, o_v), (probs, o_probs), (att, o_att), (qkvw, o_qkvw), (projw, o_projw),
                      (smalls, o_small), (res, o_res), (gates, o_gates), (kept, o_kept)):
         save(src, dst)
@@ -559,7 +559,6 @@
     o_c.wait_recv()
     own(False, osib, osum)
     save(osum, o_osum)
-    save(gw, o_gw)
     for h in range(2):
         for b in range(2):
             copy1(h, b).wait()
@@ -1410,7 +1409,7 @@
 ):
     own, width = attn_gain.shape[0], tokens.shape[1]
     small = jnp.concatenate(
-        [attn_gain[None], mlp_gain[None], jnp.zeros((14, own), BF), w_router.T], axis=0
+        [jnp.concatenate([attn_gain, mlp_gain, jnp.zeros((14 * own,), BF)]).reshape(16, own), w_router.T], axis=0
     )
     half = HEAD_WIDTH // 2
     inverse_freq = np.float32(10000.0) ** (-np.arange(half, dtype=np.float32) * np.float32(2.0 / HEAD_WIDTH))

time: 410 us -> 409 us (level)
  no operation moved by 1% of the time
where the time goes in v11:
time: 409 us
  Pallas kernels  403 us (99%)
    pallas_call x1, Pallas kernels, back(): pl.pallas_call(back_kernel, out_shape=outs, in_specs=[any_] * 20 + [vmem]...  204 us
    pallas_call x1, Pallas kernels, front(): pl.pallas_call(front_kernel, out_shape=outs, in_specs=[vmem, any_, any_,...  178 us
    pallas_call x1, Pallas kernels, finish(): pl.pallas_call(finish_kernel, grid=(steps,), out_shape=(jax.ShapeDtypeStr...  21.3 us

profile of v11, /device:TPU:0, one launch (start us, length us, event | category | flops | bytes accessed | tf_op | source)
XLA Modules:
  0.0 408.8 jit_solution(5038765790555404882)
XLA Ops:
  0.7 0.7 pad_maximum_fusion.1
  1.4 1.3 pad_maximum_fusion.small
  3.4 177.7 %front.1 = (bf16[2,4,128,1664]{3,2,1,0:T(8,128)(2,1)}, bf16[2,4,128,1536]{3,2,1,0:T(8,128)(2,1)}, bf16[4,1024,512]{2,1,0:T(8,128)(2,1)}, bf16[4,1024,256]{2,1,0:...) custom-call(bf16[128,1536]{1,0:T(8,128)(2,1)} %tok.3, ...), custom_call_target="tpu_custom_call" | custom-call | tf_op jit(solution)/shard_map/front/pallas_call | solution.py:622
  181.0 204.1 %back.1 = (bf16[2,6144,768]{2,1,0:T(8,128)(2,1)}, f32[128,1536]{1,0:T(8,128)}, bf16[8,384,320]{2,1,0:T(8,128)(2,1)}, bf16[2,4,48,1536]{3,2,1,0:T(8,128)(2,1)}, f...) custom-call(bf16[2,4,128,1664]{3,2,1,0:T(8,128)(2,1)} %get-tuple-element.41.i_x, ...), custom_call_target="tpu_custom_call" | custom-call | tf_op jit(solution)/shard_map/back/pallas_call | solution.py:1115
  385.2 0.0 copy-start
  385.2 21.3 %finish.1 = (f32[6144,1024]{1,0:T(8,128)}, f32[6144,512]{1,0:T(8,128)}, f32[384,2560]{1,0:T(8,128)}, f32[384,1536]{1,0:T(8,128)}, bf16[128,1536]{1,0:T(8,128)(2,1)}, /*index=5*/f32[16,384]{1,0:T(8,128)}) custom-call(bf16[2,6144,768]{2,1,0:T(8,128)(2,1)} %get-tuple-element.61.v, bf16[8,384,320]{2,1,0:T(8,128)(2,1)} %get-tuple-element.62.qkv, ...), custom_call_target="tpu_custom_call" | custom-call | tf_op jit(solution)/shard_map/finish/pallas_call | solution.py:1151
  406.5 1.4 slice_reduce_fusion
  407.9 0.0 copy-done
  407.9 0.9 copy.25
  (2 shorter events, 0.0 us)
Async XLA Ops:
  385.2 22.7 %copy-start = (f32[128,1536]{1,0:T(8,128)S(1)}, f32[128,1536]{1,0:T(8,128)}, u32[]{:S(2)}) copy-start(f32[128,1536]{1,0:T(8,128)} %get-tuple-element.85) | copy-start | bytes 2359300
